TPU v7x, 32 devices: a whole 2x2x4 slice. The times are simulated.
32 devices in a mesh: swath: 2 (over x), rng: 16 (over z, y, core).
Axes of the slice: x: 2, y: 2, z: 4, core: 2. Of those that a mesh axis runs over, the one named last changes fastest.
Arguments:
- echoes: float32 [2, 512, 32768], P(None, ('swath', 'rng')), parts along dimension 1, may hold values from -6 to 6
- doppler_filter: float32 [2, 32768], replicated, may hold values from -5 to 5
- migration_shift: int32 [32768], replicated, may hold values from 0 to 9, as said below
- kernel_index: int32 [32768], replicated, may hold values from 0 to 15
- kernel_taps: float32 [16, 16], replicated, may hold values from -1.5 to 1.5
Outputs:
- image: float32 [2, 512, 32768], P(None, ('swath', 'rng')), parts along dimension 1
There are 2 independent parts, one for each index of `swath`. A program takes and returns all parts, laid end to end along the dimension named above; an argument that names none is the same for every part. Nothing has to cross between parts.
Inputs may be any that keep to these rules, and one draw needn't show every extreme that they name: `migration_shift`: both 0 and 9 occur.
All inputs are finite; a program needn't handle non-finite values.
Results may differ from a plain program's by a relative error of at most 0.0041.
Values may be sent and summed in bfloat16 or wider, within the bound.
No kernel may reach another device: no remote copies, remote signals or barrier semaphores. Data moves between devices by JAX's collectives and lax.ppermute only.
A program may use at most 64 MiB of HBM per device.

v0:
```python
import functools
import math

import jax
import jax.numpy as jnp
import numpy as np
from jax import lax
from jax.experimental import pallas as pl
from jax.experimental.pallas import tpu as pltpu
from jax.sharding import PartitionSpec as P

LANES = 128
INNER = 256
SUBLANES = 8
SMAX = 9
VMEM_LIMIT = 56 * 1024 * 1024


def split(values):
    high = values.astype(jnp.bfloat16)
    low = (values - high.astype(jnp.float32)).astype(jnp.bfloat16)
    return high, low


def dft_angles(length):
    numbers = np.arange(length, dtype=np.int64)
    return (numbers[:, None] * numbers[None, :] % length) * (2.0 * math.pi / length)


def np_split(values):
    values = values.astype(np.float32)
    high = values.astype(jnp.bfloat16)
    low = (values - high.astype(np.float32)).astype(jnp.bfloat16)
    return high, low


def tables(pulse_count):
    outer = pulse_count // INNER
    outer_angles = dft_angles(outer)
    inner_angles = dft_angles(INNER)
    oc, osn = np.cos(outer_angles), np.sin(outer_angles)
    ic, isn = np.cos(inner_angles), np.sin(inner_angles)
    forward_outer = np.block([[oc, osn], [-osn, oc]])
    forward_inner = np.block([[ic, -isn], [isn, ic]])
    inverse_inner = np.block([[ic, isn], [-isn, ic]])
    inverse_outer = np.block([[oc, -osn], [osn, oc]])
    twist = (
        np.arange(outer, dtype=np.int64)[:, None] * np.arange(INNER, dtype=np.int64)[None, :]
    ) * (2.0 * math.pi / pulse_count)
    scale = 1.0 / math.sqrt(pulse_count)
    twiddle = np.stack([np.cos(twist), np.sin(twist)]) * scale
    return dict(
        forward_outer=np.stack(np_split(forward_outer)),
        forward_inner=np.stack(np_split(forward_inner)),
        inverse_inner=inverse_inner.astype(jnp.bfloat16),
        inverse_outer=inverse_outer.astype(jnp.bfloat16),
        twiddle=twiddle.astype(np.float32),
    )


def forward_kernel(
    echo_ref, outer_ref, inner_ref, twiddle_ref, response_ref, out_ref,
    tiles, response_rows, rotated_high, rotated_low,
):
    rows = echo_ref.shape[1]
    pulse_count = echo_ref.shape[2]
    outer = pulse_count // INNER
    tile_count = pulse_count // LANES
    per_row = INNER // LANES
    for part in range(2):
        for tile in range(tile_count):
            tiles[part, pl.ds(tile * rows, rows), :] = echo_ref[
                part, :, pl.ds(tile * LANES, LANES)
            ]
    for tile in range(tile_count):
        response_rows[pl.ds(tile * 2, 2), :] = response_ref[:, pl.ds(tile * LANES, LANES)]
    outer_high, outer_low = outer_ref[0], outer_ref[1]
    cosine, sine = twiddle_ref[0], twiddle_ref[1]
    for row in range(rows):
        signal = jnp.concatenate(
            [
                jnp.concatenate(
                    [
                        tiles[part, pl.ds(half * rows + row, outer, stride=per_row * rows), :]
                        for half in range(per_row)
                    ],
                    axis=1,
                )
                for part in range(2)
            ],
            axis=0,
        )
        high, low = split(signal)
        sectioned = (
            jnp.dot(outer_high, low, preferred_element_type=jnp.float32)
            + jnp.dot(outer_low, high, preferred_element_type=jnp.float32)
            + jnp.dot(outer_high, high, preferred_element_type=jnp.float32)
        )
        real, imag = sectioned[:outer], sectioned[outer:]
        place = pl.ds(row * outer, outer)
        high, low = split(real * cosine + imag * sine)
        rotated_high[place, :INNER] = high
        rotated_low[place, :INNER] = low
        high, low = split(imag * cosine - real * sine)
        rotated_high[place, INNER:] = high
        rotated_low[place, INNER:] = low
    response_real = response_rows[pl.ds(0, tile_count, stride=2), :].T
    response_imag = response_rows[pl.ds(1, tile_count, stride=2), :].T
    inner_high, inner_low = inner_ref[0], inner_ref[1]
    step = 2 * outer
    for start in range(0, rows * outer, step):
        high = rotated_high[pl.ds(start, step), :]
        low = rotated_low[pl.ds(start, step), :]
        spectrum = (
            jnp.dot(high, inner_low, preferred_element_type=jnp.float32)
            + jnp.dot(low, inner_high, preferred_element_type=jnp.float32)
            + jnp.dot(high, inner_high, preferred_element_type=jnp.float32)
        )
        for index in range(step // outer):
            row = start // outer + index
            real = spectrum[index * outer : (index + 1) * outer, :INNER]
            imag = spectrum[index * outer : (index + 1) * outer, INNER:]
            out_ref[0, row] = (real * response_real + imag * response_imag).astype(jnp.bfloat16)
            out_ref[1, row] = (imag * response_real - real * response_imag).astype(jnp.bfloat16)


def forward(echoes, doppler_filter, table, block):
    pulse_count = echoes.shape[2]
    rows = SUBLANES
    outer = pulse_count // INNER
    whole = lambda array: pl.BlockSpec(array.shape, lambda i: (0,) * array.ndim)
    operands = [table["forward_outer"], table["forward_inner"], table["twiddle"], doppler_filter]
    return pl.pallas_call(
        forward_kernel,
        grid=(1,),
        out_shape=jax.ShapeDtypeStruct((2, rows, outer, INNER), jnp.bfloat16),
        in_specs=[pl.BlockSpec((2, rows, pulse_count), lambda i: (0, block, 0))]
        + [whole(array) for array in operands],
        out_specs=pl.BlockSpec((2, rows, outer, INNER), lambda i: (0, 0, 0, 0)),
        scratch_shapes=[
            pltpu.VMEM((2, pulse_count // LANES * rows, LANES), jnp.float32),
            pltpu.VMEM((pulse_count // LANES * 2, LANES), jnp.float32),
            pltpu.VMEM((rows * outer, 2 * INNER), jnp.bfloat16),
            pltpu.VMEM((rows * outer, 2 * INNER), jnp.bfloat16),
        ],
        compiler_params=pltpu.CompilerParams(vmem_limit_bytes=VMEM_LIMIT),
        cost_estimate=pl.CostEstimate(
            flops=6 * rows * pulse_count * (2 * outer + 2 * INNER),
            bytes_accessed=12 * rows * pulse_count,
            transcendentals=0,
        ),
        name="forward_dft",
    )(echoes, *operands)


def image_kernel(
    *refs, block_count, aliased,
):
    blocks = refs[:block_count]
    shift_ref, kernel_ref, taps_ref, inner_ref, outer_ref, twiddle_ref = refs[
        block_count : block_count + 6
    ]
    out_ref, migrated, shifts, kernels, tiles = refs[block_count + 6 + aliased :]
    rows = out_ref.shape[1]
    pulse_count = out_ref.shape[2]
    outer = pulse_count // INNER
    tile_count = pulse_count // LANES
    per_row = INNER // LANES
    tap_count = taps_ref.shape[0]
    half_taps = tap_count // 2
    shifts[...] = shift_ref[...].T
    kernels[...] = kernel_ref[...].T
    reach = SMAX + half_taps - 1
    input_rows = block_count * rows
    first = reach + half_taps - tap_count + 1
    group = 2 * SUBLANES

    def migrate(step, carry):
        sub = pl.multiple_of(step * group, group)
        for half in range(per_row):
            lanes = pl.ds(half * LANES, LANES)
            shift = shifts[pl.ds(sub, group), lanes]
            kernel_index = kernels[pl.ds(sub, group), lanes]
            bits = [
                ((shift // (1 << bit)) % 2).astype(jnp.float32).astype(jnp.bfloat16)
                > jnp.bfloat16(0.5)
                for bit in range(SMAX.bit_length())
            ]
            coefficients = [
                jnp.take_along_axis(
                    jnp.broadcast_to(taps_ref[pl.ds(tap, 1), :], (group, LANES)),
                    kernel_index,
                    axis=1,
                )
                for tap in range(tap_count)
            ]
            for part in range(2):
                moved = [
                    blocks[row // rows][part, row % rows, pl.ds(sub, group), lanes]
                    for row in range(input_rows)
                ]
                for bit in reversed(range(len(bits))):
                    jump = 1 << bit
                    low = first - (jump - 1)
                    moved = [
                        jnp.where(bits[bit], moved[row - jump], moved[row])
                        if row >= max(low, jump)
                        else moved[row]
                        for row in range(input_rows)
                    ]
                wide = {row: moved[row].astype(jnp.float32) for row in range(first, input_rows)}
                for row in range(rows):
                    total = None
                    for tap in range(tap_count):
                        term = coefficients[tap] * wide[row + reach + half_taps - tap]
                        total = term if total is None else total + term
                    migrated[
                        pl.ds(pl.multiple_of(row * outer + sub, group), group),
                        pl.ds(part * INNER + half * LANES, LANES),
                    ] = total.astype(jnp.bfloat16)
        return carry

    lax.fori_loop(0, outer // group, migrate, 0)
    cosine, sine = twiddle_ref[0], twiddle_ref[1]
    step = 2 * outer
    for start in range(0, rows * outer, step):
        sectioned = jnp.dot(
            migrated[pl.ds(start, step), :], inner_ref[...], preferred_element_type=jnp.float32
        )
        for index in range(step // outer):
            row = start // outer + index
            real = sectioned[index * outer : (index + 1) * outer, :INNER]
            imag = sectioned[index * outer : (index + 1) * outer, INNER:]
            turned = jnp.concatenate(
                [
                    (real * cosine - imag * sine).astype(jnp.bfloat16),
                    (real * sine + imag * cosine).astype(jnp.bfloat16),
                ],
                axis=0,
            )
            image = jnp.dot(outer_ref[...], turned, preferred_element_type=jnp.float32)
            for part in range(2):
                for half in range(per_row):
                    tiles[part, pl.ds(half * rows + row, outer, stride=per_row * rows), :] = image[
                        part * outer : (part + 1) * outer, half * LANES : (half + 1) * LANES
                    ]
    for part in range(2):
        for tile in range(tile_count):
            out_ref[part, :, pl.ds(tile * LANES, LANES)] = tiles[
                part, pl.ds(tile * rows, rows), :
            ]


def image(blocks, shift, kernel_index, taps, table, block, shape, previous):
    row_count, pulse_count = shape
    rows = SUBLANES
    outer = pulse_count // INNER
    whole = lambda array: pl.BlockSpec(array.shape, lambda i: (0,) * array.ndim)
    operands = [
        *blocks, shift, kernel_index, taps,
        table["inverse_inner"], table["inverse_outer"], table["twiddle"],
    ]
    specs = [whole(array) for array in operands]
    aliases = {}
    if previous is not None:
        aliases = {len(operands): 0}
        operands.append(previous)
        specs.append(pl.BlockSpec(memory_space=pl.ANY))
    return pl.pallas_call(
        functools.partial(
            image_kernel, block_count=len(blocks), aliased=int(previous is not None)
        ),
        grid=(1,),
        out_shape=jax.ShapeDtypeStruct((2, row_count, pulse_count), jnp.float32),
        in_specs=specs,
        out_specs=pl.BlockSpec((2, rows, pulse_count), lambda i: (0, block, 0)),
        input_output_aliases=aliases,
        scratch_shapes=[
            pltpu.VMEM((rows * outer, 2 * INNER), jnp.bfloat16),
            pltpu.VMEM((outer, INNER), jnp.int32),
            pltpu.VMEM((outer, INNER), jnp.int32),
            pltpu.VMEM((2, pulse_count // LANES * rows, LANES), jnp.float32),
        ],
        compiler_params=pltpu.CompilerParams(vmem_limit_bytes=VMEM_LIMIT),
        cost_estimate=pl.CostEstimate(
            flops=8 * rows * pulse_count * (2 * outer + 2 * INNER),
            bytes_accessed=24 * rows * pulse_count,
            transcendentals=0,
        ),
        name="migrate_and_image",
    )(*operands)


def per_device(echoes, doppler_filter, migration_shift, kernel_index, kernel_taps):
    row_count = echoes.shape[1]
    pulse_count = echoes.shape[2]
    outer = pulse_count // INNER
    rows = SUBLANES
    table = tables(pulse_count)
    count = lax.axis_size("rng")
    ahead = [(i, i + 1) for i in range(count - 1)]
    back = [(i + 1, i) for i in range(count - 1)]

    upper = forward(echoes, doppler_filter, table, 1)
    left_upper = lax.ppermute(upper, "rng", ahead)
    lower = forward(echoes, doppler_filter, table, 0)
    right_lower = lax.ppermute(lower, "rng", back)
    left_lower = lax.ppermute(lower, "rng", ahead)

    shift = migration_shift.reshape(INNER, outer)
    index = kernel_index.reshape(INNER, outer)
    taps = jnp.pad(kernel_taps.T, ((0, 0), (0, LANES - kernel_taps.shape[0])))
    shape = (row_count, pulse_count)
    picture = image(
        [left_upper, lower, upper, right_lower], shift, index, taps, table, 1, shape, None
    )
    return image(
        [left_lower, left_upper, lower, upper], shift, index, taps, table, 0, shape, picture
    )


def solution(mesh):
    return jax.shard_map(
        per_device,
        mesh=mesh,
        in_specs=(P(None, ("swath", "rng"), None), P(), P(), P(), P()),
        out_specs=P(None, ("swath", "rng"), None),
        check_vma=False,
    )
```

profile of v0, /device:TPU:17, one launch (start us, length us, event | category | flops | bytes accessed | tf_op | source)
XLA Modules:
  0.0 66.7 jit_solution(7856582343173999194)
XLA Ops:
  0.0 6.4 %forward_dft.3.refs_2_.refs_3_ = bf16[2,8,128,256]{3,2,1,0:T(8,128)(2,1)} custom-call(f32[2,16,32768]{2,1,0:T(8,128)} %echo_ref.3, bf16[2,256,256]{2,1,0:T(8,128)(2,1)} %constant.13.clone.outer_ref, bf16[2,512,512]{2,1,0:T(8,128)(2,1)} %constant.14.clone.inner_ref, f32[2,128,256]{2,1,0:T(8,128)} %constant.15.clone.twiddle_ref.refs_9_, f32[2,32768]{1,0:T(2,128)} %response_ref.3), custom_call_target="tpu_custom_call" | custom-call | flops 1207959552 | bytes 3145728 | tf_op jit(solution)/shard_map/forward_dft/pallas_call | solution.py:133
  6.4 0.0 copy-start.3
  6.4 3.8 %collective-permute-start.1 = (bf16[2,8,128,256]{3,2,1,0:T(8,128)(2,1)}, bf16[2,8,128,256]{3,2,1,0:T(8,128)(2,1)S(1)}, u32[]{:S(2)}, u32[]{:S(2)}) collective-permute-start(bf16[2,8,128,256]{3,2,1,0:T(8,128)(2,1)} %forward_dft.3.refs_2_.refs_3_), channel_id=1, source_target_pairs={{0,1},{1,2},{2,3},{3,4},{4,5},{5,6},{6,7},{7,8},{8,9},{9,10},{10,1... | collective-permute-start | bytes 3145736 | tf_op jit(solution)/shard_map/ppermute | solution.py:305
  10.3 6.3 %forward_dft.2.refs_1_.refs_2_ = bf16[2,8,128,256]{3,2,1,0:T(8,128)(2,1)} custom-call(f32[2,16,32768]{2,1,0:T(8,128)} %echo_ref.3, bf16[2,256,256]{2,1,0:T(8,128)(2,1)} %constant.13.clone.outer_ref, bf16[2,512,512]{2,1,0:T(8,128)(2,1)} %constant.14.clone.inner_ref, f32[2,128,256]{2,1,0:T(8,128)} %constant.15.clone.twiddle_ref.refs_9_, f32[2,32768]{1,0:T(2,128)} %response_ref.3), custom_call_target="tpu_custom_call" | custom-call | flops 1207959552 | bytes 3145728 | tf_op jit(solution)/shard_map/forward_dft/pallas_call | solution.py:133
  16.6 1.9 %collective-permute-start.2 = (bf16[2,8,128,256]{3,2,1,0:T(8,128)(2,1)}, bf16[2,8,128,256]{3,2,1,0:T(8,128)(2,1)S(1)}, u32[]{:S(2)}, u32[]{:S(2)}) collective-permute-start(bf16[2,8,128,256]{3,2,1,0:T(8,128)(2,1)} %forward_dft.2.refs_1_.refs_2_), channel_id=1, source_target_pairs={{1,0},{2,1},{3,2},{4,3},{5,4},{6,5},{7,6},{8,7},{9,8},{10,9},{11,1... | collective-permute-start | bytes 3145736 | tf_op jit(solution)/shard_map/ppermute | solution.py:307
  18.5 3.6 %collective-permute-start = (bf16[2,8,128,256]{3,2,1,0:T(8,128)(2,1)}, bf16[2,8,128,256]{3,2,1,0:T(8,128)(2,1)S(1)}, u32[]{:S(2)}, u32[]{:S(2)}) collective-permute-start(bf16[2,8,128,256]{3,2,1,0:T(8,128)(2,1)} %forward_dft.2.refs_1_.refs_2_), channel_id=1, source_target_pairs={{0,1},{1,2},{2,3},{3,4},{4,5},{5,6},{6,7},{7,8},{8,9},{9,10},{10,1... | collective-permute-start | bytes 3145736 | tf_op jit(solution)/shard_map/ppermute | solution.py:308
  22.2 0.0 copy-done.3
  22.2 0.1 copy.12
  22.2 0.6 pad.4.refs_6_
  22.9 0.0 collective-permute-done.1.refs_0_.refs_1_
  22.9 0.0 copy-start
  22.9 23.4 %collective-permute-done.2.refs_3_ = bf16[2,8,128,256]{3,2,1,0:T(8,128)(2,1)S(1)} collective-permute-done((bf16[2,8,128,256]{3,2,1,0:T(8,128)(2,1)}, bf16[2,8,128,256]{3,2,1,0:T(8,128)(2,1)S(1)}, u32[]{:S(2)}, u32[]{:S(2)}) %collective-permute-start.2) | collective-permute-done | bytes 1048608 | tf_op jit(solution)/shard_map/ppermute | solution.py:307
  46.2 0.0 copy-start.2
  46.2 0.0 copy-done
  46.2 1.0 %copy-done.2 = bf16[2,8,128,256]{3,2,1,0:T(8,128)(2,1)} copy-done((bf16[2,8,128,256]{3,2,1,0:T(8,128)(2,1)}, bf16[2,8,128,256]{3,2,1,0:T(8,128)(2,1)S(1)}, u32[]{:S(2)}) %copy-start.2) | copy-done | bytes 1048600
  47.2 9.2 %migrate_and_image.2.refs_10_ = f32[2,16,32768]{2,1,0:T(8,128)} custom-call(bf16[2,8,128,256]{3,2,1,0:T(8,128)(2,1)} %copy-done, bf16[2,8,128,256]{3,2,1,0:T(8,128)(2,1)} %forward_dft.2.refs_1_.refs_2_, bf16[2,8,128,256]{3,2,1,0:T(8,128)(2,1)} %forward_dft.3.refs_2_.refs_3_, bf16[2,8,128,256]{3,2,1,0:T(8,128)(2,1)} %copy-done.2, s32[256,128]{1,0:T(8,128)} %bitcast.3, ...), custom_call_target="tpu_custom_call" | custom-call | flops 1610612736 | bytes 6291456 | tf_op jit(solution)/shard_map/migrate_and_image/pallas_call | solution.py:269
  56.5 0.0 collective-permute-done.refs_0_
  56.5 0.0 copy-start.1
  56.5 1.0 %copy-done.1 = bf16[2,8,128,256]{3,2,1,0:T(8,128)(2,1)} copy-done((bf16[2,8,128,256]{3,2,1,0:T(8,128)(2,1)}, bf16[2,8,128,256]{3,2,1,0:T(8,128)(2,1)S(1)}, u32[]{:S(2)}) %copy-start.1) | copy-done | bytes 1048600
  57.5 9.2 %migrate_and_image.3 = f32[2,16,32768]{2,1,0:T(8,128)} custom-call(bf16[2,8,128,256]{3,2,1,0:T(8,128)(2,1)} %copy-done.1, bf16[2,8,128,256]{3,2,1,0:T(8,128)(2,1)} %copy-done, bf16[2,8,128,256]{3,2,1,0:T(8,128)(2,1)} %forward_dft.2.refs_1_.refs_2_, bf16[2,8,128,256]{3,2,1,0:T(8,128)(2,1)} %forward_dft.3.refs_2_.refs_3_, ...), custom_call_target="tpu_custom_call", output_to_operand_aliasing={{}: (10, {})} | custom-call | flops 1610612736 | bytes 6291456 | tf_op jit(solution)/shard_map/migrate_and_image/pallas_call | solution.py:269
Async XLA Ops:
  6.4 15.8 %copy-start.3 = (f32[16,16]{1,0:T(8,128)S(1)}, f32[16,16]{1,0:T(8,128)}, u32[]{:S(2)}) copy-start(f32[16,16]{1,0:T(8,128)} %param.14) | copy-start | bytes 3076
  6.4 16.4 %collective-permute-start.1 = (bf16[2,8,128,256]{3,2,1,0:T(8,128)(2,1)}, bf16[2,8,128,256]{3,2,1,0:T(8,128)(2,1)S(1)}, u32[]{:S(2)}, u32[]{:S(2)}) collective-permute-start(bf16[2,8,128,256]{3,2,1,0:T(8,128)(2,1)} %forward_dft.3.refs_2_.refs_3_), channel_id=1, source_target_pairs={{0,1},{1,2},{2,3},{3,4},{4,5},{5,6},{6,7},{7,8},{8,9},{9,10},{10,1... | collective-permute-start | bytes 3145736 | tf_op jit(solution)/shard_map/ppermute | solution.py:305
  16.6 29.6 %collective-permute-start.2 = (bf16[2,8,128,256]{3,2,1,0:T(8,128)(2,1)}, bf16[2,8,128,256]{3,2,1,0:T(8,128)(2,1)S(1)}, u32[]{:S(2)}, u32[]{:S(2)}) collective-permute-start(bf16[2,8,128,256]{3,2,1,0:T(8,128)(2,1)} %forward_dft.2.refs_1_.refs_2_), channel_id=1, source_target_pairs={{1,0},{2,1},{3,2},{4,3},{5,4},{6,5},{7,6},{8,7},{9,8},{10,9},{11,1... | collective-permute-start | bytes 3145736 | tf_op jit(solution)/shard_map/ppermute | solution.py:307
  18.5 37.9 %collective-permute-start = (bf16[2,8,128,256]{3,2,1,0:T(8,128)(2,1)}, bf16[2,8,128,256]{3,2,1,0:T(8,128)(2,1)S(1)}, u32[]{:S(2)}, u32[]{:S(2)}) collective-permute-start(bf16[2,8,128,256]{3,2,1,0:T(8,128)(2,1)} %forward_dft.2.refs_1_.refs_2_), channel_id=1, source_target_pairs={{0,1},{1,2},{2,3},{3,4},{4,5},{5,6},{6,7},{7,8},{8,9},{9,10},{10,1... | collective-permute-start | bytes 3145736 | tf_op jit(solution)/shard_map/ppermute | solution.py:308
  22.9 23.4 %copy-start = (bf16[2,8,128,256]{3,2,1,0:T(8,128)(2,1)}, bf16[2,8,128,256]{3,2,1,0:T(8,128)(2,1)S(1)}, u32[]{:S(2)}) copy-start(bf16[2,8,128,256]{3,2,1,0:T(8,128)(2,1)S(1)} %collective-permute-done.1.refs_0_.refs_1_) | copy-start | bytes 3145732
  46.2 1.0 %copy-start.2 = (bf16[2,8,128,256]{3,2,1,0:T(8,128)(2,1)}, bf16[2,8,128,256]{3,2,1,0:T(8,128)(2,1)S(1)}, u32[]{:S(2)}) copy-start(bf16[2,8,128,256]{3,2,1,0:T(8,128)(2,1)S(1)} %collective-permute-done.2.refs_3_) | copy-start | bytes 3145732
  56.5 1.0 %copy-start.1 = (bf16[2,8,128,256]{3,2,1,0:T(8,128)(2,1)}, bf16[2,8,128,256]{3,2,1,0:T(8,128)(2,1)S(1)}, u32[]{:S(2)}) copy-start(bf16[2,8,128,256]{3,2,1,0:T(8,128)(2,1)S(1)} %collective-permute-done.refs_0_) | copy-start | bytes 3145732
where the time goes:
time: 66.9 us; the launch traced here: 66.7 us
  Pallas kernels  31.2 us (47%)
  waiting for transfers between devices  23.4 us (35%)
  starting transfers between devices  9.38 us (14%)
  local copies, waits for them, and re-layouts  2.66 us (4%)
    ppermute x1, waiting for transfers between devices, per_device(): right_lower = lax.ppermute(lower, 'rng', back)  23.4 us
    pallas_call x2, Pallas kernels, image(): pl.pallas_call(functools.partial(image_kernel, block_count=len(blocks), a...  18.5 us
    pallas_call x2, Pallas kernels, forward(): pl.pallas_call(forward_kernel, grid=(1,), out_shape=jax.ShapeDtypeStruct(...  12.8 us
    ppermute x1, starting transfers between devices, per_device(): left_upper = lax.ppermute(upper, 'rng', ahead)  3.83 us
    ppermute x1, starting transfers between devices, per_device(): left_lower = lax.ppermute(lower, 'rng', ahead)  3.64 us
    unnamed x9, local copies, waits for them, and re-layouts  2.05 us
    ppermute x1, starting transfers between devices, per_device(): right_lower = lax.ppermute(lower, 'rng', back)  1.91 us
  transfers between devices with their start and end apart: 3, of which 1 were waited for; matrix products, arithmetic and copies ran while one was open for 1% of the time, Pallas kernels for 23%

commit v1 on v0

v1 whole, which is shorter than its diff:
```python
import functools
import math

import jax
import jax.numpy as jnp
import numpy as np
from jax import lax
from jax.experimental import pallas as pl
from jax.experimental.pallas import tpu as pltpu
from jax.sharding import PartitionSpec as P

LANES = 128
INNER = 256
SUBLANES = 8
SMAX = 9
PER = 2
VMEM_LIMIT = 24 * 1024 * 1024
VMEM_ALL = 56 * 1024 * 1024


def split(values):
    high = values.astype(jnp.bfloat16)
    low = (values - high.astype(jnp.float32)).astype(jnp.bfloat16)
    return high, low


def dft_angles(length):
    numbers = np.arange(length, dtype=np.int64)
    return (numbers[:, None] * numbers[None, :] % length) * (2.0 * math.pi / length)


def np_split(values):
    values = values.astype(np.float32)
    high = values.astype(jnp.bfloat16)
    low = (values - high.astype(np.float32)).astype(jnp.bfloat16)
    return high, low


def tables(pulse_count):
    outer = pulse_count // INNER
    half = INNER // 2
    outer_angles = dft_angles(outer)
    oc, osn = np.cos(outer_angles), np.sin(outer_angles)
    places = np.arange(half, dtype=np.int64)
    forward_inner, inverse_inner = [], []
    for parity in range(2):
        angles = (places[:, None] * (2 * places[None, :] + parity) % INNER) * (
            2.0 * math.pi / INNER
        )
        ic, isn = np.cos(angles), np.sin(angles)
        forward_inner.append(np.stack(np_split(np.block([[ic, -isn], [isn, ic]]))))
        inverse_inner.append(np.block([[ic.T, isn.T], [-isn.T, ic.T]]).astype(jnp.bfloat16))
    forward_outer = np.block([[oc, osn], [-osn, oc]])
    inverse_outer = np.block([[oc, -osn], [osn, oc]])
    twist = (
        np.arange(outer, dtype=np.int64)[:, None] * np.arange(INNER, dtype=np.int64)[None, :]
    ) * (2.0 * math.pi / pulse_count)
    scale = 1.0 / math.sqrt(pulse_count)
    twiddle = np.stack([np.cos(twist), np.sin(twist)]) * scale
    return dict(
        forward_outer=np.stack(np_split(forward_outer)),
        forward_inner=np.stack(forward_inner),
        inverse_inner=np.stack(inverse_inner),
        inverse_outer=inverse_outer.astype(jnp.bfloat16),
        twiddle=twiddle.astype(np.float32),
    )


def forward_kernel(
    echo_hbm, outer_hbm, inner_hbm, twiddle_hbm, response_hbm, out_hbm,
    echo, outer_table, inner_table, twiddle, response, response_rows,
    signal_high, signal_low, rotated_high, rotated_low, out, semaphores, *, block
):
    rows = out.shape[1]
    pulse_count = echo.shape[2]
    outer = pulse_count // INNER
    half = INNER // 2
    chunks = 8
    chunk = pulse_count // chunks
    ready = [
        pltpu.make_async_copy(source, target, semaphores.at[index])
        for index, (source, target) in enumerate(
            [
                (response_hbm, response),
                (outer_hbm, outer_table),
                (twiddle_hbm, twiddle),
                (inner_hbm, inner_table),
            ]
        )
    ]
    for index in range(chunks):
        place = pl.ds(index * chunk, chunk)
        ready.append(
            pltpu.make_async_copy(
                echo_hbm.at[:, pl.ds(block * rows, rows), place],
                echo.at[:, :, place],
                semaphores.at[4 + index],
            )
        )
    for index in [0, *range(4, 4 + chunks), 1, 2, 3]:
        ready[index].start()
    ready[0].wait()
    for tile in range(INNER):
        response_rows[pl.ds(tile * 2, 2), :] = response[:, pl.ds(tile * outer, outer)]
    response_parts = [
        [response_rows[pl.ds(2 * parity + part, half, stride=4), :].T for part in range(2)]
        for parity in range(2)
    ]
    for index in range(chunks):
        ready[4 + index].wait()
        for part in range(2):
            for first in range(index * outer // chunks, (index + 1) * outer // chunks, SUBLANES):
                gathered = jnp.stack(
                    [
                        echo[part, :, pl.ds((first + offset) * INNER, INNER)]
                        for offset in range(SUBLANES)
                    ]
                )
                high, low = split(jnp.swapaxes(gathered, 0, 1))
                place = pl.ds(part * outer + first, SUBLANES)
                signal_high[:, place, :] = high
                signal_low[:, place, :] = low
    ready[1].wait()
    ready[2].wait()
    outer_high, outer_low = outer_table[0], outer_table[1]
    cosine, sine = twiddle[0], twiddle[1]

    def first_stage(row):
        high, low = signal_high[row], signal_low[row]
        sectioned = (
            jnp.dot(outer_high, low, preferred_element_type=jnp.float32)
            + jnp.dot(outer_low, high, preferred_element_type=jnp.float32)
            + jnp.dot(outer_high, high, preferred_element_type=jnp.float32)
        )
        real, imag = sectioned[:outer], sectioned[outer:]
        turned = (real * cosine + imag * sine, imag * cosine - real * sine)
        place = pl.ds(row * outer, outer)
        for part in range(2):
            left, right = turned[part][:, :half], turned[part][:, half:]
            for parity, value in enumerate((left + right, left - right)):
                high, low = split(value)
                lanes = pl.ds((2 * parity + part) * half, half)
                rotated_high[place, lanes] = high
                rotated_low[place, lanes] = low

    def second_stage(row):
        place = pl.ds(row * outer, PER * outer)
        for parity in range(2):
            lanes = pl.ds(parity * INNER, INNER)
            high = rotated_high[place, lanes]
            low = rotated_low[place, lanes]
            table_high, table_low = inner_table[parity, 0], inner_table[parity, 1]
            spectrum = (
                jnp.dot(high, table_low, preferred_element_type=jnp.float32)
                + jnp.dot(low, table_high, preferred_element_type=jnp.float32)
                + jnp.dot(high, table_high, preferred_element_type=jnp.float32)
            )
            response_real, response_imag = response_parts[parity]
            lanes = pl.ds(parity * half, half)
            for index in range(PER):
                real = spectrum[index * outer : (index + 1) * outer, :half]
                imag = spectrum[index * outer : (index + 1) * outer, half:]
                out[0, row + index, :, lanes] = (
                    real * response_real + imag * response_imag
                ).astype(jnp.bfloat16)
                out[1, row + index, :, lanes] = (
                    imag * response_real - real * response_imag
                ).astype(jnp.bfloat16)
        place = pl.ds(row, PER)
        leaving = pltpu.make_async_copy(
            out.at[:, place], out_hbm.at[:, place], semaphores.at[4 + row // PER]
        )
        leaving.start()
        return leaving

    leaving = []
    for row in range(rows):
        first_stage(row)
        if row == 1:
            ready[3].wait()
        if row % PER == PER - 1 and row >= PER:
            leaving.append(second_stage(row + 1 - 2 * PER))
    leaving.append(second_stage(rows - PER))
    for copy in leaving:
        copy.wait()


def forward(echoes, doppler_filter, table, block):
    pulse_count = echoes.shape[2]
    rows = SUBLANES
    outer = pulse_count // INNER
    operands = [table["forward_outer"], table["forward_inner"], table["twiddle"], doppler_filter]
    anywhere = pl.BlockSpec(memory_space=pl.ANY)
    return pl.pallas_call(
        functools.partial(forward_kernel, block=block),
        out_shape=jax.ShapeDtypeStruct((2, rows, outer, INNER), jnp.bfloat16),
        in_specs=[anywhere] * 5,
        out_specs=anywhere,
        scratch_shapes=[
            pltpu.VMEM((2, rows, pulse_count), jnp.float32),
            *[pltpu.VMEM(array.shape, array.dtype) for array in operands],
            pltpu.VMEM((2 * INNER, outer), jnp.float32),
            pltpu.VMEM((rows, 2 * outer, INNER), jnp.bfloat16),
            pltpu.VMEM((rows, 2 * outer, INNER), jnp.bfloat16),
            pltpu.VMEM((rows * outer, 2 * INNER), jnp.bfloat16),
            pltpu.VMEM((rows * outer, 2 * INNER), jnp.bfloat16),
            pltpu.VMEM((2, rows, outer, INNER), jnp.bfloat16),
            pltpu.SemaphoreType.DMA((12,)),
        ],
        compiler_params=pltpu.CompilerParams(vmem_limit_bytes=VMEM_ALL),
        cost_estimate=pl.CostEstimate(
            flops=6 * rows * pulse_count * (2 * outer + INNER),
            bytes_accessed=12 * rows * pulse_count,
            transcendentals=0,
        ),
        name="forward_dft",
    )(echoes, *operands)


def migrate(inputs, known, taps, shifts, kernels, rows, store):
    outer = shifts.shape[0]
    half = INNER // 2
    tap_count = taps.shape[0]
    half_taps = tap_count // 2
    group = 2 * SUBLANES
    reach = SMAX + half_taps - 1
    input_rows = len(known) * rows
    first = reach + half_taps - tap_count + 1
    present = [known[row // rows] for row in range(input_rows)]

    def body(step, carry):
        sub = pl.multiple_of(step * group, group)
        for parity in range(2):
            lanes = pl.ds(parity * half, half)
            shift_here = shifts[pl.ds(sub, group), lanes]
            kernel_here = kernels[pl.ds(sub, group), lanes]
            bits = [
                ((shift_here // (1 << bit)) % 2).astype(jnp.float32).astype(jnp.bfloat16)
                > jnp.bfloat16(0.5)
                for bit in range(SMAX.bit_length())
            ]
            coefficients = [
                jnp.take_along_axis(
                    jnp.broadcast_to(taps[pl.ds(tap, 1), :], (group, LANES)), kernel_here, axis=1
                )
                for tap in range(tap_count)
            ]
            nothing = jnp.zeros((group, LANES), jnp.bfloat16)
            for part in range(2):
                moved = [
                    inputs[row // rows][part, row % rows, pl.ds(sub, group), lanes]
                    if present[row]
                    else None
                    for row in range(input_rows)
                ]
                for bit in reversed(range(len(bits))):
                    jump = 1 << bit
                    low = first - (jump - 1)
                    later = []
                    for row in range(input_rows):
                        here = moved[row]
                        if row >= max(low, jump):
                            there = moved[row - jump]
                            if here is not None or there is not None:
                                here = jnp.where(
                                    bits[bit],
                                    nothing if there is None else there,
                                    nothing if here is None else here,
                                )
                        later.append(here)
                    moved = later
                wide = {
                    row: moved[row].astype(jnp.float32)
                    for row in range(first, input_rows)
                    if any(present[max(row - SMAX, 0) : row + 1])
                }
                for row in range(rows):
                    total = None
                    for tap in range(tap_count):
                        source = row + reach + half_taps - tap
                        if source in wide:
                            term = coefficients[tap] * wide[source]
                            total = term if total is None else total + term
                    store(part, parity, row, pl.ds(sub, group), total)
        return carry

    lax.fori_loop(0, outer // group, body, 0)


def order_indices(shift, kernel, shifts, kernels):
    half = INNER // 2
    for parity in range(2):
        lanes = pl.ds(parity * half, half)
        shifts[:, lanes] = shift[pl.ds(parity, half, stride=2), :].T
        kernels[:, lanes] = kernel[pl.ds(parity, half, stride=2), :].T


def partial_kernel(*refs, known, has_partial):
    count = sum(known)
    earlier = refs[count] if has_partial else None
    shift, kernel, taps, out, shifts, kernels = refs[count + has_partial :]
    half = INNER // 2
    blocks = iter(refs[:count])
    inputs = [next(blocks) if there else None for there in known]
    order_indices(shift, kernel, shifts, kernels)

    def store(part, parity, row, place, total):
        lanes = pl.ds(parity * half, half)
        if has_partial:
            before = earlier[part, row, place, lanes]
            total = before if total is None else total + before
        out[part, row, place, lanes] = total

    migrate(inputs, known, taps, shifts, kernels, out.shape[1], store)


def partial(blocks, known, shift, kernel_index, taps, earlier):
    operands = [*blocks, *([] if earlier is None else [earlier]), shift, kernel_index, taps]
    rows, outer = blocks[0].shape[1], blocks[0].shape[2]
    inside = pl.BlockSpec(memory_space=pltpu.VMEM)
    return pl.pallas_call(
        functools.partial(
            partial_kernel, known=known, has_partial=int(earlier is not None)
        ),
        out_shape=jax.ShapeDtypeStruct(blocks[0].shape, jnp.float32),
        in_specs=[inside] * len(operands),
        out_specs=inside,
        scratch_shapes=[
            pltpu.VMEM((outer, INNER), jnp.int32),
            pltpu.VMEM((outer, INNER), jnp.int32),
        ],
        compiler_params=pltpu.CompilerParams(vmem_limit_bytes=VMEM_LIMIT),
        cost_estimate=pl.CostEstimate(
            flops=8 * rows * outer * INNER * 500,
            bytes_accessed=24 * rows * outer * INNER,
            transcendentals=0,
        ),
        name="migrate_known_rows",
    )(*operands)


def image_kernel(*refs, known, has_partial, aliased, block):
    count = sum(known)
    blocks = iter(refs[:count])
    inputs = [next(blocks) if there else None for there in known]
    earlier = refs[count] if has_partial else None
    count += has_partial
    shift, kernel, taps, inner_table, outer_table, twiddle = refs[count : count + 6]
    out_hbm, shifts, kernels, migrated, images, out, semaphores = refs[count + 6 + aliased :]
    rows = out.shape[1]
    pulse_count = out.shape[2]
    outer = pulse_count // INNER
    half = INNER // 2
    order_indices(shift, kernel, shifts, kernels)

    def store(part, parity, row, place, total):
        if has_partial:
            before = earlier[part, row, place, pl.ds(parity * half, half)]
            total = before if total is None else total + before
        migrated[row, place, pl.ds((2 * parity + part) * half, half)] = total.astype(jnp.bfloat16)

    migrate(inputs, known, taps, shifts, kernels, rows, store)
    cosine, sine = twiddle[0], twiddle[1]
    for start in range(0, rows, PER):
        left_parts, right_parts = (
            migrated[pl.ds(start, PER), :, pl.ds(parity * INNER, INNER)].reshape(PER * outer, INNER)
            for parity in range(2)
        )
        even = jnp.dot(left_parts, inner_table[0], preferred_element_type=jnp.float32)
        odd = jnp.dot(right_parts, inner_table[1], preferred_element_type=jnp.float32)
        left, right = even + odd, even - odd
        for index in range(PER):
            here = slice(index * outer, (index + 1) * outer)
            turned = [], []
            for side, value in enumerate((left, right)):
                lanes = slice(side * half, (side + 1) * half)
                real, imag = value[here, :half], value[here, half:]
                turned[0].append(real * cosine[:, lanes] - imag * sine[:, lanes])
                turned[1].append(real * sine[:, lanes] + imag * cosine[:, lanes])
            turned = jnp.concatenate(
                [jnp.concatenate(pair, axis=1).astype(jnp.bfloat16) for pair in turned], axis=0
            )
            images[start + index] = jnp.dot(
                outer_table[...], turned, preferred_element_type=jnp.float32
            )
    chunks = 4
    chunk = pulse_count // chunks
    leaving = []
    for index in range(chunks):
        for part in range(2):
            for first_place in range(
                index * outer // chunks, (index + 1) * outer // chunks, SUBLANES
            ):
                swapped = jnp.swapaxes(
                    images[:, pl.ds(part * outer + first_place, SUBLANES), :], 0, 1
                )
                for offset in range(SUBLANES):
                    out[part, :, pl.ds((first_place + offset) * INNER, INNER)] = swapped[offset]
        place = pl.ds(index * chunk, chunk)
        leaving.append(
            pltpu.make_async_copy(
                out.at[:, :, place],
                out_hbm.at[:, pl.ds(block * rows, rows), place],
                semaphores.at[index],
            )
        )
        leaving[-1].start()
    for copy in leaving:
        copy.wait()


def image(blocks, known, shift, kernel_index, taps, table, block, shape, earlier, previous):
    row_count, pulse_count = shape
    rows = SUBLANES
    outer = pulse_count // INNER
    operands = [
        *blocks, *([] if earlier is None else [earlier]), shift, kernel_index, taps,
        table["inverse_inner"], table["inverse_outer"], table["twiddle"],
    ]
    specs = [pl.BlockSpec(memory_space=pltpu.VMEM)] * len(operands)
    aliases = {}
    anywhere = pl.BlockSpec(memory_space=pl.ANY)
    if previous is not None:
        aliases = {len(operands): 0}
        operands.append(previous)
        specs.append(anywhere)
    return pl.pallas_call(
        functools.partial(
            image_kernel, known=known, has_partial=int(earlier is not None),
            aliased=len(aliases), block=block,
        ),
        out_shape=jax.ShapeDtypeStruct((2, row_count, pulse_count), jnp.float32),
        in_specs=specs,
        out_specs=anywhere,
        input_output_aliases=aliases,
        scratch_shapes=[
            pltpu.VMEM((outer, INNER), jnp.int32),
            pltpu.VMEM((outer, INNER), jnp.int32),
            pltpu.VMEM((rows, outer, 2 * INNER), jnp.bfloat16),
            pltpu.VMEM((rows, 2 * outer, INNER), jnp.float32),
            pltpu.VMEM((2, rows, pulse_count), jnp.float32),
            pltpu.SemaphoreType.DMA((4,)),
        ],
        compiler_params=pltpu.CompilerParams(vmem_limit_bytes=VMEM_LIMIT),
        cost_estimate=pl.CostEstimate(
            flops=8 * rows * pulse_count * (2 * outer + 2 * INNER),
            bytes_accessed=24 * rows * pulse_count,
            transcendentals=0,
        ),
        name="migrate_and_image",
    )(*operands)


def per_device(echoes, doppler_filter, migration_shift, kernel_index, kernel_taps):
    row_count = echoes.shape[1]
    pulse_count = echoes.shape[2]
    outer = pulse_count // INNER
    table = tables(pulse_count)
    count = lax.axis_size("rng")
    ahead = [(i, i + 1) for i in range(count - 1)]
    back = [(i + 1, i) for i in range(count - 1)]
    shift = migration_shift.reshape(INNER, outer)
    index = kernel_index.reshape(INNER, outer)
    taps = jnp.pad(kernel_taps.T, ((0, 0), (0, LANES - kernel_taps.shape[0])))
    shape = (row_count, pulse_count)

    upper = forward(echoes, doppler_filter, table, 1)
    left_upper = lax.ppermute(upper, "rng", ahead)
    lower = forward(echoes, doppler_filter, table, 0)
    right_lower = lax.ppermute(lower, "rng", back)
    high_part = partial([lower, upper], (False, True, True, False), shift, index, taps, None)
    low_part = partial([lower, upper], (False, False, True, True), shift, index, taps, None)
    lower_again, high_part, low_part = lax.optimization_barrier((lower, high_part, low_part))
    left_lower = lax.ppermute(lower_again, "rng", ahead)
    picture = image(
        [left_upper, right_lower], (True, False, False, True),
        shift, index, taps, table, 1, shape, high_part, None,
    )
    low_part = partial(
        [left_upper], (False, True, False, False), shift, index, taps, low_part
    )
    return image(
        [left_lower], (True, False, False, False),
        shift, index, taps, table, 0, shape, low_part, picture,
    )


def solution(mesh):
    return jax.shard_map(
        per_device,
        mesh=mesh,
        in_specs=(P(None, ("swath", "rng"), None), P(), P(), P(), P()),
        out_specs=P(None, ("swath", "rng"), None),
        check_vma=False,
    )
```

time: 66.9 us -> 55 us (0.82)
  waiting for transfers between devices: 23.4 us -> 13.5 us
  local copies, waits for them, and re-layouts: 2.66 us -> 0.12 us
    ppermute x1, waiting for transfers between devices: 23.4 us -> 9.71 us  [per_device(): right_lower = lax.ppermute(lower, 'rng', back)]
    ppermute x1, waiting for transfers between devices: 0.01 us -> 3.77 us  [per_device(): left_upper = lax.ppermute(upper, 'rng', ahead)]
    unnamed x9 -> x15, local copies, waits for them, and re-layouts: 2.05 us -> 0.12 us
    pallas_call x4 -> x7, Pallas kernels: 31.2 us -> 31.5 us  [the longest x3 11.8 us: partial(): pl.pallas_call(functools.partial(partial_kernel, known=known, has_partial...]
  transfers between devices with their start and end apart: 3 -> 3, of which waited for: 1 -> 2; matrix products, arithmetic and copies ran while one was open for 1% -> 0% of each run, Pallas kernels for 23% -> 40%
where the time goes in v1:
time: 55 us; the launch traced here: 54.7 us
  Pallas kernels  31.5 us (57%)
  waiting for transfers between devices  13.5 us (25%)
  starting transfers between devices  9.4 us (17%)
    pallas_call x3, Pallas kernels, partial(): pl.pallas_call(functools.partial(partial_kernel, known=known, has_partial...  11.8 us
    pallas_call x2, Pallas kernels, image(): pl.pallas_call(functools.partial(image_kernel, known=known, has_partial=i...  9.88 us
    pallas_call x2, Pallas kernels, forward(): pl.pallas_call(functools.partial(forward_kernel, block=block), out_shape=...  9.83 us
    ppermute x1, waiting for transfers between devices, per_device(): right_lower = lax.ppermute(lower, 'rng', back)  9.71 us
    ppermute x1, starting transfers between devices, per_device(): left_upper = lax.ppermute(upper, 'rng', ahead)  3.84 us
    ppermute x1, waiting for transfers between devices, per_device(): left_upper = lax.ppermute(upper, 'rng', ahead)  3.77 us
    ppermute x1, starting transfers between devices, per_device(): left_lower = lax.ppermute(lower_again, 'rng', ahead)  3.64 us
    ppermute x1, starting transfers between devices, per_device(): right_lower = lax.ppermute(lower, 'rng', back)  1.92 us
  transfers between devices with their start and end apart: 3, of which 2 were waited for; matrix products, arithmetic and copies ran while one was open for 0% of the time, Pallas kernels for 40%

profile of v1, /device:TPU:17, one launch (start us, length us, event | category | flops | bytes accessed | tf_op | source)
XLA Modules:
  0.0 54.7 jit_solution(9115048270576836444)
XLA Ops:
  0.0 4.9 %forward_dft.3.refs_1_ = bf16[2,8,128,256]{3,2,1,0:T(8,128)(2,1)} custom-call(f32[2,16,32768]{2,1,0:T(8,128)} %echo_hbm.3, bf16[2,256,256]{2,1,0:T(8,128)(2,1)} %constant.13.clone.outer_hbm, bf16[2,2,256,256]{3,2,1,0:T(8,128)(2,1)} %constant.14.clone.inner_hbm, f32[2,128,256]{2,1,0:T(8,128)} %constant.15.clone.twiddle_hbm.refs_8_.refs_7_, ...), custom_call_target="tpu_custom_call" | custom-call | flops 805306368 | bytes 3145728 | tf_op jit(solution)/shard_map/forward_dft/pallas_call | solution.py:194
  4.9 0.0 copy-start.6
  4.9 0.0 copy-start
  4.9 0.0 copy-start.2
  5.0 0.0 copy-start.3
  5.0 3.8 %collective-permute-start.1 = (bf16[2,8,128,256]{3,2,1,0:T(8,128)(2,1)}, bf16[2,8,128,256]{3,2,1,0:T(8,128)(2,1)S(1)}, u32[]{:S(2)}, u32[]{:S(2)}) collective-permute-start(bf16[2,8,128,256]{3,2,1,0:T(8,128)(2,1)} %forward_dft.3.refs_1_), channel_id=1, source_target_pairs={{0,1},{1,2},{2,3},{3,4},{4,5},{5,6},{6,7},{7,8},{8,9},{9,10},{10,1... | collective-permute-start | bytes 3145736 | tf_op jit(solution)/shard_map/ppermute | solution.py:468
  8.8 4.9 %forward_dft.2.refs_0_ = bf16[2,8,128,256]{3,2,1,0:T(8,128)(2,1)} custom-call(f32[2,16,32768]{2,1,0:T(8,128)} %echo_hbm.3, bf16[2,256,256]{2,1,0:T(8,128)(2,1)} %constant.13.clone.outer_hbm, bf16[2,2,256,256]{3,2,1,0:T(8,128)(2,1)} %constant.14.clone.inner_hbm, f32[2,128,256]{2,1,0:T(8,128)} %constant.15.clone.twiddle_hbm.refs_8_.refs_7_, ...), custom_call_target="tpu_custom_call" | custom-call | flops 805306368 | bytes 3145728 | tf_op jit(solution)/shard_map/forward_dft/pallas_call | solution.py:194
  13.7 1.9 %collective-permute-start.2 = (bf16[2,8,128,256]{3,2,1,0:T(8,128)(2,1)}, bf16[2,8,128,256]{3,2,1,0:T(8,128)(2,1)S(1)}, u32[]{:S(2)}, u32[]{:S(2)}) collective-permute-start(bf16[2,8,128,256]{3,2,1,0:T(8,128)(2,1)} %forward_dft.2.refs_0_), channel_id=1, source_target_pairs={{1,0},{2,1},{3,2},{4,3},{5,4},{6,5},{7,6},{8,7},{9,8},{10,9},{11,1... | collective-permute-start | bytes 3145736 | tf_op jit(solution)/shard_map/ppermute | solution.py:470
  15.7 0.0 copy-done.6
  15.7 0.1 copy.12
  15.8 0.0 copy-done
  15.8 0.0 copy-done.2
  15.8 0.0 copy-done.3
  15.8 4.1 %migrate_known_rows.4.refs_1_ = f32[2,8,128,256]{3,2,1,0:T(8,128)S(1)} custom-call(bf16[2,8,128,256]{3,2,1,0:T(8,128)(2,1)} %forward_dft.2.refs_0_, bf16[2,8,128,256]{3,2,1,0:T(8,128)(2,1)S(1)} %copy-done, s32[256,128]{1,0:T(8,128)S(1)} %bitcast.3, s32[256,128]{1,0:T(8,128)S(1)} %bitcast.8, f32[16,128]{1,0:T(8,128)S(1)} %pad.4.refs_4_.refs_5_), custom_call_target="tpu_custom_call" | custom-call | flops 1048576000 | bytes 6291456 | tf_op jit(solution)/shard_map/migrate_known_rows/pallas_call | solution.py:321
  19.8 0.0 copy-start.1
  19.9 0.0 copy-start.4
  19.9 0.0 copy-start.5
  19.9 4.8 %migrate_known_rows.3.refs_2_ = f32[2,8,128,256]{3,2,1,0:T(8,128)S(1)} custom-call(bf16[2,8,128,256]{3,2,1,0:T(8,128)(2,1)} %forward_dft.2.refs_0_, bf16[2,8,128,256]{3,2,1,0:T(8,128)(2,1)S(1)} %copy-done, s32[256,128]{1,0:T(8,128)S(1)} %bitcast.4, s32[256,128]{1,0:T(8,128)S(1)} %bitcast.9, f32[16,128]{1,0:T(8,128)S(1)} %pad.4.refs_4_.refs_5_), custom_call_target="tpu_custom_call" | custom-call | flops 1048576000 | bytes 6291456 | tf_op jit(solution)/shard_map/migrate_known_rows/pallas_call | solution.py:321
  24.7 3.6 %collective-permute-start = (bf16[2,8,128,256]{3,2,1,0:T(8,128)(2,1)}, bf16[2,8,128,256]{3,2,1,0:T(8,128)(2,1)S(1)}, u32[]{:S(2)}, u32[]{:S(2)}) collective-permute-start(bf16[2,8,128,256]{3,2,1,0:T(8,128)(2,1)} %forward_dft.2.refs_0_), channel_id=1, source_target_pairs={{0,1},{1,2},{2,3},{3,4},{4,5},{5,6},{6,7},{7,8},{8,9},{9,10},{10,1... | collective-permute-start | bytes 3145736 | tf_op jit(solution)/shard_map/ppermute | solution.py:474
  28.3 3.8 %collective-permute-done.1.refs_0_ = bf16[2,8,128,256]{3,2,1,0:T(8,128)(2,1)S(1)} collective-permute-done((bf16[2,8,128,256]{3,2,1,0:T(8,128)(2,1)}, bf16[2,8,128,256]{3,2,1,0:T(8,128)(2,1)S(1)}, u32[]{:S(2)}, u32[]{:S(2)}) %collective-permute-start.1) | collective-permute-done | bytes 1048608 | tf_op jit(solution)/shard_map/ppermute | solution.py:468
  32.1 3.0 %migrate_known_rows.5.refs_1_ = f32[2,8,128,256]{3,2,1,0:T(8,128)S(1)} custom-call(bf16[2,8,128,256]{3,2,1,0:T(8,128)(2,1)S(1)} %collective-permute-done.1.refs_0_, f32[2,8,128,256]{3,2,1,0:T(8,128)S(1)} %migrate_known_rows.4.refs_1_, s32[256,128]{1,0:T(8,128)S(1)} %bitcast.5, s32[256,128]{1,0:T(8,128)S(1)} %bitcast.10, f32[16,128]{1,0:T(8,128)S(1)} %pad.4.refs_4_.refs_5_), custom_call_target="tpu_custom_call" | custom-call | flops 1048576000 | bytes 6291456 | tf_op jit(solution)/shard_map/migrate_known_rows/pallas_call | solution.py:321
  35.1 9.7 %collective-permute-done.2.refs_1_ = bf16[2,8,128,256]{3,2,1,0:T(8,128)(2,1)S(1)} collective-permute-done((bf16[2,8,128,256]{3,2,1,0:T(8,128)(2,1)}, bf16[2,8,128,256]{3,2,1,0:T(8,128)(2,1)S(1)}, u32[]{:S(2)}, u32[]{:S(2)}) %collective-permute-start.2) | collective-permute-done | bytes 1048608 | tf_op jit(solution)/shard_map/ppermute | solution.py:470
  44.8 0.0 copy-done.1
  44.8 0.0 copy-done.4
  44.8 0.0 copy-done.5
  44.8 5.3 %migrate_and_image.2.refs_8_ = f32[2,16,32768]{2,1,0:T(8,128)} custom-call(bf16[2,8,128,256]{3,2,1,0:T(8,128)(2,1)S(1)} %collective-permute-done.1.refs_0_, bf16[2,8,128,256]{3,2,1,0:T(8,128)(2,1)S(1)} %collective-permute-done.2.refs_1_, f32[2,8,128,256]{3,2,1,0:T(8,128)S(1)} %migrate_known_rows.3.refs_2_, s32[256,128]{1,0:T(8,128)S(1)} %bitcast.6, ...), custom_call_target="tpu_custom_call" | custom-call | flops 1610612736 | bytes 6291456 | tf_op jit(solution)/shard_map/migrate_and_image/pallas_call | solution.py:427
  50.1 0.0 collective-permute-done.refs_0_
  50.1 4.6 %migrate_and_image.3 = f32[2,16,32768]{2,1,0:T(8,128)} custom-call(bf16[2,8,128,256]{3,2,1,0:T(8,128)(2,1)S(1)} %collective-permute-done.refs_0_, f32[2,8,128,256]{3,2,1,0:T(8,128)S(1)} %migrate_known_rows.5.refs_1_, s32[256,128]{1,0:T(8,128)S(1)} %bitcast.7, s32[256,128]{1,0:T(8,128)S(1)} %bitcast.12, ...), custom_call_target="tpu_custom_call", output_to_operand_aliasing={{}: (8, {})} | custom-call | flops 1610612736 | bytes 6291456 | tf_op jit(solution)/shard_map/migrate_and_image/pallas_call | solution.py:427
  (1 shorter events, 0.0 us)
Async XLA Ops:
  4.9 10.8 %copy-start.6 = (f32[16,16]{1,0:T(8,128)S(1)}, f32[16,16]{1,0:T(8,128)}, u32[]{:S(2)}) copy-start(f32[16,16]{1,0:T(8,128)} %param.14) | copy-start | bytes 3076
  4.9 10.8 %copy-start = (bf16[2,8,128,256]{3,2,1,0:T(8,128)(2,1)S(1)}, bf16[2,8,128,256]{3,2,1,0:T(8,128)(2,1)}, u32[]{:S(2)}) copy-start(bf16[2,8,128,256]{3,2,1,0:T(8,128)(2,1)} %forward_dft.3.refs_1_) | copy-start | bytes 3145732
  4.9 10.8 %copy-start.2 = (s32[32768]{0:T(1024)S(1)}, s32[32768]{0:T(1024)}, u32[]{:S(2)}) copy-start(s32[32768]{0:T(1024)} %param.12) | copy-start | bytes 393220
  5.0 10.8 %copy-start.3 = (s32[32768]{0:T(1024)S(1)}, s32[32768]{0:T(1024)}, u32[]{:S(2)}) copy-start(s32[32768]{0:T(1024)} %param.13) | copy-start | bytes 393220
  5.0 27.1 %collective-permute-start.1 = (bf16[2,8,128,256]{3,2,1,0:T(8,128)(2,1)}, bf16[2,8,128,256]{3,2,1,0:T(8,128)(2,1)S(1)}, u32[]{:S(2)}, u32[]{:S(2)}) collective-permute-start(bf16[2,8,128,256]{3,2,1,0:T(8,128)(2,1)} %forward_dft.3.refs_1_), channel_id=1, source_target_pairs={{0,1},{1,2},{2,3},{3,4},{4,5},{5,6},{6,7},{7,8},{8,9},{9,10},{10,1... | collective-permute-start | bytes 3145736 | tf_op jit(solution)/shard_map/ppermute | solution.py:468
  13.7 31.0 %collective-permute-start.2 = (bf16[2,8,128,256]{3,2,1,0:T(8,128)(2,1)}, bf16[2,8,128,256]{3,2,1,0:T(8,128)(2,1)S(1)}, u32[]{:S(2)}, u32[]{:S(2)}) collective-permute-start(bf16[2,8,128,256]{3,2,1,0:T(8,128)(2,1)} %forward_dft.2.refs_0_), channel_id=1, source_target_pairs={{1,0},{2,1},{3,2},{4,3},{5,4},{6,5},{7,6},{8,7},{9,8},{10,9},{11,1... | collective-permute-start | bytes 3145736 | tf_op jit(solution)/shard_map/ppermute | solution.py:470
  19.8 24.9 %copy-start.1 = (f32[2,128,256]{2,1,0:T(8,128)S(1)}, f32[2,128,256]{2,1,0:T(8,128)}, u32[]{:S(2)}) copy-start(f32[2,128,256]{2,1,0:T(8,128)} %constant.15.clone.twiddle_hbm.refs_8_.refs_7_) | copy-start | bytes 786436
  19.9 24.9 %copy-start.4 = (bf16[2,256,256]{2,1,0:T(8,128)(2,1)S(1)}, bf16[2,256,256]{2,1,0:T(8,128)(2,1)}, u32[]{:S(2)}) copy-start(bf16[2,256,256]{2,1,0:T(8,128)(2,1)} %constant.16.clone.refs_6_.refs_5_) | copy-start | bytes 786436
  19.9 24.9 %copy-start.5 = (bf16[256,256]{1,0:T(8,128)(2,1)S(1)}, bf16[256,256]{1,0:T(8,128)(2,1)}, u32[]{:S(2)}) copy-start(bf16[256,256]{1,0:T(8,128)(2,1)} %constant.17.clone.refs_7_.refs_6_) | copy-start | bytes 393220
  24.7 25.4 %collective-permute-start = (bf16[2,8,128,256]{3,2,1,0:T(8,128)(2,1)}, bf16[2,8,128,256]{3,2,1,0:T(8,128)(2,1)S(1)}, u32[]{:S(2)}, u32[]{:S(2)}) collective-permute-start(bf16[2,8,128,256]{3,2,1,0:T(8,128)(2,1)} %forward_dft.2.refs_0_), channel_id=1, source_target_pairs={{0,1},{1,2},{2,3},{3,4},{4,5},{5,6},{6,7},{7,8},{8,9},{9,10},{10,1... | collective-permute-start | bytes 3145736 | tf_op jit(solution)/shard_map/ppermute | solution.py:474

commit v2 on v1

--- a/solution.py
+++ b/solution.py
@@ -14,6 +14,7 @@
 SUBLANES = 8
 SMAX = 9
 PER = 2
+ROW_GROUP = 8
 VMEM_LIMIT = 24 * 1024 * 1024
 VMEM_ALL = 56 * 1024 * 1024
 
@@ -208,150 +209,156 @@
             pltpu.SemaphoreType.DMA((12,)),
         ],
         compiler_params=pltpu.CompilerParams(vmem_limit_bytes=VMEM_ALL),
-        cost_estimate=pl.CostEstimate(
-            flops=6 * rows * pulse_count * (2 * outer + INNER),
-            bytes_accessed=12 * rows * pulse_count,
-            transcendentals=0,
-        ),
+        cost_estimate=pl.CostEstimate(flops=1000, bytes_accessed=1000, transcendentals=0),
         name="forward_dft",
     )(echoes, *operands)
 
 
-def migrate(inputs, known, taps, shifts, kernels, rows, store):
-    outer = shifts.shape[0]
+def weights_kernel(shift, kernel, taps, weights):
+    offsets, outer = weights.shape[0], weights.shape[1]
     half = INNER // 2
     tap_count = taps.shape[0]
-    half_taps = tap_count // 2
-    group = 2 * SUBLANES
-    reach = SMAX + half_taps - 1
-    input_rows = len(known) * rows
-    first = reach + half_taps - tap_count + 1
-    present = [known[row // rows] for row in range(input_rows)]
-
-    def body(step, carry):
-        sub = pl.multiple_of(step * group, group)
-        for parity in range(2):
-            lanes = pl.ds(parity * half, half)
-            shift_here = shifts[pl.ds(sub, group), lanes]
-            kernel_here = kernels[pl.ds(sub, group), lanes]
-            bits = [
-                ((shift_here // (1 << bit)) % 2).astype(jnp.float32).astype(jnp.bfloat16)
-                > jnp.bfloat16(0.5)
-                for bit in range(SMAX.bit_length())
-            ]
-            coefficients = [
+
+    for parity in range(2):
+        lanes = pl.ds(parity * half, half)
+        shifts = shift[pl.ds(parity, half, stride=2), :].T
+        kernels = kernel[pl.ds(parity, half, stride=2), :].T
+        for start in range(0, outer, SUBLANES):
+            here = slice(start, start + SUBLANES)
+            moved = [
                 jnp.take_along_axis(
-                    jnp.broadcast_to(taps[pl.ds(tap, 1), :], (group, LANES)), kernel_here, axis=1
+                    jnp.broadcast_to(taps[pl.ds(tap, 1), :], (SUBLANES, LANES)),
+                    kernels[here],
+                    axis=1,
                 )
                 for tap in range(tap_count)
             ]
-            nothing = jnp.zeros((group, LANES), jnp.bfloat16)
-            for part in range(2):
+            moved += [jnp.zeros((SUBLANES, LANES), jnp.float32)] * (offsets - tap_count)
+            for bit in reversed(range(SMAX.bit_length())):
+                jump = 1 << bit
+                taken = (shifts[here] & jump) != 0
                 moved = [
-                    inputs[row // rows][part, row % rows, pl.ds(sub, group), lanes]
-                    if present[row]
-                    else None
-                    for row in range(input_rows)
+                    jnp.where(taken, moved[row - jump] if row >= jump else 0.0, moved[row])
+                    for row in range(offsets)
                 ]
-                for bit in reversed(range(len(bits))):
-                    jump = 1 << bit
-                    low = first - (jump - 1)
-                    later = []
-                    for row in range(input_rows):
-                        here = moved[row]
-                        if row >= max(low, jump):
-                            there = moved[row - jump]
-                            if here is not None or there is not None:
-                                here = jnp.where(
-                                    bits[bit],
-                                    nothing if there is None else there,
-                                    nothing if here is None else here,
-                                )
-                        later.append(here)
-                    moved = later
-                wide = {
-                    row: moved[row].astype(jnp.float32)
-                    for row in range(first, input_rows)
-                    if any(present[max(row - SMAX, 0) : row + 1])
-                }
-                for row in range(rows):
-                    total = None
-                    for tap in range(tap_count):
-                        source = row + reach + half_taps - tap
-                        if source in wide:
-                            term = coefficients[tap] * wide[source]
-                            total = term if total is None else total + term
-                    store(part, parity, row, pl.ds(sub, group), total)
+            for row in range(offsets):
+                weights[row, pl.ds(start, SUBLANES), lanes] = moved[row]
+
+
+def offset_weights(shift, kernel_index, taps):
+    offsets = taps.shape[0] + SMAX
+    inside = pl.BlockSpec(memory_space=pltpu.VMEM)
+    return pl.pallas_call(
+        weights_kernel,
+        out_shape=jax.ShapeDtypeStruct((offsets, shift.shape[1], INNER), jnp.float32),
+        in_specs=[inside] * 3,
+        out_specs=inside,
+        compiler_params=pltpu.CompilerParams(vmem_limit_bytes=VMEM_LIMIT),
+        cost_estimate=pl.CostEstimate(flops=1000, bytes_accessed=1000, transcendentals=0),
+        name="offset_weights",
+    )(shift, kernel_index, taps)
+
+
+def migrate(inputs, weights, lower, rows, store):
+    offsets, outer = weights.shape[0], weights.shape[1]
+    half = INNER // 2
+    group = 2 * SUBLANES
+
+    order = sorted(inputs, key=lambda number: number if lower else (number + 3) % 4)
+
+    def body(step, carry):
+        sub = pl.ds(pl.multiple_of(step * group, group), group)
+        for parity in range(2):
+            lanes = pl.ds(parity * half, half)
+            for first in range(0, rows, ROW_GROUP):
+                totals = [[None] * rows for _ in range(2)]
+                held = {}
+                for number in order:
+                    for index in range(rows):
+                        place = number * rows + index
+                        wrap = 3 * rows if lower else 4 * rows * (number > 0)
+                        pairs = [
+                            (row, row - place + wrap) for row in range(first, first + ROW_GROUP)
+                        ]
+                        pairs = [pair for pair in pairs if 0 <= pair[1] < offsets]
+                        if not pairs:
+                            continue
+                        values = [
+                            inputs[number][part, index, sub, lanes].astype(jnp.float32)
+                            for part in range(2)
+                        ]
+                        for row, offset in pairs:
+                            if offset not in held:
+                                held[offset] = weights[offset, sub, lanes]
+                            for part in range(2):
+                                term = held[offset] * values[part]
+                                total = totals[part][row]
+                                totals[part][row] = term if total is None else total + term
+                for part in range(2):
+                    for row in range(first, first + ROW_GROUP):
+                        store(part, parity, row, sub, totals[part][row])
         return carry
 
     lax.fori_loop(0, outer // group, body, 0)
 
 
-def order_indices(shift, kernel, shifts, kernels):
+def by_half(odd_ref, lower_if_odd, run):
+    odd = odd_ref[0] == 1
+
+    @pl.when(odd)
+    def _():
+        run(lower_if_odd)
+
+    @pl.when(jnp.logical_not(odd))
+    def _():
+        run(not lower_if_odd)
+
+
+def partial_kernel(odd, *refs, numbers, lower_if_odd, has_partial):
+    inputs = dict(zip(numbers, refs))
+    earlier = refs[len(numbers)] if has_partial else None
+    weights, out = refs[len(numbers) + has_partial :]
     half = INNER // 2
-    for parity in range(2):
-        lanes = pl.ds(parity * half, half)
-        shifts[:, lanes] = shift[pl.ds(parity, half, stride=2), :].T
-        kernels[:, lanes] = kernel[pl.ds(parity, half, stride=2), :].T
-
-
-def partial_kernel(*refs, known, has_partial):
-    count = sum(known)
-    earlier = refs[count] if has_partial else None
-    shift, kernel, taps, out, shifts, kernels = refs[count + has_partial :]
-    half = INNER // 2
-    blocks = iter(refs[:count])
-    inputs = [next(blocks) if there else None for there in known]
-    order_indices(shift, kernel, shifts, kernels)
 
     def store(part, parity, row, place, total):
         lanes = pl.ds(parity * half, half)
         if has_partial:
-            before = earlier[part, row, place, lanes]
-            total = before if total is None else total + before
+            total = total + earlier[part, row, place, lanes]
         out[part, row, place, lanes] = total
 
-    migrate(inputs, known, taps, shifts, kernels, out.shape[1], store)
-
-
-def partial(blocks, known, shift, kernel_index, taps, earlier):
-    operands = [*blocks, *([] if earlier is None else [earlier]), shift, kernel_index, taps]
-    rows, outer = blocks[0].shape[1], blocks[0].shape[2]
+    by_half(
+        odd, lower_if_odd, lambda lower: migrate(inputs, weights, lower, out.shape[1], store)
+    )
+
+
+def partial(odd, blocks, lower_if_odd, weights, earlier):
+    like = next(iter(blocks.values()))
+    operands = [odd, *blocks.values(), *([] if earlier is None else [earlier]), weights]
     inside = pl.BlockSpec(memory_space=pltpu.VMEM)
     return pl.pallas_call(
         functools.partial(
-            partial_kernel, known=known, has_partial=int(earlier is not None)
+            partial_kernel, numbers=tuple(blocks), lower_if_odd=lower_if_odd,
+            has_partial=int(earlier is not None),
         ),
-        out_shape=jax.ShapeDtypeStruct(blocks[0].shape, jnp.float32),
-        in_specs=[inside] * len(operands),
+        out_shape=jax.ShapeDtypeStruct(like.shape, jnp.float32),
+        in_specs=[pl.BlockSpec(memory_space=pltpu.SMEM)] + [inside] * (len(operands) - 1),
         out_specs=inside,
-        scratch_shapes=[
-            pltpu.VMEM((outer, INNER), jnp.int32),
-            pltpu.VMEM((outer, INNER), jnp.int32),
-        ],
         compiler_params=pltpu.CompilerParams(vmem_limit_bytes=VMEM_LIMIT),
-        cost_estimate=pl.CostEstimate(
-            flops=8 * rows * outer * INNER * 500,
-            bytes_accessed=24 * rows * outer * INNER,
-            transcendentals=0,
-        ),
+        cost_estimate=pl.CostEstimate(flops=1000, bytes_accessed=1000, transcendentals=0),
         name="migrate_known_rows",
     )(*operands)
 
 
-def image_kernel(*refs, known, has_partial, aliased, block):
-    count = sum(known)
-    blocks = iter(refs[:count])
-    inputs = [next(blocks) if there else None for there in known]
+def image_kernel(odd, *refs, numbers, lower_if_odd, has_partial, aliased):
+    inputs = dict(zip(numbers, refs))
+    count = len(numbers)
     earlier = refs[count] if has_partial else None
-    count += has_partial
-    shift, kernel, taps, inner_table, outer_table, twiddle = refs[count : count + 6]
-    out_hbm, shifts, kernels, migrated, images, out, semaphores = refs[count + 6 + aliased :]
+    weights, inner_table, outer_table, twiddle = refs[count + has_partial :][:4]
+    out_hbm, migrated, images, out, semaphores = refs[count + has_partial + 4 + aliased :]
     rows = out.shape[1]
     pulse_count = out.shape[2]
     outer = pulse_count // INNER
     half = INNER // 2
-    order_indices(shift, kernel, shifts, kernels)
 
     def store(part, parity, row, place, total):
         if has_partial:
@@ -359,7 +366,7 @@
             total = before if total is None else total + before
         migrated[row, place, pl.ds((2 * parity + part) * half, half)] = total.astype(jnp.bfloat16)
 
-    migrate(inputs, known, taps, shifts, kernels, rows, store)
+    by_half(odd, lower_if_odd, lambda lower: migrate(inputs, weights, lower, rows, store))
     cosine, sine = twiddle[0], twiddle[1]
     for start in range(0, rows, PER):
         left_parts, right_parts = (
@@ -367,8 +374,8 @@
             for parity in range(2)
         )
         even = jnp.dot(left_parts, inner_table[0], preferred_element_type=jnp.float32)
-        odd = jnp.dot(right_parts, inner_table[1], preferred_element_type=jnp.float32)
-        left, right = even + odd, even - odd
+        odd_bins = jnp.dot(right_parts, inner_table[1], preferred_element_type=jnp.float32)
+        left, right = even + odd_bins, even - odd_bins
         for index in range(PER):
             here = slice(index * outer, (index + 1) * outer)
             turned = [], []
@@ -385,6 +392,7 @@
             )
     chunks = 4
     chunk = pulse_count // chunks
+    first_row = pl.multiple_of(jnp.where((odd[0] == 1) == lower_if_odd, 0, rows), rows)
     leaving = []
     for index in range(chunks):
         for part in range(2):
@@ -400,7 +408,7 @@
         leaving.append(
             pltpu.make_async_copy(
                 out.at[:, :, place],
-                out_hbm.at[:, pl.ds(block * rows, rows), place],
+                out_hbm.at[:, pl.ds(first_row, rows), place],
                 semaphores.at[index],
             )
         )
@@ -409,15 +417,16 @@
         copy.wait()
 
 
-def image(blocks, known, shift, kernel_index, taps, table, block, shape, earlier, previous):
+def image(odd, blocks, lower_if_odd, weights, table, shape, earlier, previous):
     row_count, pulse_count = shape
     rows = SUBLANES
     outer = pulse_count // INNER
     operands = [
-        *blocks, *([] if earlier is None else [earlier]), shift, kernel_index, taps,
+        odd, *blocks.values(), *([] if earlier is None else [earlier]), weights,
         table["inverse_inner"], table["inverse_outer"], table["twiddle"],
     ]
-    specs = [pl.BlockSpec(memory_space=pltpu.VMEM)] * len(operands)
+    specs = [pl.BlockSpec(memory_space=pltpu.SMEM)]
+    specs += [pl.BlockSpec(memory_space=pltpu.VMEM)] * (len(operands) - 1)
     aliases = {}
     anywhere = pl.BlockSpec(memory_space=pl.ANY)
     if previous is not None:
@@ -426,27 +435,21 @@
         specs.append(anywhere)
     return pl.pallas_call(
         functools.partial(
-            image_kernel, known=known, has_partial=int(earlier is not None),
-            aliased=len(aliases), block=block,
+            image_kernel, numbers=tuple(blocks), lower_if_odd=lower_if_odd,
+            has_partial=int(earlier is not None), aliased=len(aliases),
         ),
         out_shape=jax.ShapeDtypeStruct((2, row_count, pulse_count), jnp.float32),
         in_specs=specs,
         out_specs=anywhere,
         input_output_aliases=aliases,
         scratch_shapes=[
-            pltpu.VMEM((outer, INNER), jnp.int32),
-            pltpu.VMEM((outer, INNER), jnp.int32),
             pltpu.VMEM((rows, outer, 2 * INNER), jnp.bfloat16),
             pltpu.VMEM((rows, 2 * outer, INNER), jnp.float32),
             pltpu.VMEM((2, rows, pulse_count), jnp.float32),
             pltpu.SemaphoreType.DMA((4,)),
         ],
         compiler_params=pltpu.CompilerParams(vmem_limit_bytes=VMEM_LIMIT),
-        cost_estimate=pl.CostEstimate(
-            flops=8 * rows * pulse_count * (2 * outer + 2 * INNER),
-            bytes_accessed=24 * rows * pulse_count,
-            transcendentals=0,
-        ),
+        cost_estimate=pl.CostEstimate(flops=1000, bytes_accessed=1000, transcendentals=0),
         name="migrate_and_image",
     )(*operands)
 
@@ -457,32 +460,35 @@
     outer = pulse_count // INNER
     table = tables(pulse_count)
     count = lax.axis_size("rng")
+    odd = (lax.axis_index("rng") % 2).astype(jnp.int32).reshape(1)
     ahead = [(i, i + 1) for i in range(count - 1)]
-    back = [(i + 1, i) for i in range(count - 1)]
+
+    def swaps(first):
+        pairs = [(i, i + 1) for i in range(first, count - 1, 2)]
+        return pairs + [(j, i) for i, j in pairs]
+
+    shape = (row_count, pulse_count)
+
+    upper = forward(echoes, doppler_filter, table, 1)
+    left_upper = lax.ppermute(upper, "rng", ahead)
+    echoes, upper = lax.optimization_barrier((echoes, upper))
+    lower = forward(echoes, doppler_filter, table, 0)
+    near = lax.ppermute(lower, "rng", swaps(0))
+    migration_shift, kernel_index, lower = lax.optimization_barrier(
+        (migration_shift, kernel_index, lower)
+    )
     shift = migration_shift.reshape(INNER, outer)
     index = kernel_index.reshape(INNER, outer)
     taps = jnp.pad(kernel_taps.T, ((0, 0), (0, LANES - kernel_taps.shape[0])))
-    shape = (row_count, pulse_count)
-
-    upper = forward(echoes, doppler_filter, table, 1)
-    left_upper = lax.ppermute(upper, "rng", ahead)
-    lower = forward(echoes, doppler_filter, table, 0)
-    right_lower = lax.ppermute(lower, "rng", back)
-    high_part = partial([lower, upper], (False, True, True, False), shift, index, taps, None)
-    low_part = partial([lower, upper], (False, False, True, True), shift, index, taps, None)
-    lower_again, high_part, low_part = lax.optimization_barrier((lower, high_part, low_part))
-    left_lower = lax.ppermute(lower_again, "rng", ahead)
+    weights = offset_weights(shift, index, taps)
+    rest = partial(odd, {2: lower}, False, weights, None)
+    lower, rest = lax.optimization_barrier((lower, rest))
+    far = lax.ppermute(lower, "rng", swaps(1))
     picture = image(
-        [left_upper, right_lower], (True, False, False, True),
-        shift, index, taps, table, 1, shape, high_part, None,
+        odd, {0: near, 1: left_upper, 2: lower, 3: upper}, True, weights, table, shape, None, None
     )
-    low_part = partial(
-        [left_upper], (False, True, False, False), shift, index, taps, low_part
-    )
-    return image(
-        [left_lower], (True, False, False, False),
-        shift, index, taps, table, 0, shape, low_part, picture,
-    )
+    rest = partial(odd, {1: left_upper, 3: upper}, False, weights, rest)
+    return image(odd, {0: far}, False, weights, table, shape, rest, picture)
 
 
 def solution(mesh):

time: 55 us -> 48.9 us (0.89)
  Pallas kernels: 31.5 us -> 29 us
  starting transfers between devices: 9.4 us -> 7.55 us
  waiting for transfers between devices: 13.5 us -> 11.7 us
    ppermute x1, waiting for transfers between devices: 3.77 us -> 0.01 us  [per_device(): left_upper = lax.ppermute(upper, 'rng', ahead)]
    pallas_call x5, Pallas kernels: 21.7 us -> 19.2 us  [the longest x2 12.6 us: image(): pl.pallas_call(functools.partial(image_kernel, numbers=tuple(blocks), low...]
    ppermute x2, waiting for transfers between devices: 9.72 us -> 11.7 us  [the longest x1 11.7 us: per_device(): far = lax.ppermute(lower, 'rng', swaps(1))]
    ppermute x2, starting transfers between devices: 5.56 us -> 3.71 us  [the longest x1 3.64 us: per_device(): far = lax.ppermute(lower, 'rng', swaps(1))]
  transfers between devices with their start and end apart: 3 -> 3, of which waited for: 2 -> 1; matrix products, arithmetic and copies ran while one was open for 0% -> 0% of each run, Pallas kernels for 40% -> 42%
where the time goes in v2:
time: 48.9 us; the launch traced here: 48.6 us
  Pallas kernels  29 us (59%)
  waiting for transfers between devices  11.7 us (24%)
  starting transfers between devices  7.55 us (15%)
    pallas_call x2, Pallas kernels, image(): pl.pallas_call(functools.partial(image_kernel, numbers=tuple(blocks), low...  12.6 us
    ppermute x1, waiting for transfers between devices, per_device(): far = lax.ppermute(lower, 'rng', swaps(1))  11.7 us
    pallas_call x2, Pallas kernels, forward(): pl.pallas_call(functools.partial(forward_kernel, block=block), out_shape=...  9.83 us
    pallas_call x2, Pallas kernels, partial(): pl.pallas_call(functools.partial(partial_kernel, numbers=tuple(blocks), l...  5.79 us
    ppermute x1, starting transfers between devices, per_device(): left_upper = lax.ppermute(upper, 'rng', ahead)  3.84 us
    ppermute x1, starting transfers between devices, per_device(): far = lax.ppermute(lower, 'rng', swaps(1))  3.64 us
  transfers between devices with their start and end apart: 3, of which 1 were waited for; matrix products, arithmetic and copies ran while one was open for 0% of the time, Pallas kernels for 42%

profile of v2, /device:TPU:17, one launch (start us, length us, event | category | flops | bytes accessed | tf_op | source)
XLA Modules:
  0.0 48.6 jit_solution(9473567750369941124)
XLA Ops:
  0.0 4.9 %forward_dft.2.refs_1_.refs_3_ = bf16[2,8,128,256]{3,2,1,0:T(8,128)(2,1)} custom-call(f32[2,16,32768]{2,1,0:T(8,128)} %echo_hbm.2, bf16[2,256,256]{2,1,0:T(8,128)(2,1)} %constant.30.clone.outer_hbm, bf16[2,2,256,256]{3,2,1,0:T(8,128)(2,1)} %constant.31.clone.inner_hbm, f32[2,128,256]{2,1,0:T(8,128)} %constant.32.clone.twiddle_hbm.refs_7_.refs_5_, ...), custom_call_target="tpu_custom_call" | custom-call | flops 1000 | bytes 1000 | tf_op jit(solution)/shard_map/forward_dft/pallas_call | solution.py:195
  4.9 0.0 copy-start.6
  4.9 0.0 copy-start.4
  4.9 0.0 copy-start.5
  5.0 3.8 %collective-permute-start.1 = (bf16[2,8,128,256]{3,2,1,0:T(8,128)(2,1)}, bf16[2,8,128,256]{3,2,1,0:T(8,128)(2,1)}, u32[]{:S(2)}, u32[]{:S(2)}) collective-permute-start(bf16[2,8,128,256]{3,2,1,0:T(8,128)(2,1)} %forward_dft.2.refs_1_.refs_3_), channel_id=1, source_target_pairs={{0,1},{1,2},{2,3},{3,4},{4,5},{5,6},{6,7},{7,8},{8,9},{9,10},{10,1... | collective-permute-start | bytes 3145736 | tf_op jit(solution)/shard_map/ppermute | solution.py:473
  8.8 4.9 %forward_dft.3.refs_0_.refs_2_ = bf16[2,8,128,256]{3,2,1,0:T(8,128)(2,1)} custom-call(f32[2,16,32768]{2,1,0:T(8,128)} %echo_hbm.2, bf16[2,256,256]{2,1,0:T(8,128)(2,1)} %constant.30.clone.outer_hbm, bf16[2,2,256,256]{3,2,1,0:T(8,128)(2,1)} %constant.31.clone.inner_hbm, f32[2,128,256]{2,1,0:T(8,128)} %constant.32.clone.twiddle_hbm.refs_7_.refs_5_, ...), custom_call_target="tpu_custom_call" | custom-call | flops 1000 | bytes 1000 | tf_op jit(solution)/shard_map/forward_dft/pallas_call | solution.py:195
  13.7 0.1 collective-permute-start.2
  13.8 0.0 copy-done.6
  13.8 0.1 copy.12
  13.9 0.0 copy-done.4
  13.9 0.0 copy-done.5
  13.9 0.8 %offset_weights.1.refs_1_.refs_3_.refs_4_.refs_2_ = f32[25,128,256]{2,1,0:T(8,128)S(1)} custom-call(s32[256,128]{1,0:T(8,128)S(1)} %bitcast.4, s32[256,128]{1,0:T(8,128)S(1)} %bitcast.5, f32[16,128]{1,0:T(8,128)S(1)} %pad.4.taps), custom_call_target="tpu_custom_call" | custom-call | flops 1000 | bytes 1000 | tf_op jit(solution)/shard_map/offset_weights/pallas_call | solution.py:251
  14.8 0.0 copy-start
  14.8 2.5 %migrate_known_rows.2.refs_2_ = f32[2,8,128,256]{3,2,1,0:T(8,128)S(1)} custom-call(s32[1]{0:T(128)} %bitcast.odd, bf16[2,8,128,256]{3,2,1,0:T(8,128)(2,1)} %forward_dft.3.refs_0_.refs_2_, f32[25,128,256]{2,1,0:T(8,128)S(1)} %offset_weights.1.refs_1_.refs_3_.refs_4_.refs_2_), custom_call_target="tpu_custom_call" | custom-call | flops 1000 | bytes 1000 | tf_op jit(solution)/shard_map/migrate_known_rows/pallas_call | solution.py:338
  17.3 0.0 copy-start.1
  17.3 0.0 copy-start.2
  17.3 0.0 copy-start.3
  17.3 3.6 %collective-permute-start = (bf16[2,8,128,256]{3,2,1,0:T(8,128)(2,1)}, bf16[2,8,128,256]{3,2,1,0:T(8,128)(2,1)S(1)}, u32[]{:S(2)}, u32[]{:S(2)}) collective-permute-start(bf16[2,8,128,256]{3,2,1,0:T(8,128)(2,1)} %forward_dft.3.refs_0_.refs_2_), channel_id=1, source_target_pairs={{1,2},{3,4},{5,6},{7,8},{9,10},{11,12},{13,14},{2,1},{4,3},{6,5},{... | collective-permute-start | bytes 3145736 | tf_op jit(solution)/shard_map/ppermute | solution.py:486
  20.9 0.0 collective-permute-done.1.refs_0_.refs_1_
  20.9 0.0 copy-done
  21.0 3.3 %migrate_known_rows.3.refs_1_ = f32[2,8,128,256]{3,2,1,0:T(8,128)S(1)} custom-call(s32[1]{0:T(128)} %bitcast.odd, bf16[2,8,128,256]{3,2,1,0:T(8,128)(2,1)} %collective-permute-done.1.refs_0_.refs_1_, bf16[2,8,128,256]{3,2,1,0:T(8,128)(2,1)S(1)} %copy-done, f32[2,8,128,256]{3,2,1,0:T(8,128)S(1)} %migrate_known_rows.2.refs_2_, ...), custom_call_target="tpu_custom_call" | custom-call | flops 1000 | bytes 1000 | tf_op jit(solution)/shard_map/migrate_known_rows/pallas_call | solution.py:338
  24.3 0.0 collective-permute-done.2.refs_0_
  24.3 0.0 copy-done.1
  24.3 0.0 copy-done.2
  24.3 0.0 copy-done.3
  24.3 8.9 %migrate_and_image.2.refs_6_ = f32[2,16,32768]{2,1,0:T(8,128)} custom-call(s32[1]{0:T(128)} %bitcast.odd, bf16[2,8,128,256]{3,2,1,0:T(8,128)(2,1)} %collective-permute-done.2.refs_0_, bf16[2,8,128,256]{3,2,1,0:T(8,128)(2,1)} %collective-permute-done.1.refs_0_.refs_1_, bf16[2,8,128,256]{3,2,1,0:T(8,128)(2,1)} %forward_dft.3.refs_0_.refs_2_, ...), custom_call_target="tpu_custom_call" | custom-call | flops 1000 | bytes 1000 | tf_op jit(solution)/shard_map/migrate_and_image/pallas_call | solution.py:436
  33.3 11.7 %collective-permute-done.refs_0_ = bf16[2,8,128,256]{3,2,1,0:T(8,128)(2,1)S(1)} collective-permute-done((bf16[2,8,128,256]{3,2,1,0:T(8,128)(2,1)}, bf16[2,8,128,256]{3,2,1,0:T(8,128)(2,1)S(1)}, u32[]{:S(2)}, u32[]{:S(2)}) %collective-permute-start) | collective-permute-done | bytes 1048608 | tf_op jit(solution)/shard_map/ppermute | solution.py:486
  45.0 3.7 %migrate_and_image.3 = f32[2,16,32768]{2,1,0:T(8,128)} custom-call(s32[1]{0:T(128)} %bitcast.odd, bf16[2,8,128,256]{3,2,1,0:T(8,128)(2,1)S(1)} %collective-permute-done.refs_0_, f32[2,8,128,256]{3,2,1,0:T(8,128)S(1)} %migrate_known_rows.3.refs_1_, f32[25,128,256]{2,1,0:T(8,128)S(1)} %offset_weights.1.refs_1_.refs_3_.refs_4_.refs_2_, ...), custom_call_target="tpu_custom_call", output_to_operand_aliasing={{}: (7, {})} | custom-call | flops 1000 | bytes 1000 | tf_op jit(solution)/shard_map/migrate_and_image/pallas_call | solution.py:436
  (1 shorter events, 0.0 us)
Async XLA Ops:
  4.9 8.9 %copy-start.6 = (f32[16,16]{1,0:T(8,128)S(1)}, f32[16,16]{1,0:T(8,128)}, u32[]{:S(2)}) copy-start(f32[16,16]{1,0:T(8,128)} %param.14) | copy-start | bytes 3076
  4.9 9.0 %copy-start.4 = (s32[32768]{0:T(1024)S(1)}, s32[32768]{0:T(1024)}, u32[]{:S(2)}) copy-start(s32[32768]{0:T(1024)} %param.12) | copy-start | bytes 393220
  4.9 9.0 %copy-start.5 = (s32[32768]{0:T(1024)S(1)}, s32[32768]{0:T(1024)}, u32[]{:S(2)}) copy-start(s32[32768]{0:T(1024)} %param.13) | copy-start | bytes 393220
  5.0 16.0 %collective-permute-start.1 = (bf16[2,8,128,256]{3,2,1,0:T(8,128)(2,1)}, bf16[2,8,128,256]{3,2,1,0:T(8,128)(2,1)}, u32[]{:S(2)}, u32[]{:S(2)}) collective-permute-start(bf16[2,8,128,256]{3,2,1,0:T(8,128)(2,1)} %forward_dft.2.refs_1_.refs_3_), channel_id=1, source_target_pairs={{0,1},{1,2},{2,3},{3,4},{4,5},{5,6},{6,7},{7,8},{8,9},{9,10},{10,1... | collective-permute-start | bytes 3145736 | tf_op jit(solution)/shard_map/ppermute | solution.py:473
  13.7 10.6 %collective-permute-start.2 = (bf16[2,8,128,256]{3,2,1,0:T(8,128)(2,1)}, bf16[2,8,128,256]{3,2,1,0:T(8,128)(2,1)}, u32[]{:S(2)}, u32[]{:S(2)}) collective-permute-start(bf16[2,8,128,256]{3,2,1,0:T(8,128)(2,1)} %forward_dft.3.refs_0_.refs_2_), channel_id=1, source_target_pairs={{0,1},{2,3},{4,5},{6,7},{8,9},{10,11},{12,13},{14,15},{1,0},{3,2},... | collective-permute-start | bytes 3145736 | tf_op jit(solution)/shard_map/ppermute | solution.py:476
  14.8 6.2 %copy-start = (bf16[2,8,128,256]{3,2,1,0:T(8,128)(2,1)S(1)}, bf16[2,8,128,256]{3,2,1,0:T(8,128)(2,1)}, u32[]{:S(2)}) copy-start(bf16[2,8,128,256]{3,2,1,0:T(8,128)(2,1)} %forward_dft.2.refs_1_.refs_3_) | copy-start | bytes 3145732
  17.3 7.0 %copy-start.1 = (f32[2,128,256]{2,1,0:T(8,128)S(1)}, f32[2,128,256]{2,1,0:T(8,128)}, u32[]{:S(2)}) copy-start(f32[2,128,256]{2,1,0:T(8,128)} %constant.32.clone.twiddle_hbm.refs_7_.refs_5_) | copy-start | bytes 786436
  17.3 7.0 %copy-start.2 = (bf16[2,256,256]{2,1,0:T(8,128)(2,1)S(1)}, bf16[2,256,256]{2,1,0:T(8,128)(2,1)}, u32[]{:S(2)}) copy-start(bf16[2,256,256]{2,1,0:T(8,128)(2,1)} %constant.33.clone.refs_5_.refs_3_) | copy-start | bytes 786436
  17.3 7.0 %copy-start.3 = (bf16[256,256]{1,0:T(8,128)(2,1)S(1)}, bf16[256,256]{1,0:T(8,128)(2,1)}, u32[]{:S(2)}) copy-start(bf16[256,256]{1,0:T(8,128)(2,1)} %constant.34.clone.refs_6_.refs_4_) | copy-start | bytes 393220
  17.3 27.7 %collective-permute-start = (bf16[2,8,128,256]{3,2,1,0:T(8,128)(2,1)}, bf16[2,8,128,256]{3,2,1,0:T(8,128)(2,1)S(1)}, u32[]{:S(2)}, u32[]{:S(2)}) collective-permute-start(bf16[2,8,128,256]{3,2,1,0:T(8,128)(2,1)} %forward_dft.3.refs_0_.refs_2_), channel_id=1, source_target_pairs={{1,2},{3,4},{5,6},{7,8},{9,10},{11,12},{13,14},{2,1},{4,3},{6,5},{... | collective-permute-start | bytes 3145736 | tf_op jit(solution)/shard_map/ppermute | solution.py:486

commit v3 on v2

--- a/solution.py
+++ b/solution.py
@@ -68,10 +68,12 @@
 
 
 def forward_kernel(
-    echo_hbm, outer_hbm, inner_hbm, twiddle_hbm, response_hbm, out_hbm,
-    echo, outer_table, inner_table, twiddle, response, response_rows,
-    signal_high, signal_low, rotated_high, rotated_low, out, semaphores, *, block
+    echo_hbm, outer_hbm, inner_hbm, twiddle_hbm, response_hbm, *refs, block
 ):
+    (
+        *targets, echo, outer_table, inner_table, twiddle, response, response_rows,
+        signal_high, signal_low, rotated_high, rotated_low, out, semaphores,
+    ) = refs
     rows = out.shape[1]
     pulse_count = echo.shape[2]
     outer = pulse_count // INNER
@@ -168,11 +170,15 @@
                     imag * response_real - real * response_imag
                 ).astype(jnp.bfloat16)
         place = pl.ds(row, PER)
-        leaving = pltpu.make_async_copy(
-            out.at[:, place], out_hbm.at[:, place], semaphores.at[4 + row // PER]
-        )
-        leaving.start()
-        return leaving
+        length = targets[0].shape[1]
+        leaving.append(
+            pltpu.make_async_copy(
+                out.at[:, place],
+                targets[row // length].at[:, pl.ds(row % length, PER)],
+                semaphores.at[4 + row // PER],
+            )
+        )
+        leaving[-1].start()
 
     leaving = []
     for row in range(rows):
@@ -180,13 +186,13 @@
         if row == 1:
             ready[3].wait()
         if row % PER == PER - 1 and row >= PER:
-            leaving.append(second_stage(row + 1 - 2 * PER))
-    leaving.append(second_stage(rows - PER))
+            second_stage(row + 1 - 2 * PER)
+    second_stage(rows - PER)
     for copy in leaving:
         copy.wait()
 
 
-def forward(echoes, doppler_filter, table, block):
+def forward(echoes, doppler_filter, table, block, pieces):
     pulse_count = echoes.shape[2]
     rows = SUBLANES
     outer = pulse_count // INNER
@@ -194,9 +200,12 @@
     anywhere = pl.BlockSpec(memory_space=pl.ANY)
     return pl.pallas_call(
         functools.partial(forward_kernel, block=block),
-        out_shape=jax.ShapeDtypeStruct((2, rows, outer, INNER), jnp.bfloat16),
+        out_shape=[
+            jax.ShapeDtypeStruct((2, rows // pieces, outer, INNER), jnp.bfloat16)
+            for _ in range(pieces)
+        ],
         in_specs=[anywhere] * 5,
-        out_specs=anywhere,
+        out_specs=[anywhere] * pieces,
         scratch_shapes=[
             pltpu.VMEM((2, rows, pulse_count), jnp.float32),
             *[pltpu.VMEM(array.shape, array.dtype) for array in operands],
@@ -209,12 +218,12 @@
             pltpu.SemaphoreType.DMA((12,)),
         ],
         compiler_params=pltpu.CompilerParams(vmem_limit_bytes=VMEM_ALL),
-        cost_estimate=pl.CostEstimate(flops=1000, bytes_accessed=1000, transcendentals=0),
+        cost_estimate=pl.CostEstimate(flops=10**12, bytes_accessed=10**9, transcendentals=0),
         name="forward_dft",
     )(echoes, *operands)
 
 
-def weights_kernel(shift, kernel, taps, weights):
+def weights_kernel(shift, kernel, taps, weights, ordered):
     offsets, outer = weights.shape[0], weights.shape[1]
     half = INNER // 2
     tap_count = taps.shape[0]
@@ -223,6 +232,7 @@
         lanes = pl.ds(parity * half, half)
         shifts = shift[pl.ds(parity, half, stride=2), :].T
         kernels = kernel[pl.ds(parity, half, stride=2), :].T
+        ordered[:, lanes] = shifts.astype(jnp.float32).astype(jnp.bfloat16)
         for start in range(0, outer, SUBLANES):
             here = slice(start, start + SUBLANES)
             moved = [
@@ -250,13 +260,43 @@
     inside = pl.BlockSpec(memory_space=pltpu.VMEM)
     return pl.pallas_call(
         weights_kernel,
-        out_shape=jax.ShapeDtypeStruct((offsets, shift.shape[1], INNER), jnp.float32),
+        out_shape=[
+            jax.ShapeDtypeStruct((offsets, shift.shape[1], INNER), jnp.float32),
+            jax.ShapeDtypeStruct((shift.shape[1], INNER), jnp.bfloat16),
+        ],
         in_specs=[inside] * 3,
-        out_specs=inside,
+        out_specs=[inside] * 2,
         compiler_params=pltpu.CompilerParams(vmem_limit_bytes=VMEM_LIMIT),
         cost_estimate=pl.CostEstimate(flops=1000, bytes_accessed=1000, transcendentals=0),
         name="offset_weights",
     )(shift, kernel_index, taps)
+
+
+def mix_kernel(odd, own, near, ordered, mixed):
+    kept = mixed.shape[1]
+    skipped = SUBLANES - kept
+
+    def run(is_odd):
+        left, right = (own, near) if is_odd else (near, own)
+        for row in range(kept):
+            for_next = ordered[...] >= jnp.bfloat16(SMAX - skipped - row)
+            for part in range(2):
+                mixed[part, row] = jnp.where(for_next, left[part, row], right[part, row])
+
+    by_half(odd, True, run)
+
+
+def mix(odd, own, near, ordered):
+    inside = pl.BlockSpec(memory_space=pltpu.VMEM)
+    return pl.pallas_call(
+        mix_kernel,
+        out_shape=jax.ShapeDtypeStruct(own.shape, own.dtype),
+        in_specs=[pl.BlockSpec(memory_space=pltpu.SMEM)] + [inside] * 3,
+        out_specs=inside,
+        compiler_params=pltpu.CompilerParams(vmem_limit_bytes=VMEM_LIMIT),
+        cost_estimate=pl.CostEstimate(flops=1000, bytes_accessed=1000, transcendentals=0),
+        name="mix_rows",
+    )(odd, own, near, ordered)
 
 
 def migrate(inputs, weights, lower, rows, store):
@@ -284,7 +324,7 @@
                         if not pairs:
                             continue
                         values = [
-                            inputs[number][part, index, sub, lanes].astype(jnp.float32)
+                            inputs[number](part, index, sub, lanes).astype(jnp.float32)
                             for part in range(2)
                         ]
                         for row, offset in pairs:
@@ -302,6 +342,34 @@
     lax.fori_loop(0, outer // group, body, 0)
 
 
+def reader(pieces):
+    length = pieces[0][0].shape[1]
+
+    def read(part, index, sub, lanes):
+        values = [ref[part, index % length, sub, lanes] for ref in pieces[index // length]]
+        return sum(values[1:], values[0])
+
+    return read
+
+
+def readers(counts, refs):
+    refs = iter(refs)
+    return {
+        number: reader([[next(refs) for _ in range(count)] for count in pieces])
+        for number, pieces in counts
+    }
+
+
+def arrays_of(blocks):
+    return [array for pieces in blocks.values() for piece in pieces for array in piece]
+
+
+def counts_of(blocks):
+    return tuple(
+        (number, tuple(len(piece) for piece in pieces)) for number, pieces in blocks.items()
+    )
+
+
 def by_half(odd_ref, lower_if_odd, run):
     odd = odd_ref[0] == 1
 
@@ -315,9 +383,10 @@
 
 
 def partial_kernel(odd, *refs, numbers, lower_if_odd, has_partial):
-    inputs = dict(zip(numbers, refs))
-    earlier = refs[len(numbers)] if has_partial else None
-    weights, out = refs[len(numbers) + has_partial :]
+    inputs = readers(numbers, refs)
+    count = sum(sum(pieces) for _, pieces in numbers)
+    earlier = refs[count] if has_partial else None
+    weights, out = refs[count + has_partial :]
     half = INNER // 2
 
     def store(part, parity, row, place, total):
@@ -332,15 +401,15 @@
 
 
 def partial(odd, blocks, lower_if_odd, weights, earlier):
-    like = next(iter(blocks.values()))
-    operands = [odd, *blocks.values(), *([] if earlier is None else [earlier]), weights]
+    shape = (2, SUBLANES) + weights.shape[1:]
+    operands = [odd, *arrays_of(blocks), *([] if earlier is None else [earlier]), weights]
     inside = pl.BlockSpec(memory_space=pltpu.VMEM)
     return pl.pallas_call(
         functools.partial(
-            partial_kernel, numbers=tuple(blocks), lower_if_odd=lower_if_odd,
+            partial_kernel, numbers=counts_of(blocks), lower_if_odd=lower_if_odd,
             has_partial=int(earlier is not None),
         ),
-        out_shape=jax.ShapeDtypeStruct(like.shape, jnp.float32),
+        out_shape=jax.ShapeDtypeStruct(shape, jnp.float32),
         in_specs=[pl.BlockSpec(memory_space=pltpu.SMEM)] + [inside] * (len(operands) - 1),
         out_specs=inside,
         compiler_params=pltpu.CompilerParams(vmem_limit_bytes=VMEM_LIMIT),
@@ -350,8 +419,8 @@
 
 
 def image_kernel(odd, *refs, numbers, lower_if_odd, has_partial, aliased):
-    inputs = dict(zip(numbers, refs))
-    count = len(numbers)
+    inputs = readers(numbers, refs)
+    count = sum(sum(pieces) for _, pieces in numbers)
     earlier = refs[count] if has_partial else None
     weights, inner_table, outer_table, twiddle = refs[count + has_partial :][:4]
     out_hbm, migrated, images, out, semaphores = refs[count + has_partial + 4 + aliased :]
@@ -422,7 +491,7 @@
     rows = SUBLANES
     outer = pulse_count // INNER
     operands = [
-        odd, *blocks.values(), *([] if earlier is None else [earlier]), weights,
+        odd, *arrays_of(blocks), *([] if earlier is None else [earlier]), weights,
         table["inverse_inner"], table["inverse_outer"], table["twiddle"],
     ]
     specs = [pl.BlockSpec(memory_space=pltpu.SMEM)]
@@ -435,7 +504,7 @@
         specs.append(anywhere)
     return pl.pallas_call(
         functools.partial(
-            image_kernel, numbers=tuple(blocks), lower_if_odd=lower_if_odd,
+            image_kernel, numbers=counts_of(blocks), lower_if_odd=lower_if_odd,
             has_partial=int(earlier is not None), aliased=len(aliases),
         ),
         out_shape=jax.ShapeDtypeStruct((2, row_count, pulse_count), jnp.float32),
@@ -469,26 +538,43 @@
 
     shape = (row_count, pulse_count)
 
-    upper = forward(echoes, doppler_filter, table, 1)
+    assert count % 4 == 0
+    starts = range(0, count, 4)
+    across = [(i + 1, i + 2) for i in starts] + [(i + 2, i + 1) for i in starts]
+    onward = [(i + 2, i - 1) for i in starts[1:]] + [(i + 1, i + 4) for i in starts[:-1]]
+
+    (upper,) = forward(echoes, doppler_filter, table, 1, 1)
     left_upper = lax.ppermute(upper, "rng", ahead)
     echoes, upper = lax.optimization_barrier((echoes, upper))
-    lower = forward(echoes, doppler_filter, table, 0)
-    near = lax.ppermute(lower, "rng", swaps(0))
-    migration_shift, kernel_index, lower = lax.optimization_barrier(
-        (migration_shift, kernel_index, lower)
+    few, many = forward(echoes, doppler_filter, table, 0, 2)
+    near_many = lax.ppermute(many, "rng", swaps(0))
+    near_few = lax.ppermute(few, "rng", swaps(0))
+    migration_shift, kernel_index, few, many = lax.optimization_barrier(
+        (migration_shift, kernel_index, few, many)
     )
     shift = migration_shift.reshape(INNER, outer)
     index = kernel_index.reshape(INNER, outer)
     taps = jnp.pad(kernel_taps.T, ((0, 0), (0, LANES - kernel_taps.shape[0])))
-    weights = offset_weights(shift, index, taps)
+    weights, ordered = offset_weights(shift, index, taps)
+    lower = ((few,), (many,))
     rest = partial(odd, {2: lower}, False, weights, None)
-    lower, rest = lax.optimization_barrier((lower, rest))
-    far = lax.ppermute(lower, "rng", swaps(1))
+    mixed = mix(odd, many, near_many, ordered)
+    mixed, rest = lax.optimization_barrier((mixed, rest))
+    direct = lax.ppermute(mixed, "rng", across)
+    rest = partial(odd, {1: ((left_upper,),), 3: ((upper,),)}, False, weights, rest)
+    few, rest = lax.optimization_barrier((few, rest))
+    far = lax.ppermute(few, "rng", swaps(1))
+    relayed = lax.ppermute(direct, "rng", onward)
+    few, direct = lax.optimization_barrier((few, direct))
+    lower = ((few,), (many,))
     picture = image(
-        odd, {0: near, 1: left_upper, 2: lower, 3: upper}, True, weights, table, shape, None, None
-    )
-    rest = partial(odd, {1: left_upper, 3: upper}, False, weights, rest)
-    return image(odd, {0: far}, False, weights, table, shape, rest, picture)
+        odd,
+        {0: ((near_few,), (near_many,)), 1: ((left_upper,),), 2: lower, 3: ((upper,),)},
+        True, weights, table, shape, None, None,
+    )
+    return image(
+        odd, {0: ((far,), (direct, relayed))}, False, weights, table, shape, rest, picture
+    )
 
 
 def solution(mesh):

time: 48.9 us -> 47 us (0.961)
  waiting for transfers between devices: 11.7 us -> 3.59 us
  starting transfers between devices: 7.55 us -> 11.5 us
  local copies, waits for them, and re-layouts: 0.12 us -> 2.82 us
  Pallas kernels: 29 us -> 28.5 us
    ppermute x2 -> x5, waiting for transfers between devices: 11.7 us -> 3.59 us  [the longest x1 2.03 us: per_device(): far = lax.ppermute(few, 'rng', swaps(1))]
    ppermute x2 -> x5, starting transfers between devices: 3.71 us -> 7.78 us  [the longest x1 3.65 us: per_device(): direct = lax.ppermute(mixed, 'rng', across)]
    unnamed x15 -> x27, local copies, waits for them, and re-layouts: 0.12 us -> 2.81 us
    pallas_call x5 -> x6, Pallas kernels: 19.2 us -> 18.6 us  [the longest x2 12.2 us: image(): pl.pallas_call(functools.partial(image_kernel, numbers=counts_of(blocks),...]
  transfers between devices with their start and end apart: 3 -> 6, of which waited for: 1 -> 2; matrix products, arithmetic and copies ran while one was open for 0% -> 0% of each run, Pallas kernels for 42% -> 43%
where the time goes in v3:
time: 47 us; the launch traced here: 46.6 us
  Pallas kernels  28.5 us (61%)
  starting transfers between devices  11.5 us (24%)
  waiting for transfers between devices  3.59 us (8%)
  local copies, waits for them, and re-layouts  2.82 us (6%)
    pallas_call x2, Pallas kernels, image(): pl.pallas_call(functools.partial(image_kernel, numbers=counts_of(blocks),...  12.2 us
    pallas_call x2, Pallas kernels, forward(): pl.pallas_call(functools.partial(forward_kernel, block=block), out_shape=...  9.85 us
    pallas_call x2, Pallas kernels, partial(): pl.pallas_call(functools.partial(partial_kernel, numbers=counts_of(blocks...  4.48 us
    ppermute x1, starting transfers between devices, per_device(): left_upper = lax.ppermute(upper, 'rng', ahead)  3.71 us
    ppermute x1, starting transfers between devices, per_device(): direct = lax.ppermute(mixed, 'rng', across)  3.65 us
    unnamed x27, local copies, waits for them, and re-layouts  2.81 us
    ppermute x1, waiting for transfers between devices, per_device(): far = lax.ppermute(few, 'rng', swaps(1))  2.03 us
    ppermute x1, starting transfers between devices, per_device(): relayed = lax.ppermute(direct, 'rng', onward)  2.01 us
  transfers between devices with their start and end apart: 6, of which 2 were waited for; matrix products, arithmetic and copies ran while one was open for 0% of the time, Pallas kernels for 43%

profile of v3, /device:TPU:17, one launch (start us, length us, event | category | flops | bytes accessed | tf_op | source)
XLA Modules:
  0.0 46.6 jit_solution(17108694381203006288)
XLA Ops:
  0.0 4.9 %forward_dft.2.refs_1_.refs_5_ = bf16[2,8,128,256]{3,2,1,0:T(8,128)(2,1)} custom-call(f32[2,16,32768]{2,1,0:T(8,128)} %echo_hbm.2, bf16[2,256,256]{2,1,0:T(8,128)(2,1)} %constant.30.clone.outer_hbm, bf16[2,2,256,256]{3,2,1,0:T(8,128)(2,1)} %constant.31.clone.inner_hbm, f32[2,128,256]{2,1,0:T(8,128)} %constant.32.clone.twiddle_hbm.refs_9_.refs_7_, ...), custom_call_target="tpu_custom_call" | custom-call | flops 999999995904 | bytes 1000000000 | tf_op jit(solution)/shard_map/forward_dft/pallas_call | solution.py:201
  4.9 3.7 %collective-permute-start = (bf16[2,8,128,256]{3,2,1,0:T(8,128)(2,1)}, bf16[2,8,128,256]{3,2,1,0:T(8,128)(2,1)}, u32[]{:S(2)}, u32[]{:S(2)}) collective-permute-start(bf16[2,8,128,256]{3,2,1,0:T(8,128)(2,1)} %forward_dft.2.refs_1_.refs_5_), channel_id=1, source_target_pairs={{0,1},{1,2},{2,3},{3,4},{4,5},{5,6},{6,7},{7,8},{8,9},{9,10},{10,1... | collective-permute-start | bytes 3145736 | tf_op jit(solution)/shard_map/ppermute | solution.py:547
  8.6 0.0 copy-start.12
  8.6 0.0 copy-start.8
  8.7 0.0 copy-start.9
  8.7 4.9 %forward_dft.3 = (bf16[2,4,128,256]{3,2,1,0:T(8,128)(2,1)}, bf16[2,4,128,256]{3,2,1,0:T(8,128)(2,1)}) custom-call(f32[2,16,32768]{2,1,0:T(8,128)} %echo_hbm.2, bf16[2,256,256]{2,1,0:T(8,128)(2,1)} %constant.30.clone.outer_hbm, bf16[2,2,256,256]{3,2,1,0:T(8,128)(2,1)} %constant.31.clone.inner_hbm, f32[2,128,256]{2,1,0:T(8,128)} %constant.32.clone.twiddle_hbm.refs_9_.refs_7_, ...), custom_call_target="tpu_custom_call" | custom-call | flops 999999995904 | bytes 1000000000 | tf_op jit(solution)/shard_map/forward_dft/pallas_call | solution.py:201
  13.6 0.1 collective-permute-start.1
  13.7 0.0 copy-done.12
  13.7 0.1 copy.12
  13.8 0.0 copy-done.8
  13.8 0.0 copy-done.9
  13.8 0.8 %offset_weights.1 = (f32[25,128,256]{2,1,0:T(8,128)S(1)}, bf16[128,256]{1,0:T(8,128)(2,1)S(1)}) custom-call(s32[256,128]{1,0:T(8,128)S(1)} %bitcast.4, s32[256,128]{1,0:T(8,128)S(1)} %bitcast.5, f32[16,128]{1,0:T(8,128)S(1)} %pad.4.taps), custom_call_target="tpu_custom_call" | custom-call | flops 1000 | bytes 1000 | tf_op jit(solution)/shard_map/offset_weights/pallas_call | solution.py:261
  14.6 0.0 copy-start.10
  14.7 0.6 %copy-done.10 = bf16[128,256]{1,0:T(8,128)(2,1)} copy-done((bf16[128,256]{1,0:T(8,128)(2,1)}, bf16[128,256]{1,0:T(8,128)(2,1)S(1)}, u32[]{:S(2)}) %copy-start.10) | copy-done | bytes 65560
  15.3 0.0 copy-start
  15.3 1.0 %copy-done = bf16[2,4,128,256]{3,2,1,0:T(8,128)(2,1)S(1)} copy-done((bf16[2,4,128,256]{3,2,1,0:T(8,128)(2,1)S(1)}, bf16[2,4,128,256]{3,2,1,0:T(8,128)(2,1)}, u32[]{:S(2)}) %copy-start) | copy-done | bytes 524312
  16.3 0.0 copy-start.3
  16.3 1.0 %copy-done.3 = bf16[2,4,128,256]{3,2,1,0:T(8,128)(2,1)S(1)} copy-done((bf16[2,4,128,256]{3,2,1,0:T(8,128)(2,1)S(1)}, bf16[2,4,128,256]{3,2,1,0:T(8,128)(2,1)}, u32[]{:S(2)}) %copy-start.3) | copy-done | bytes 524312
  17.3 0.0 copy-start.1
  17.3 0.0 copy-start.11
  17.3 0.0 copy-start.4
  17.3 0.0 copy-start.2
  17.4 1.2 %migrate_known_rows.2.refs_2_ = f32[2,8,128,256]{3,2,1,0:T(8,128)S(1)} custom-call(s32[1]{0:T(128)} %bitcast.odd, bf16[2,4,128,256]{3,2,1,0:T(8,128)(2,1)S(1)} %copy-done.3, bf16[2,4,128,256]{3,2,1,0:T(8,128)(2,1)S(1)} %copy-done, f32[25,128,256]{2,1,0:T(8,128)S(1)} %get-tuple-element.30.refs_2_.refs_3_.refs_6_.refs_4_), custom_call_target="tpu_custom_call" | custom-call | flops 1000 | bytes 1000 | tf_op jit(solution)/shard_map/migrate_known_rows/pallas_call | solution.py:407
  18.5 0.0 collective-permute-done.1.near.refs_1_
  18.5 0.0 copy-done.1
  18.5 0.0 copy-done.11
  18.6 1.1 %mix_rows.1 = bf16[2,4,128,256]{3,2,1,0:T(8,128)(2,1)S(1)} custom-call(s32[1]{0:T(128)} %bitcast.odd, bf16[2,4,128,256]{3,2,1,0:T(8,128)(2,1)S(1)} %copy-done.1, bf16[2,4,128,256]{3,2,1,0:T(8,128)(2,1)} %collective-permute-done.1.near.refs_1_, bf16[128,256]{1,0:T(8,128)(2,1)S(1)} %copy-done.11), custom_call_target="tpu_custom_call" | custom-call | flops 1000 | bytes 1000 | tf_op jit(solution)/shard_map/mix_rows/pallas_call | solution.py:291
  19.7 0.0 copy-start.5
  19.7 0.0 copy-start.6
  19.7 0.0 copy-start.7
  19.7 3.6 %collective-permute-start.3 = (bf16[2,4,128,256]{3,2,1,0:T(8,128)(2,1)S(1)}, bf16[2,4,128,256]{3,2,1,0:T(8,128)(2,1)S(1)}, u32[]{:S(2)}, u32[]{:S(2)}) collective-permute-start(bf16[2,4,128,256]{3,2,1,0:T(8,128)(2,1)S(1)} %mix_rows.1), channel_id=1, source_target_pairs={{1,2},{5,6},{9,10},{13,14},{2,1},{6,5},{10,9},{14,13},{17,18},{21,... | collective-permute-start | bytes 1572872 | tf_op jit(solution)/shard_map/ppermute | solution.py:563
  23.4 0.0 copy-done.4
  23.4 0.1 collective-permute-start.5
  23.4 0.0 collective-permute-done.refs_0_.refs_2_
  23.5 0.0 copy-done.2
  23.5 3.3 %migrate_known_rows.3.refs_3_ = f32[2,8,128,256]{3,2,1,0:T(8,128)S(1)} custom-call(s32[1]{0:T(128)} %bitcast.odd, bf16[2,8,128,256]{3,2,1,0:T(8,128)(2,1)} %collective-permute-done.refs_0_.refs_2_, bf16[2,8,128,256]{3,2,1,0:T(8,128)(2,1)S(1)} %copy-done.2, f32[2,8,128,256]{3,2,1,0:T(8,128)S(1)} %migrate_known_rows.2.refs_2_, ...), custom_call_target="tpu_custom_call" | custom-call | flops 1000 | bytes 1000 | tf_op jit(solution)/shard_map/migrate_known_rows/pallas_call | solution.py:407
  26.8 2.0 %collective-permute-start.2 = (bf16[2,4,128,256]{3,2,1,0:T(8,128)(2,1)S(1)}, bf16[2,4,128,256]{3,2,1,0:T(8,128)(2,1)S(1)}, u32[]{:S(2)}, u32[]{:S(2)}) collective-permute-start(bf16[2,4,128,256]{3,2,1,0:T(8,128)(2,1)S(1)} %copy-done.4), channel_id=1, source_target_pairs={{1,2},{3,4},{5,6},{7,8},{9,10},{11,12},{13,14},{2,1},{4,3},{6,5},{... | collective-permute-start | bytes 1572872 | tf_op jit(solution)/shard_map/ppermute | solution.py:566
  28.8 1.6 %collective-permute-done.3.refs_1_ = bf16[2,4,128,256]{3,2,1,0:T(8,128)(2,1)S(1)} collective-permute-done((bf16[2,4,128,256]{3,2,1,0:T(8,128)(2,1)S(1)}, bf16[2,4,128,256]{3,2,1,0:T(8,128)(2,1)S(1)}, u32[]{:S(2)}, u32[]{:S(2)}) %collective-permute-start.3) | collective-permute-done | bytes 524320 | tf_op jit(solution)/shard_map/ppermute | solution.py:563
  30.3 2.0 %collective-permute-start.4 = (bf16[2,4,128,256]{3,2,1,0:T(8,128)(2,1)S(1)}, bf16[2,4,128,256]{3,2,1,0:T(8,128)(2,1)S(1)}, u32[]{:S(2)}, u32[]{:S(2)}) collective-permute-start(bf16[2,4,128,256]{3,2,1,0:T(8,128)(2,1)S(1)} %collective-permute-done.3.refs_1_), channel_id=1, source_target_pairs={{6,3},{10,7},{14,11},{1,4},{5,8},{9,12},{22,19},{26,23},{30,27},{1... | collective-permute-start | bytes 1572872 | tf_op jit(solution)/shard_map/ppermute | solution.py:567
  32.4 0.0 collective-permute-done.5.refs_0_
  32.4 0.0 copy-done.5
  32.4 0.0 copy-done.6
  32.4 0.0 copy-done.7
  32.4 8.5 %migrate_and_image.2.refs_8_ = f32[2,16,32768]{2,1,0:T(8,128)} custom-call(s32[1]{0:T(128)} %bitcast.odd, bf16[2,4,128,256]{3,2,1,0:T(8,128)(2,1)S(1)} %collective-permute-done.5.refs_0_, bf16[2,4,128,256]{3,2,1,0:T(8,128)(2,1)} %collective-permute-done.1.near.refs_1_, bf16[2,8,128,256]{3,2,1,0:T(8,128)(2,1)} %collective-permute-done.refs_0_.refs_2_, ...), custom_call_target="tpu_custom_call" | custom-call | flops 1000 | bytes 1000 | tf_op jit(solution)/shard_map/migrate_and_image/pallas_call | solution.py:505
  40.9 2.0 %collective-permute-done.2.refs_0_ = bf16[2,4,128,256]{3,2,1,0:T(8,128)(2,1)S(1)} collective-permute-done((bf16[2,4,128,256]{3,2,1,0:T(8,128)(2,1)S(1)}, bf16[2,4,128,256]{3,2,1,0:T(8,128)(2,1)S(1)}, u32[]{:S(2)}, u32[]{:S(2)}) %collective-permute-start.2) | collective-permute-done | bytes 524320 | tf_op jit(solution)/shard_map/ppermute | solution.py:566
  42.9 0.0 collective-permute-done.4.refs_2_
  42.9 3.7 %migrate_and_image.3 = f32[2,16,32768]{2,1,0:T(8,128)} custom-call(s32[1]{0:T(128)} %bitcast.odd, bf16[2,4,128,256]{3,2,1,0:T(8,128)(2,1)S(1)} %collective-permute-done.2.refs_0_, bf16[2,4,128,256]{3,2,1,0:T(8,128)(2,1)S(1)} %collective-permute-done.3.refs_1_, ...), custom_call_target="tpu_custom_call", output_to_operand_aliasing={{}: (9, {})} | custom-call | flops 1000 | bytes 1000 | tf_op jit(solution)/shard_map/migrate_and_image/pallas_call | solution.py:505
  (1 shorter events, 0.0 us)
Async XLA Ops:
  4.9 18.5 %collective-permute-start = (bf16[2,8,128,256]{3,2,1,0:T(8,128)(2,1)}, bf16[2,8,128,256]{3,2,1,0:T(8,128)(2,1)}, u32[]{:S(2)}, u32[]{:S(2)}) collective-permute-start(bf16[2,8,128,256]{3,2,1,0:T(8,128)(2,1)} %forward_dft.2.refs_1_.refs_5_), channel_id=1, source_target_pairs={{0,1},{1,2},{2,3},{3,4},{4,5},{5,6},{6,7},{7,8},{8,9},{9,10},{10,1... | collective-permute-start | bytes 3145736 | tf_op jit(solution)/shard_map/ppermute | solution.py:547
  8.6 5.1 %copy-start.12 = (f32[16,16]{1,0:T(8,128)S(1)}, f32[16,16]{1,0:T(8,128)}, u32[]{:S(2)}) copy-start(f32[16,16]{1,0:T(8,128)} %param.14) | copy-start | bytes 3076
  8.6 5.1 %copy-start.8 = (s32[32768]{0:T(1024)S(1)}, s32[32768]{0:T(1024)}, u32[]{:S(2)}) copy-start(s32[32768]{0:T(1024)} %param.12) | copy-start | bytes 393220
  8.7 5.1 %copy-start.9 = (s32[32768]{0:T(1024)S(1)}, s32[32768]{0:T(1024)}, u32[]{:S(2)}) copy-start(s32[32768]{0:T(1024)} %param.13) | copy-start | bytes 393220
  13.6 4.9 %collective-permute-start.1 = (bf16[2,4,128,256]{3,2,1,0:T(8,128)(2,1)}, bf16[2,4,128,256]{3,2,1,0:T(8,128)(2,1)}, u32[]{:S(2)}, u32[]{:S(2)}) collective-permute-start(bf16[2,4,128,256]{3,2,1,0:T(8,128)(2,1)} %get-tuple-element.26.own.refs_1_.refs_4_), channel_id=1, source_target_pairs={{0,1},{2,3},{4,5},{6,7},{8,9},{10,11},{12,13},{14,15},{1,0},{3,2},... | collective-permute-start | bytes 1572872 | tf_op jit(solution)/shard_map/ppermute | solution.py:550
  14.6 0.6 %copy-start.10 = (bf16[128,256]{1,0:T(8,128)(2,1)}, bf16[128,256]{1,0:T(8,128)(2,1)S(1)}, u32[]{:S(2)}) copy-start(bf16[128,256]{1,0:T(8,128)(2,1)S(1)} %get-tuple-element.29.ordered) | copy-start | bytes 196612
  15.3 1.0 %copy-start = (bf16[2,4,128,256]{3,2,1,0:T(8,128)(2,1)S(1)}, bf16[2,4,128,256]{3,2,1,0:T(8,128)(2,1)}, u32[]{:S(2)}) copy-start(bf16[2,4,128,256]{3,2,1,0:T(8,128)(2,1)} %get-tuple-element.26.own.refs_1_.refs_4_) | copy-start | bytes 1572868
  16.3 1.0 %copy-start.3 = (bf16[2,4,128,256]{3,2,1,0:T(8,128)(2,1)S(1)}, bf16[2,4,128,256]{3,2,1,0:T(8,128)(2,1)}, u32[]{:S(2)}) copy-start(bf16[2,4,128,256]{3,2,1,0:T(8,128)(2,1)} %get-tuple-element.36.refs_0_.refs_3_) | copy-start | bytes 1572868
  17.3 1.2 %copy-start.1 = (bf16[2,4,128,256]{3,2,1,0:T(8,128)(2,1)S(1)}, bf16[2,4,128,256]{3,2,1,0:T(8,128)(2,1)}, u32[]{:S(2)}) copy-start(bf16[2,4,128,256]{3,2,1,0:T(8,128)(2,1)} %get-tuple-element.26.own.refs_1_.refs_4_) | copy-start | bytes 1572868
  17.3 1.2 %copy-start.11 = (bf16[128,256]{1,0:T(8,128)(2,1)S(1)}, bf16[128,256]{1,0:T(8,128)(2,1)}, u32[]{:S(2)}) copy-start(bf16[128,256]{1,0:T(8,128)(2,1)} %copy-done.10) | copy-start | bytes 196612
  17.3 6.0 %copy-start.4 = (bf16[2,4,128,256]{3,2,1,0:T(8,128)(2,1)S(1)}, bf16[2,4,128,256]{3,2,1,0:T(8,128)(2,1)}, u32[]{:S(2)}) copy-start(bf16[2,4,128,256]{3,2,1,0:T(8,128)(2,1)} %get-tuple-element.36.refs_0_.refs_3_) | copy-start | bytes 1572868
  17.3 6.1 %copy-start.2 = (bf16[2,8,128,256]{3,2,1,0:T(8,128)(2,1)S(1)}, bf16[2,8,128,256]{3,2,1,0:T(8,128)(2,1)}, u32[]{:S(2)}) copy-start(bf16[2,8,128,256]{3,2,1,0:T(8,128)(2,1)} %forward_dft.2.refs_1_.refs_5_) | copy-start | bytes 3145732
  19.7 12.7 %copy-start.5 = (f32[2,128,256]{2,1,0:T(8,128)S(1)}, f32[2,128,256]{2,1,0:T(8,128)}, u32[]{:S(2)}) copy-start(f32[2,128,256]{2,1,0:T(8,128)} %constant.32.clone.twiddle_hbm.refs_9_.refs_7_) | copy-start | bytes 786436
  19.7 12.7 %copy-start.6 = (bf16[2,256,256]{2,1,0:T(8,128)(2,1)S(1)}, bf16[2,256,256]{2,1,0:T(8,128)(2,1)}, u32[]{:S(2)}) copy-start(bf16[2,256,256]{2,1,0:T(8,128)(2,1)} %constant.33.clone.refs_7_.refs_5_) | copy-start | bytes 786436
  19.7 12.7 %copy-start.7 = (bf16[256,256]{1,0:T(8,128)(2,1)S(1)}, bf16[256,256]{1,0:T(8,128)(2,1)}, u32[]{:S(2)}) copy-start(bf16[256,256]{1,0:T(8,128)(2,1)} %constant.34.clone.refs_8_.refs_6_) | copy-start | bytes 393220
  19.7 10.6 %collective-permute-start.3 = (bf16[2,4,128,256]{3,2,1,0:T(8,128)(2,1)S(1)}, bf16[2,4,128,256]{3,2,1,0:T(8,128)(2,1)S(1)}, u32[]{:S(2)}, u32[]{:S(2)}) collective-permute-start(bf16[2,4,128,256]{3,2,1,0:T(8,128)(2,1)S(1)} %mix_rows.1), channel_id=1, source_target_pairs={{1,2},{5,6},{9,10},{13,14},{2,1},{6,5},{10,9},{14,13},{17,18},{21,... | collective-permute-start | bytes 1572872 | tf_op jit(solution)/shard_map/ppermute | solution.py:563
  23.4 9.0 %collective-permute-start.5 = (bf16[2,4,128,256]{3,2,1,0:T(8,128)(2,1)S(1)}, bf16[2,4,128,256]{3,2,1,0:T(8,128)(2,1)S(1)}, u32[]{:S(2)}, u32[]{:S(2)}) collective-permute-start(bf16[2,4,128,256]{3,2,1,0:T(8,128)(2,1)S(1)} %copy-done.4), channel_id=1, source_target_pairs={{0,1},{2,3},{4,5},{6,7},{8,9},{10,11},{12,13},{14,15},{1,0},{3,2},... | collective-permute-start | bytes 1572872 | tf_op jit(solution)/shard_map/ppermute | solution.py:551
  26.8 16.1 %collective-permute-start.2 = (bf16[2,4,128,256]{3,2,1,0:T(8,128)(2,1)S(1)}, bf16[2,4,128,256]{3,2,1,0:T(8,128)(2,1)S(1)}, u32[]{:S(2)}, u32[]{:S(2)}) collective-permute-start(bf16[2,4,128,256]{3,2,1,0:T(8,128)(2,1)S(1)} %copy-done.4), channel_id=1, source_target_pairs={{1,2},{3,4},{5,6},{7,8},{9,10},{11,12},{13,14},{2,1},{4,3},{6,5},{... | collective-permute-start | bytes 1572872 | tf_op jit(solution)/shard_map/ppermute | solution.py:566
  30.3 12.6 %collective-permute-start.4 = (bf16[2,4,128,256]{3,2,1,0:T(8,128)(2,1)S(1)}, bf16[2,4,128,256]{3,2,1,0:T(8,128)(2,1)S(1)}, u32[]{:S(2)}, u32[]{:S(2)}) collective-permute-start(bf16[2,4,128,256]{3,2,1,0:T(8,128)(2,1)S(1)} %collective-permute-done.3.refs_1_), channel_id=1, source_target_pairs={{6,3},{10,7},{14,11},{1,4},{5,8},{9,12},{22,19},{26,23},{30,27},{1... | collective-permute-start | bytes 1572872 | tf_op jit(solution)/shard_map/ppermute | solution.py:567

commit v4 on v3

--- a/solution.py
+++ b/solution.py
@@ -68,13 +68,15 @@
 
 
 def forward_kernel(
-    echo_hbm, outer_hbm, inner_hbm, twiddle_hbm, response_hbm, *refs, block
+    echo_hbm, outer_hbm, inner_hbm, twiddle_hbm, response_hbm, *refs, block, copied
 ):
     (
         *targets, echo, outer_table, inner_table, twiddle, response, response_rows,
-        signal_high, signal_low, rotated_high, rotated_low, out, semaphores,
-    ) = refs
-    rows = out.shape[1]
+        signal_high, signal_low, rotated_high, rotated_low, semaphores,
+    ) = refs[: len(refs) - copied]
+    length = targets[0].shape[1]
+    outs = [refs[-1]] if copied else targets
+    rows = SUBLANES
     pulse_count = echo.shape[2]
     outer = pulse_count // INNER
     half = INNER // 2
@@ -163,22 +165,21 @@
             for index in range(PER):
                 real = spectrum[index * outer : (index + 1) * outer, :half]
                 imag = spectrum[index * outer : (index + 1) * outer, half:]
-                out[0, row + index, :, lanes] = (
+                out, slot = outs[(row + index) // length], (row + index) % length
+                out[0, slot, :, lanes] = (
                     real * response_real + imag * response_imag
                 ).astype(jnp.bfloat16)
-                out[1, row + index, :, lanes] = (
+                out[1, slot, :, lanes] = (
                     imag * response_real - real * response_imag
                 ).astype(jnp.bfloat16)
-        place = pl.ds(row, PER)
-        length = targets[0].shape[1]
-        leaving.append(
-            pltpu.make_async_copy(
-                out.at[:, place],
-                targets[row // length].at[:, pl.ds(row % length, PER)],
-                semaphores.at[4 + row // PER],
+        if copied:
+            place = pl.ds(row, PER)
+            leaving.append(
+                pltpu.make_async_copy(
+                    outs[0].at[:, place], targets[0].at[:, place], semaphores.at[4 + row // PER]
+                )
             )
-        )
-        leaving[-1].start()
+            leaving[-1].start()
 
     leaving = []
     for row in range(rows):
@@ -192,20 +193,20 @@
         copy.wait()
 
 
-def forward(echoes, doppler_filter, table, block, pieces):
+def forward(echoes, doppler_filter, table, block, pieces, copied, limit):
     pulse_count = echoes.shape[2]
     rows = SUBLANES
     outer = pulse_count // INNER
     operands = [table["forward_outer"], table["forward_inner"], table["twiddle"], doppler_filter]
     anywhere = pl.BlockSpec(memory_space=pl.ANY)
     return pl.pallas_call(
-        functools.partial(forward_kernel, block=block),
+        functools.partial(forward_kernel, block=block, copied=copied),
         out_shape=[
             jax.ShapeDtypeStruct((2, rows // pieces, outer, INNER), jnp.bfloat16)
             for _ in range(pieces)
         ],
         in_specs=[anywhere] * 5,
-        out_specs=[anywhere] * pieces,
+        out_specs=[anywhere if copied else pl.BlockSpec(memory_space=pltpu.VMEM)] * pieces,
         scratch_shapes=[
             pltpu.VMEM((2, rows, pulse_count), jnp.float32),
             *[pltpu.VMEM(array.shape, array.dtype) for array in operands],
@@ -214,16 +215,16 @@
             pltpu.VMEM((rows, 2 * outer, INNER), jnp.bfloat16),
             pltpu.VMEM((rows * outer, 2 * INNER), jnp.bfloat16),
             pltpu.VMEM((rows * outer, 2 * INNER), jnp.bfloat16),
-            pltpu.VMEM((2, rows, outer, INNER), jnp.bfloat16),
             pltpu.SemaphoreType.DMA((12,)),
-        ],
-        compiler_params=pltpu.CompilerParams(vmem_limit_bytes=VMEM_ALL),
+        ]
+        + [pltpu.VMEM((2, rows, outer, INNER), jnp.bfloat16)] * copied,
+        compiler_params=pltpu.CompilerParams(vmem_limit_bytes=limit),
         cost_estimate=pl.CostEstimate(flops=10**12, bytes_accessed=10**9, transcendentals=0),
         name="forward_dft",
     )(echoes, *operands)
 
 
-def weights_kernel(shift, kernel, taps, weights, ordered):
+def weights_kernel(shift, kernel, taps, weights):
     offsets, outer = weights.shape[0], weights.shape[1]
     half = INNER // 2
     tap_count = taps.shape[0]
@@ -232,7 +233,6 @@
         lanes = pl.ds(parity * half, half)
         shifts = shift[pl.ds(parity, half, stride=2), :].T
         kernels = kernel[pl.ds(parity, half, stride=2), :].T
-        ordered[:, lanes] = shifts.astype(jnp.float32).astype(jnp.bfloat16)
         for start in range(0, outer, SUBLANES):
             here = slice(start, start + SUBLANES)
             moved = [
@@ -260,33 +260,37 @@
     inside = pl.BlockSpec(memory_space=pltpu.VMEM)
     return pl.pallas_call(
         weights_kernel,
-        out_shape=[
-            jax.ShapeDtypeStruct((offsets, shift.shape[1], INNER), jnp.float32),
-            jax.ShapeDtypeStruct((shift.shape[1], INNER), jnp.bfloat16),
-        ],
+        out_shape=jax.ShapeDtypeStruct((offsets, shift.shape[1], INNER), jnp.float32),
         in_specs=[inside] * 3,
-        out_specs=[inside] * 2,
+        out_specs=inside,
         compiler_params=pltpu.CompilerParams(vmem_limit_bytes=VMEM_LIMIT),
         cost_estimate=pl.CostEstimate(flops=1000, bytes_accessed=1000, transcendentals=0),
         name="offset_weights",
     )(shift, kernel_index, taps)
 
 
-def mix_kernel(odd, own, near, ordered, mixed):
+def mix_kernel(odd, own, near, shift, mixed):
     kept = mixed.shape[1]
     skipped = SUBLANES - kept
+    half = INNER // 2
 
     def run(is_odd):
         left, right = (own, near) if is_odd else (near, own)
-        for row in range(kept):
-            for_next = ordered[...] >= jnp.bfloat16(SMAX - skipped - row)
-            for part in range(2):
-                mixed[part, row] = jnp.where(for_next, left[part, row], right[part, row])
+        for parity in range(2):
+            lanes = pl.ds(parity * half, half)
+            shifts = shift[pl.ds(parity, half, stride=2), :].T
+            shifts = shifts.astype(jnp.float32).astype(jnp.bfloat16)
+            for row in range(kept):
+                for_next = shifts >= jnp.bfloat16(SMAX - skipped - row)
+                for part in range(2):
+                    mixed[part, row, :, lanes] = jnp.where(
+                        for_next, left[part, row, :, lanes], right[part, row, :, lanes]
+                    )
 
     by_half(odd, True, run)
 
 
-def mix(odd, own, near, ordered):
+def mix(odd, own, near, shift):
     inside = pl.BlockSpec(memory_space=pltpu.VMEM)
     return pl.pallas_call(
         mix_kernel,
@@ -296,7 +300,7 @@
         compiler_params=pltpu.CompilerParams(vmem_limit_bytes=VMEM_LIMIT),
         cost_estimate=pl.CostEstimate(flops=1000, bytes_accessed=1000, transcendentals=0),
         name="mix_rows",
-    )(odd, own, near, ordered)
+    )(odd, own, near, shift)
 
 
 def migrate(inputs, weights, lower, rows, store):
@@ -382,17 +386,13 @@
         run(not lower_if_odd)
 
 
-def partial_kernel(odd, *refs, numbers, lower_if_odd, has_partial):
+def partial_kernel(odd, *refs, numbers, lower_if_odd):
     inputs = readers(numbers, refs)
-    count = sum(sum(pieces) for _, pieces in numbers)
-    earlier = refs[count] if has_partial else None
-    weights, out = refs[count + has_partial :]
+    weights, out = refs[-2:]
     half = INNER // 2
 
     def store(part, parity, row, place, total):
         lanes = pl.ds(parity * half, half)
-        if has_partial:
-            total = total + earlier[part, row, place, lanes]
         out[part, row, place, lanes] = total
 
     by_half(
@@ -400,14 +400,13 @@
     )
 
 
-def partial(odd, blocks, lower_if_odd, weights, earlier):
+def partial(odd, blocks, lower_if_odd, weights):
     shape = (2, SUBLANES) + weights.shape[1:]
-    operands = [odd, *arrays_of(blocks), *([] if earlier is None else [earlier]), weights]
+    operands = [odd, *arrays_of(blocks), weights]
     inside = pl.BlockSpec(memory_space=pltpu.VMEM)
     return pl.pallas_call(
         functools.partial(
-            partial_kernel, numbers=counts_of(blocks), lower_if_odd=lower_if_odd,
-            has_partial=int(earlier is not None),
+            partial_kernel, numbers=counts_of(blocks), lower_if_odd=lower_if_odd
         ),
         out_shape=jax.ShapeDtypeStruct(shape, jnp.float32),
         in_specs=[pl.BlockSpec(memory_space=pltpu.SMEM)] + [inside] * (len(operands) - 1),
@@ -418,21 +417,19 @@
     )(*operands)
 
 
-def image_kernel(odd, *refs, numbers, lower_if_odd, has_partial, aliased):
+def image_kernel(odd, *refs, numbers, lower_if_odd, other_numbers, aliased):
     inputs = readers(numbers, refs)
     count = sum(sum(pieces) for _, pieces in numbers)
-    earlier = refs[count] if has_partial else None
-    weights, inner_table, outer_table, twiddle = refs[count + has_partial :][:4]
-    out_hbm, migrated, images, out, semaphores = refs[count + has_partial + 4 + aliased :]
+    earlier, weights, inner_table, outer_table, twiddle = refs[count : count + 5]
+    out_hbm, *rest, migrated, images, out, semaphores = refs[count + 5 + aliased :]
     rows = out.shape[1]
     pulse_count = out.shape[2]
     outer = pulse_count // INNER
     half = INNER // 2
 
     def store(part, parity, row, place, total):
-        if has_partial:
-            before = earlier[part, row, place, pl.ds(parity * half, half)]
-            total = before if total is None else total + before
+        if not other_numbers:
+            total = total + earlier[part, row, place, pl.ds(parity * half, half)]
         migrated[row, place, pl.ds((2 * parity + part) * half, half)] = total.astype(jnp.bfloat16)
 
     by_half(odd, lower_if_odd, lambda lower: migrate(inputs, weights, lower, rows, store))
@@ -482,16 +479,28 @@
             )
         )
         leaving[-1].start()
+    if other_numbers:
+        others = {number: inputs[number] for number in other_numbers}
+
+        def store_rest(part, parity, row, place, total):
+            lanes = pl.ds(parity * half, half)
+            rest[0][part, row, place, lanes] = total + earlier[part, row, place, lanes]
+
+        by_half(
+            odd,
+            not lower_if_odd,
+            lambda lower: migrate(others, weights, lower, rows, store_rest),
+        )
     for copy in leaving:
         copy.wait()
 
 
-def image(odd, blocks, lower_if_odd, weights, table, shape, earlier, previous):
+def image(odd, blocks, lower_if_odd, weights, table, shape, earlier, others, previous):
     row_count, pulse_count = shape
     rows = SUBLANES
     outer = pulse_count // INNER
     operands = [
-        odd, *arrays_of(blocks), *([] if earlier is None else [earlier]), weights,
+        odd, *arrays_of(blocks), earlier, weights,
         table["inverse_inner"], table["inverse_outer"], table["twiddle"],
     ]
     specs = [pl.BlockSpec(memory_space=pltpu.SMEM)]
@@ -505,11 +514,12 @@
     return pl.pallas_call(
         functools.partial(
             image_kernel, numbers=counts_of(blocks), lower_if_odd=lower_if_odd,
-            has_partial=int(earlier is not None), aliased=len(aliases),
+            other_numbers=others, aliased=len(aliases),
         ),
-        out_shape=jax.ShapeDtypeStruct((2, row_count, pulse_count), jnp.float32),
+        out_shape=[jax.ShapeDtypeStruct((2, row_count, pulse_count), jnp.float32)]
+        + [jax.ShapeDtypeStruct(earlier.shape, earlier.dtype)] * bool(others),
         in_specs=specs,
-        out_specs=anywhere,
+        out_specs=[anywhere] + [pl.BlockSpec(memory_space=pltpu.VMEM)] * bool(others),
         input_output_aliases=aliases,
         scratch_shapes=[
             pltpu.VMEM((rows, outer, 2 * INNER), jnp.bfloat16),
@@ -543,38 +553,40 @@
     across = [(i + 1, i + 2) for i in starts] + [(i + 2, i + 1) for i in starts]
     onward = [(i + 2, i - 1) for i in starts[1:]] + [(i + 1, i + 4) for i in starts[:-1]]
 
-    (upper,) = forward(echoes, doppler_filter, table, 1, 1)
+    (upper,) = forward(echoes, doppler_filter, table, 1, 1, True, VMEM_ALL)
     left_upper = lax.ppermute(upper, "rng", ahead)
     echoes, upper = lax.optimization_barrier((echoes, upper))
-    few, many = forward(echoes, doppler_filter, table, 0, 2)
+    few, many = forward(echoes, doppler_filter, table, 0, 2, False, VMEM_LIMIT)
     near_many = lax.ppermute(many, "rng", swaps(0))
     near_few = lax.ppermute(few, "rng", swaps(0))
-    migration_shift, kernel_index, few, many = lax.optimization_barrier(
-        (migration_shift, kernel_index, few, many)
-    )
     shift = migration_shift.reshape(INNER, outer)
+    mixed = mix(odd, many, near_many, shift)
+    direct = lax.ppermute(mixed, "rng", across)
+    kernel_index, kernel_taps, mixed = lax.optimization_barrier(
+        (kernel_index, kernel_taps, mixed)
+    )
     index = kernel_index.reshape(INNER, outer)
     taps = jnp.pad(kernel_taps.T, ((0, 0), (0, LANES - kernel_taps.shape[0])))
-    weights, ordered = offset_weights(shift, index, taps)
-    lower = ((few,), (many,))
-    rest = partial(odd, {2: lower}, False, weights, None)
-    mixed = mix(odd, many, near_many, ordered)
-    mixed, rest = lax.optimization_barrier((mixed, rest))
-    direct = lax.ppermute(mixed, "rng", across)
-    rest = partial(odd, {1: ((left_upper,),), 3: ((upper,),)}, False, weights, rest)
-    few, rest = lax.optimization_barrier((few, rest))
+    weights = offset_weights(shift, index, taps)
+    rest = partial(odd, {2: ((few,), (many,))}, False, weights)
+    few, rest, left_upper = lax.optimization_barrier((few, rest, left_upper))
     far = lax.ppermute(few, "rng", swaps(1))
     relayed = lax.ppermute(direct, "rng", onward)
     few, direct = lax.optimization_barrier((few, direct))
-    lower = ((few,), (many,))
-    picture = image(
+    picture, rest = image(
         odd,
-        {0: ((near_few,), (near_many,)), 1: ((left_upper,),), 2: lower, 3: ((upper,),)},
-        True, weights, table, shape, None, None,
-    )
-    return image(
-        odd, {0: ((far,), (direct, relayed))}, False, weights, table, shape, rest, picture
-    )
+        {
+            0: ((near_few,), (near_many,)),
+            1: ((left_upper,),),
+            2: ((few,), (many,)),
+            3: ((upper,),),
+        },
+        True, weights, table, shape, rest, (1, 3), None,
+    )
+    (picture,) = image(
+        odd, {0: ((far,), (direct, relayed))}, False, weights, table, shape, rest, (), picture
+    )
+    return picture
 
 
 def solution(mesh):

time: 47 us -> 43.1 us (0.917)
  Pallas kernels: 28.5 us -> 23.6 us
  local copies, waits for them, and re-layouts: 2.82 us -> 1.03 us
  waiting for transfers between devices: 3.59 us -> 5.31 us
  starting transfers between devices: 11.5 us -> 12.7 us
    pallas_call x2 -> x1, Pallas kernels: 4.48 us -> 1.16 us  [partial(): pl.pallas_call(functools.partial(partial_kernel, numbers=counts_of(blocks...]
    ppermute x1, starting transfers between devices: 1.97 us -> 4.38 us  [per_device(): far = lax.ppermute(few, 'rng', swaps(1))]
    ppermute x1, waiting for transfers between devices: 0.01 us -> 1.89 us  [per_device(): near_many = lax.ppermute(many, 'rng', swaps(0))]
    unnamed x27 -> x22, local copies, waits for them, and re-layouts: 2.81 us -> 0.95 us
    ppermute x1, waiting for transfers between devices: 2.03 us -> 0.65 us  [per_device(): far = lax.ppermute(few, 'rng', swaps(1))]
    pallas_call x3, Pallas kernels: 10.7 us -> 9.36 us  [the longest x2 8.52 us: forward(): pl.pallas_call(functools.partial(forward_kernel, block=block, copied=copi...]
    ppermute x1, waiting for transfers between devices: 1.55 us -> 2.69 us  [per_device(): direct = lax.ppermute(mixed, 'rng', across)]
    pallas_call x1, Pallas kernels: 1.1 us -> 0.17 us  [mix(): pl.pallas_call(mix_kernel, out_shape=jax.ShapeDtypeStruct(own.shape, own....]
  transfers between devices with their start and end apart: 6 -> 6, of which waited for: 2 -> 4; matrix products, arithmetic and copies ran while one was open for 0% -> 0% of each run, Pallas kernels for 43% -> 35%
where the time goes in v4:
time: 43.1 us; the launch traced here: 42.9 us
  Pallas kernels  23.6 us (55%)
  starting transfers between devices  12.7 us (29%)
  waiting for transfers between devices  5.31 us (12%)
  local copies, waits for them, and re-layouts  1.03 us (2%)
    pallas_call x2, Pallas kernels, image(): pl.pallas_call(functools.partial(image_kernel, numbers=counts_of(blocks),...  12.9 us
    pallas_call x2, Pallas kernels, forward(): pl.pallas_call(functools.partial(forward_kernel, block=block, copied=copi...  8.52 us
    ppermute x1, starting transfers between devices, per_device(): far = lax.ppermute(few, 'rng', swaps(1))  4.38 us
    ppermute x1, starting transfers between devices, per_device(): left_upper = lax.ppermute(upper, 'rng', ahead)  3.71 us
    ppermute x1, starting transfers between devices, per_device(): direct = lax.ppermute(mixed, 'rng', across)  3.16 us
    ppermute x1, waiting for transfers between devices, per_device(): direct = lax.ppermute(mixed, 'rng', across)  2.69 us
    ppermute x1, waiting for transfers between devices, per_device(): near_many = lax.ppermute(many, 'rng', swaps(0))  1.89 us
    ppermute x1, starting transfers between devices, per_device(): relayed = lax.ppermute(direct, 'rng', onward)  1.31 us
  transfers between devices with their start and end apart: 6, of which 4 were waited for; matrix products, arithmetic and copies ran while one was open for 0% of the time, Pallas kernels for 35%

profile of v4, /device:TPU:17, one launch (start us, length us, event | category | flops | bytes accessed | tf_op | source)
XLA Modules:
  0.0 42.9 jit_solution(291957064989305368)
XLA Ops:
  0.0 0.0 copy-start
  0.0 0.0 copy-start.6
  0.0 0.0 copy-start.7
  0.0 0.0 copy-start.8
  0.0 0.0 copy-start.9
  0.0 5.1 %forward_dft.2.refs_5_ = bf16[2,8,128,256]{3,2,1,0:T(8,128)(2,1)} custom-call(f32[2,16,32768]{2,1,0:T(8,128)} %echo_hbm.2, bf16[2,256,256]{2,1,0:T(8,128)(2,1)} %constant.30.clone.outer_hbm, bf16[2,2,256,256]{3,2,1,0:T(8,128)(2,1)} %constant.31.clone.inner_hbm, f32[2,128,256]{2,1,0:T(8,128)} %constant.32.clone.twiddle_hbm.refs_10_.refs_7_, ...), custom_call_target="tpu_custom_call" | custom-call | flops 999999995904 | bytes 1000000000 | tf_op jit(solution)/shard_map/forward_dft/pallas_call | solution.py:202
  5.1 3.7 %collective-permute-start.1 = (bf16[2,8,128,256]{3,2,1,0:T(8,128)(2,1)}, bf16[2,8,128,256]{3,2,1,0:T(8,128)(2,1)}, u32[]{:S(2)}, u32[]{:S(2)}) collective-permute-start(bf16[2,8,128,256]{3,2,1,0:T(8,128)(2,1)} %forward_dft.2.refs_5_), channel_id=1, source_target_pairs={{0,1},{1,2},{2,3},{3,4},{4,5},{5,6},{6,7},{7,8},{8,9},{9,10},{10,1... | collective-permute-start | bytes 3145736 | tf_op jit(solution)/shard_map/ppermute | solution.py:557
  8.8 0.0 copy-done
  8.8 0.0 copy-done.6
  8.8 0.0 copy-done.7
  8.9 0.0 copy-done.8
  8.9 0.0 copy-done.9
  8.9 0.0 copy-start.4
  8.9 0.0 copy-start.10
  8.9 3.5 %forward_dft.3 = (bf16[2,4,128,256]{3,2,1,0:T(8,128)(2,1)S(1)}, bf16[2,4,128,256]{3,2,1,0:T(8,128)(2,1)S(1)}) custom-call(f32[2,16,32768]{2,1,0:T(8,128)S(1)} %copy-done.6, bf16[2,256,256]{2,1,0:T(8,128)(2,1)S(1)} %copy-done.9, bf16[2,2,256,256]{3,2,1,0:T(8,128)(2,1)S(1)} %copy-done.8, f32[2,128,256]{2,1,0:T(8,128)S(1)} %copy-done, f32[2,32768]{1,0:T(2,128)S(1)} %copy-done.7), custom_call_target="tpu_custom_call" | custom-call | flops 999999995904 | bytes 1000000000 | tf_op jit(solution)/shard_map/forward_dft/pallas_call | solution.py:202
  12.4 0.1 collective-permute-start
  12.5 1.9 %collective-permute-done.near.refs_1_ = bf16[2,4,128,256]{3,2,1,0:T(8,128)(2,1)S(1)} collective-permute-done((bf16[2,4,128,256]{3,2,1,0:T(8,128)(2,1)S(1)}, bf16[2,4,128,256]{3,2,1,0:T(8,128)(2,1)S(1)}, u32[]{:S(2)}, u32[]{:S(2)}) %collective-permute-start) | collective-permute-done | bytes 524320 | tf_op jit(solution)/shard_map/ppermute | solution.py:560
  14.3 0.0 copy-done.4
  14.3 0.2 mix_rows.1
  14.5 3.2 %collective-permute-start.3 = (bf16[2,4,128,256]{3,2,1,0:T(8,128)(2,1)S(1)}, bf16[2,4,128,256]{3,2,1,0:T(8,128)(2,1)S(1)}, u32[]{:S(2)}, u32[]{:S(2)}) collective-permute-start(bf16[2,4,128,256]{3,2,1,0:T(8,128)(2,1)S(1)} %mix_rows.1), channel_id=1, source_target_pairs={{1,2},{5,6},{9,10},{13,14},{2,1},{6,5},{10,9},{14,13},{17,18},{21,... | collective-permute-start | bytes 1572872 | tf_op jit(solution)/shard_map/ppermute | solution.py:564
  17.7 0.1 collective-permute-start.5
  17.8 0.0 copy-done.10
  17.8 0.1 copy.12
  17.9 0.0 copy-start.5
  17.9 0.9 %copy-done.5 = s32[32768]{0:T(1024)S(1)} copy-done((s32[32768]{0:T(1024)S(1)}, s32[32768]{0:T(1024)}, u32[]{:S(2)}) %copy-start.5) | copy-done | bytes 131096
  18.8 0.0 copy-start.1
  18.8 0.0 copy-start.2
  18.8 0.0 copy-start.3
  18.8 0.8 %offset_weights.1.refs_2_.refs_7_.refs_4_ = f32[25,128,256]{2,1,0:T(8,128)S(1)} custom-call(s32[256,128]{1,0:T(8,128)S(1)} %bitcast.5, s32[256,128]{1,0:T(8,128)S(1)} %bitcast.6, f32[16,128]{1,0:T(8,128)S(1)} %pad.4.taps), custom_call_target="tpu_custom_call" | custom-call | flops 1000 | bytes 1000 | tf_op jit(solution)/shard_map/offset_weights/pallas_call | solution.py:261
  19.6 1.2 %migrate_known_rows.1.refs_6_ = f32[2,8,128,256]{3,2,1,0:T(8,128)S(1)} custom-call(s32[1]{0:T(128)} %bitcast.odd, bf16[2,4,128,256]{3,2,1,0:T(8,128)(2,1)S(1)} %get-tuple-element.26.refs_0_.refs_3_, bf16[2,4,128,256]{3,2,1,0:T(8,128)(2,1)S(1)} %get-tuple-element.20.own.refs_1_.refs_4_, f32[25,128,256]{2,1,0:T(8,128)S(1)} %offset_weights.1.refs_2_.refs_7_.refs_4_), custom_call_target="tpu_custom_call" | custom-call | flops 1000 | bytes 1000 | tf_op jit(solution)/shard_map/migrate_known_rows/pallas_call | solution.py:407
  20.8 0.1 collective-permute-done.1.refs_2_
  20.9 4.4 %collective-permute-start.2 = (bf16[2,4,128,256]{3,2,1,0:T(8,128)(2,1)S(1)}, bf16[2,4,128,256]{3,2,1,0:T(8,128)(2,1)S(1)}, u32[]{:S(2)}, u32[]{:S(2)}) collective-permute-start(bf16[2,4,128,256]{3,2,1,0:T(8,128)(2,1)S(1)} %get-tuple-element.26.refs_0_.refs_3_), channel_id=1, source_target_pairs={{1,2},{3,4},{5,6},{7,8},{9,10},{11,12},{13,14},{2,1},{4,3},{6,5},{... | collective-permute-start | bytes 1572872 | tf_op jit(solution)/shard_map/ppermute | solution.py:573
  25.2 2.7 %collective-permute-done.3.refs_1_ = bf16[2,4,128,256]{3,2,1,0:T(8,128)(2,1)S(1)} collective-permute-done((bf16[2,4,128,256]{3,2,1,0:T(8,128)(2,1)S(1)}, bf16[2,4,128,256]{3,2,1,0:T(8,128)(2,1)S(1)}, u32[]{:S(2)}, u32[]{:S(2)}) %collective-permute-start.3) | collective-permute-done | bytes 524320 | tf_op jit(solution)/shard_map/ppermute | solution.py:564
  27.9 1.3 %collective-permute-start.4 = (bf16[2,4,128,256]{3,2,1,0:T(8,128)(2,1)S(1)}, bf16[2,4,128,256]{3,2,1,0:T(8,128)(2,1)S(1)}, u32[]{:S(2)}, u32[]{:S(2)}) collective-permute-start(bf16[2,4,128,256]{3,2,1,0:T(8,128)(2,1)S(1)} %collective-permute-done.3.refs_1_), channel_id=1, source_target_pairs={{6,3},{10,7},{14,11},{1,4},{5,8},{9,12},{22,19},{26,23},{30,27},{1... | collective-permute-start | bytes 1572872 | tf_op jit(solution)/shard_map/ppermute | solution.py:574
  29.3 0.0 collective-permute-done.5.refs_0_
  29.3 0.0 copy-done.1
  29.3 0.0 copy-done.2
  29.3 0.0 copy-done.3
  29.3 9.2 %migrate_and_image.2 = (f32[2,16,32768]{2,1,0:T(8,128)}, f32[2,8,128,256]{3,2,1,0:T(8,128)S(1)}) custom-call(s32[1]{0:T(128)} %bitcast.odd, bf16[2,4,128,256]{3,2,1,0:T(8,128)(2,1)S(1)} %collective-permute-done.5.refs_0_, bf16[2,4,128,256]{3,2,1,0:T(8,128)(2,1)S(1)} %collective-permute-done.near.refs_1_, ...), custom_call_target="tpu_custom_call" | custom-call | flops 1000 | bytes 1000 | tf_op jit(solution)/shard_map/migrate_and_image/pallas_call | solution.py:514
  38.5 0.7 %collective-permute-done.2.refs_0_ = bf16[2,4,128,256]{3,2,1,0:T(8,128)(2,1)S(1)} collective-permute-done((bf16[2,4,128,256]{3,2,1,0:T(8,128)(2,1)S(1)}, bf16[2,4,128,256]{3,2,1,0:T(8,128)(2,1)S(1)}, u32[]{:S(2)}, u32[]{:S(2)}) %collective-permute-start.2) | collective-permute-done | bytes 524320 | tf_op jit(solution)/shard_map/ppermute | solution.py:573
  39.2 0.0 collective-permute-done.4.refs_2_
  39.2 3.7 %migrate_and_image.3 = f32[2,16,32768]{2,1,0:T(8,128)} custom-call(s32[1]{0:T(128)} %bitcast.odd, bf16[2,4,128,256]{3,2,1,0:T(8,128)(2,1)S(1)} %collective-permute-done.2.refs_0_, bf16[2,4,128,256]{3,2,1,0:T(8,128)(2,1)S(1)} %collective-permute-done.3.refs_1_, ...), custom_call_target="tpu_custom_call", output_to_operand_aliasing={{}: (9, {})} | custom-call | flops 1000 | bytes 1000 | tf_op jit(solution)/shard_map/migrate_and_image/pallas_call | solution.py:514
  (1 shorter events, 0.0 us)
Async XLA Ops:
  0.0 8.8 %copy-start = (f32[2,128,256]{2,1,0:T(8,128)S(1)}, f32[2,128,256]{2,1,0:T(8,128)}, u32[]{:S(2)}) copy-start(f32[2,128,256]{2,1,0:T(8,128)} %constant.32.clone.twiddle_hbm.refs_10_.refs_7_) | copy-start | bytes 786436
  0.0 8.8 %copy-start.6 = (f32[2,16,32768]{2,1,0:T(8,128)S(1)}, f32[2,16,32768]{2,1,0:T(8,128)}, u32[]{:S(2)}) copy-start(f32[2,16,32768]{2,1,0:T(8,128)} %echo_hbm.2) | copy-start | bytes 12582916
  0.0 8.8 %copy-start.7 = (f32[2,32768]{1,0:T(2,128)S(1)}, f32[2,32768]{1,0:T(2,128)}, u32[]{:S(2)}) copy-start(f32[2,32768]{1,0:T(2,128)} %response_hbm.3) | copy-start | bytes 786436
  0.0 8.8 %copy-start.8 = (bf16[2,2,256,256]{3,2,1,0:T(8,128)(2,1)S(1)}, bf16[2,2,256,256]{3,2,1,0:T(8,128)(2,1)}, u32[]{:S(2)}) copy-start(bf16[2,2,256,256]{3,2,1,0:T(8,128)(2,1)} %constant.31.clone.inner_hbm) | copy-start | bytes 1572868
  0.0 8.8 %copy-start.9 = (bf16[2,256,256]{2,1,0:T(8,128)(2,1)S(1)}, bf16[2,256,256]{2,1,0:T(8,128)(2,1)}, u32[]{:S(2)}) copy-start(bf16[2,256,256]{2,1,0:T(8,128)(2,1)} %constant.30.clone.outer_hbm) | copy-start | bytes 786436
  5.1 15.8 %collective-permute-start.1 = (bf16[2,8,128,256]{3,2,1,0:T(8,128)(2,1)}, bf16[2,8,128,256]{3,2,1,0:T(8,128)(2,1)}, u32[]{:S(2)}, u32[]{:S(2)}) collective-permute-start(bf16[2,8,128,256]{3,2,1,0:T(8,128)(2,1)} %forward_dft.2.refs_5_), channel_id=1, source_target_pairs={{0,1},{1,2},{2,3},{3,4},{4,5},{5,6},{6,7},{7,8},{8,9},{9,10},{10,1... | collective-permute-start | bytes 3145736 | tf_op jit(solution)/shard_map/ppermute | solution.py:557
  8.9 5.5 %copy-start.4 = (s32[32768]{0:T(1024)S(1)}, s32[32768]{0:T(1024)}, u32[]{:S(2)}) copy-start(s32[32768]{0:T(1024)} %param.12) | copy-start | bytes 393220
  8.9 8.9 %copy-start.10 = (f32[16,16]{1,0:T(8,128)S(1)}, f32[16,16]{1,0:T(8,128)}, u32[]{:S(2)}) copy-start(f32[16,16]{1,0:T(8,128)} %param.14) | copy-start | bytes 3076
  12.4 2.0 %collective-permute-start = (bf16[2,4,128,256]{3,2,1,0:T(8,128)(2,1)S(1)}, bf16[2,4,128,256]{3,2,1,0:T(8,128)(2,1)S(1)}, u32[]{:S(2)}, u32[]{:S(2)}) collective-permute-start(bf16[2,4,128,256]{3,2,1,0:T(8,128)(2,1)S(1)} %get-tuple-element.20.own.refs_1_.refs_4_), channel_id=1, source_target_pairs={{0,1},{2,3},{4,5},{6,7},{8,9},{10,11},{12,13},{14,15},{1,0},{3,2},... | collective-permute-start | bytes 1572872 | tf_op jit(solution)/shard_map/ppermute | solution.py:560
  14.5 13.4 %collective-permute-start.3 = (bf16[2,4,128,256]{3,2,1,0:T(8,128)(2,1)S(1)}, bf16[2,4,128,256]{3,2,1,0:T(8,128)(2,1)S(1)}, u32[]{:S(2)}, u32[]{:S(2)}) collective-permute-start(bf16[2,4,128,256]{3,2,1,0:T(8,128)(2,1)S(1)} %mix_rows.1), channel_id=1, source_target_pairs={{1,2},{5,6},{9,10},{13,14},{2,1},{6,5},{10,9},{14,13},{17,18},{21,... | collective-permute-start | bytes 1572872 | tf_op jit(solution)/shard_map/ppermute | solution.py:564
  17.7 11.6 %collective-permute-start.5 = (bf16[2,4,128,256]{3,2,1,0:T(8,128)(2,1)S(1)}, bf16[2,4,128,256]{3,2,1,0:T(8,128)(2,1)S(1)}, u32[]{:S(2)}, u32[]{:S(2)}) collective-permute-start(bf16[2,4,128,256]{3,2,1,0:T(8,128)(2,1)S(1)} %get-tuple-element.26.refs_0_.refs_3_), channel_id=1, source_target_pairs={{0,1},{2,3},{4,5},{6,7},{8,9},{10,11},{12,13},{14,15},{1,0},{3,2},... | collective-permute-start | bytes 1572872 | tf_op jit(solution)/shard_map/ppermute | solution.py:561
  17.9 0.9 %copy-start.5 = (s32[32768]{0:T(1024)S(1)}, s32[32768]{0:T(1024)}, u32[]{:S(2)}) copy-start(s32[32768]{0:T(1024)} %param.13) | copy-start | bytes 393220
  18.8 10.5 %copy-start.1 = (bf16[2,256,256]{2,1,0:T(8,128)(2,1)S(1)}, bf16[2,256,256]{2,1,0:T(8,128)(2,1)}, u32[]{:S(2)}) copy-start(bf16[2,256,256]{2,1,0:T(8,128)(2,1)} %constant.33.clone.refs_8_.refs_5_) | copy-start | bytes 786436
  18.8 10.5 %copy-start.2 = (bf16[2,8,128,256]{3,2,1,0:T(8,128)(2,1)S(1)}, bf16[2,8,128,256]{3,2,1,0:T(8,128)(2,1)}, u32[]{:S(2)}) copy-start(bf16[2,8,128,256]{3,2,1,0:T(8,128)(2,1)} %forward_dft.2.refs_5_) | copy-start | bytes 3145732
  18.8 10.5 %copy-start.3 = (bf16[256,256]{1,0:T(8,128)(2,1)S(1)}, bf16[256,256]{1,0:T(8,128)(2,1)}, u32[]{:S(2)}) copy-start(bf16[256,256]{1,0:T(8,128)(2,1)} %constant.34.clone.refs_9_.refs_6_) | copy-start | bytes 393220
  20.9 18.3 %collective-permute-start.2 = (bf16[2,4,128,256]{3,2,1,0:T(8,128)(2,1)S(1)}, bf16[2,4,128,256]{3,2,1,0:T(8,128)(2,1)S(1)}, u32[]{:S(2)}, u32[]{:S(2)}) collective-permute-start(bf16[2,4,128,256]{3,2,1,0:T(8,128)(2,1)S(1)} %get-tuple-element.26.refs_0_.refs_3_), channel_id=1, source_target_pairs={{1,2},{3,4},{5,6},{7,8},{9,10},{11,12},{13,14},{2,1},{4,3},{6,5},{... | collective-permute-start | bytes 1572872 | tf_op jit(solution)/shard_map/ppermute | solution.py:573
  27.9 11.2 %collective-permute-start.4 = (bf16[2,4,128,256]{3,2,1,0:T(8,128)(2,1)S(1)}, bf16[2,4,128,256]{3,2,1,0:T(8,128)(2,1)S(1)}, u32[]{:S(2)}, u32[]{:S(2)}) collective-permute-start(bf16[2,4,128,256]{3,2,1,0:T(8,128)(2,1)S(1)} %collective-permute-done.3.refs_1_), channel_id=1, source_target_pairs={{6,3},{10,7},{14,11},{1,4},{5,8},{9,12},{22,19},{26,23},{30,27},{1... | collective-permute-start | bytes 1572872 | tf_op jit(solution)/shard_map/ppermute | solution.py:574

commit v5 on v4

--- a/solution.py
+++ b/solution.py
@@ -15,6 +15,9 @@
 SMAX = 9
 PER = 2
 ROW_GROUP = 8
+MERGED = 4
+CHUNKS = 2
+PIECES = 2
 VMEM_LIMIT = 24 * 1024 * 1024
 VMEM_ALL = 56 * 1024 * 1024
 
@@ -52,7 +55,13 @@
         forward_inner.append(np.stack(np_split(np.block([[ic, -isn], [isn, ic]]))))
         inverse_inner.append(np.block([[ic.T, isn.T], [-isn.T, ic.T]]).astype(jnp.bfloat16))
     forward_outer = np.block([[oc, osn], [-osn, oc]])
-    inverse_outer = np.block([[oc, -osn], [osn, oc]])
+    length = outer // CHUNKS
+    inverse_outer = np.concatenate(
+        [
+            np.block([[oc[here], -osn[here]], [osn[here], oc[here]]])
+            for here in (slice(start, start + length) for start in range(0, outer, length))
+        ]
+    )
     twist = (
         np.arange(outer, dtype=np.int64)[:, None] * np.arange(INNER, dtype=np.int64)[None, :]
     ) * (2.0 * math.pi / pulse_count)
@@ -74,8 +83,8 @@
         *targets, echo, outer_table, inner_table, twiddle, response, response_rows,
         signal_high, signal_low, rotated_high, rotated_low, semaphores,
     ) = refs[: len(refs) - copied]
-    length = targets[0].shape[1]
     outs = [refs[-1]] if copied else targets
+    slots = [(ref, slot) for ref in outs for slot in range(ref.shape[1])]
     rows = SUBLANES
     pulse_count = echo.shape[2]
     outer = pulse_count // INNER
@@ -165,7 +174,7 @@
             for index in range(PER):
                 real = spectrum[index * outer : (index + 1) * outer, :half]
                 imag = spectrum[index * outer : (index + 1) * outer, half:]
-                out, slot = outs[(row + index) // length], (row + index) % length
+                out, slot = slots[row + index]
                 out[0, slot, :, lanes] = (
                     real * response_real + imag * response_imag
                 ).astype(jnp.bfloat16)
@@ -193,7 +202,7 @@
         copy.wait()
 
 
-def forward(echoes, doppler_filter, table, block, pieces, copied, limit):
+def forward(echoes, doppler_filter, table, block, lengths, copied, limit):
     pulse_count = echoes.shape[2]
     rows = SUBLANES
     outer = pulse_count // INNER
@@ -202,11 +211,10 @@
     return pl.pallas_call(
         functools.partial(forward_kernel, block=block, copied=copied),
         out_shape=[
-            jax.ShapeDtypeStruct((2, rows // pieces, outer, INNER), jnp.bfloat16)
-            for _ in range(pieces)
+            jax.ShapeDtypeStruct((2, length, outer, INNER), jnp.bfloat16) for length in lengths
         ],
         in_specs=[anywhere] * 5,
-        out_specs=[anywhere if copied else pl.BlockSpec(memory_space=pltpu.VMEM)] * pieces,
+        out_specs=[anywhere if copied else pl.BlockSpec(memory_space=pltpu.VMEM)] * len(lengths),
         scratch_shapes=[
             pltpu.VMEM((2, rows, pulse_count), jnp.float32),
             *[pltpu.VMEM(array.shape, array.dtype) for array in operands],
@@ -347,10 +355,11 @@
 
 
 def reader(pieces):
-    length = pieces[0][0].shape[1]
+    slots = [(piece, slot) for piece in pieces for slot in range(piece[0].shape[1])]
 
     def read(part, index, sub, lanes):
-        values = [ref[part, index % length, sub, lanes] for ref in pieces[index // length]]
+        piece, slot = slots[index]
+        values = [ref[part, slot, sub, lanes] for ref in piece]
         return sum(values[1:], values[0])
 
     return read
@@ -421,7 +430,7 @@
     inputs = readers(numbers, refs)
     count = sum(sum(pieces) for _, pieces in numbers)
     earlier, weights, inner_table, outer_table, twiddle = refs[count : count + 5]
-    out_hbm, *rest, migrated, images, out, semaphores = refs[count + 5 + aliased :]
+    out_hbm, *rest, migrated, sections, images, out, semaphores = refs[count + 5 + aliased :]
     rows = out.shape[1]
     pulse_count = out.shape[2]
     outer = pulse_count // INNER
@@ -450,35 +459,44 @@
                 real, imag = value[here, :half], value[here, half:]
                 turned[0].append(real * cosine[:, lanes] - imag * sine[:, lanes])
                 turned[1].append(real * sine[:, lanes] + imag * cosine[:, lanes])
-            turned = jnp.concatenate(
-                [jnp.concatenate(pair, axis=1).astype(jnp.bfloat16) for pair in turned], axis=0
-            )
-            images[start + index] = jnp.dot(
-                outer_table[...], turned, preferred_element_type=jnp.float32
-            )
-    chunks = 4
-    chunk = pulse_count // chunks
+            for part in range(2):
+                sections[start + index, pl.ds(part * outer, outer), :] = jnp.concatenate(
+                    turned[part], axis=1
+                ).astype(jnp.bfloat16)
     first_row = pl.multiple_of(jnp.where((odd[0] == 1) == lower_if_odd, 0, rows), rows)
     leaving = []
-    for index in range(chunks):
-        for part in range(2):
-            for first_place in range(
-                index * outer // chunks, (index + 1) * outer // chunks, SUBLANES
-            ):
-                swapped = jnp.swapaxes(
-                    images[:, pl.ds(part * outer + first_place, SUBLANES), :], 0, 1
+    length = outer // CHUNKS
+    for chunk in range(CHUNKS):
+        table = outer_table[pl.ds(2 * length * chunk, 2 * length), :]
+        for row in range(rows):
+            images[row, pl.ds(2 * length * chunk, 2 * length), :] = jnp.dot(
+                table, sections[row], preferred_element_type=jnp.float32
+            )
+        for piece in range(PIECES):
+            for part in range(2):
+                for first_place in range(
+                    piece * length // PIECES, (piece + 1) * length // PIECES, SUBLANES
+                ):
+                    swapped = jnp.swapaxes(
+                        images[
+                            :, pl.ds((2 * chunk + part) * length + first_place, SUBLANES), :
+                        ],
+                        0,
+                        1,
+                    )
+                    for offset in range(SUBLANES):
+                        lanes = pl.ds((chunk * length + first_place + offset) * INNER, INNER)
+                        out[part, :, lanes] = swapped[offset]
+            number = chunk * PIECES + piece
+            place = pl.ds(number * (pulse_count // (CHUNKS * PIECES)), pulse_count // (CHUNKS * PIECES))
+            leaving.append(
+                pltpu.make_async_copy(
+                    out.at[:, :, place],
+                    out_hbm.at[:, pl.ds(first_row, rows), place],
+                    semaphores.at[number],
                 )
-                for offset in range(SUBLANES):
-                    out[part, :, pl.ds((first_place + offset) * INNER, INNER)] = swapped[offset]
-        place = pl.ds(index * chunk, chunk)
-        leaving.append(
-            pltpu.make_async_copy(
-                out.at[:, :, place],
-                out_hbm.at[:, pl.ds(first_row, rows), place],
-                semaphores.at[index],
             )
-        )
-        leaving[-1].start()
+            leaving[-1].start()
     if other_numbers:
         others = {number: inputs[number] for number in other_numbers}
 
@@ -523,9 +541,10 @@
         input_output_aliases=aliases,
         scratch_shapes=[
             pltpu.VMEM((rows, outer, 2 * INNER), jnp.bfloat16),
+            pltpu.VMEM((rows, 2 * outer, INNER), jnp.bfloat16),
             pltpu.VMEM((rows, 2 * outer, INNER), jnp.float32),
             pltpu.VMEM((2, rows, pulse_count), jnp.float32),
-            pltpu.SemaphoreType.DMA((4,)),
+            pltpu.SemaphoreType.DMA((CHUNKS * PIECES,)),
         ],
         compiler_params=pltpu.CompilerParams(vmem_limit_bytes=VMEM_LIMIT),
         cost_estimate=pl.CostEstimate(flops=1000, bytes_accessed=1000, transcendentals=0),
@@ -553,10 +572,11 @@
     across = [(i + 1, i + 2) for i in starts] + [(i + 2, i + 1) for i in starts]
     onward = [(i + 2, i - 1) for i in starts[1:]] + [(i + 1, i + 4) for i in starts[:-1]]
 
-    (upper,) = forward(echoes, doppler_filter, table, 1, 1, True, VMEM_ALL)
+    (upper,) = forward(echoes, doppler_filter, table, 1, (SUBLANES,), True, VMEM_ALL)
     left_upper = lax.ppermute(upper, "rng", ahead)
     echoes, upper = lax.optimization_barrier((echoes, upper))
-    few, many = forward(echoes, doppler_filter, table, 0, 2, False, VMEM_LIMIT)
+    lengths = (SUBLANES - MERGED, MERGED)
+    few, many = forward(echoes, doppler_filter, table, 0, lengths, False, VMEM_LIMIT)
     near_many = lax.ppermute(many, "rng", swaps(0))
     near_few = lax.ppermute(few, "rng", swaps(0))
     shift = migration_shift.reshape(INNER, outer)
@@ -568,7 +588,7 @@
     index = kernel_index.reshape(INNER, outer)
     taps = jnp.pad(kernel_taps.T, ((0, 0), (0, LANES - kernel_taps.shape[0])))
     weights = offset_weights(shift, index, taps)
-    rest = partial(odd, {2: ((few,), (many,))}, False, weights)
+    rest = partial(odd, {2: ((few,), (many,)), 3: ((upper,),)}, False, weights)
     few, rest, left_upper = lax.optimization_barrier((few, rest, left_upper))
     far = lax.ppermute(few, "rng", swaps(1))
     relayed = lax.ppermute(direct, "rng", onward)
@@ -581,7 +601,7 @@
             2: ((few,), (many,)),
             3: ((upper,),),
         },
-        True, weights, table, shape, rest, (1, 3), None,
+        True, weights, table, shape, rest, (1,), None,
     )
     (picture,) = image(
         odd, {0: ((far,), (direct, relayed))}, False, weights, table, shape, rest, (), picture

time: 43.1 us -> 42.5 us (0.986)
  starting transfers between devices: 12.7 us -> 10.6 us
  waiting for transfers between devices: 5.31 us -> 6.66 us
    ppermute x1, starting transfers between devices: 4.38 us -> 2.29 us  [per_device(): far = lax.ppermute(few, 'rng', swaps(1))]
    pallas_call x2, Pallas kernels: 12.9 us -> 10.9 us  [image(): pl.pallas_call(functools.partial(image_kernel, numbers=counts_of(blocks),...]
    ppermute x1, waiting for transfers between devices: 0.65 us -> 2.08 us  [per_device(): far = lax.ppermute(few, 'rng', swaps(1))]
    pallas_call x1, Pallas kernels: 1.16 us -> 2.47 us  [partial(): pl.pallas_call(functools.partial(partial_kernel, numbers=counts_of(blocks...]
    pallas_call x1, Pallas kernels: 0.17 us -> 0.99 us  [mix(): pl.pallas_call(mix_kernel, out_shape=jax.ShapeDtypeStruct(own.shape, own....]
  transfers between devices with their start and end apart: 6 -> 6, of which waited for: 4 -> 3; matrix products, arithmetic and copies ran while one was open for 0% -> 0% of each run, Pallas kernels for 35% -> 37%
where the time goes in v5:
time: 42.5 us; the launch traced here: 42.3 us
  Pallas kernels  23.7 us (56%)
  starting transfers between devices  10.6 us (25%)
  waiting for transfers between devices  6.66 us (16%)
  local copies, waits for them, and re-layouts  1.04 us (2%)
    pallas_call x2, Pallas kernels, image(): pl.pallas_call(functools.partial(image_kernel, numbers=counts_of(blocks),...  10.9 us
    pallas_call x2, Pallas kernels, forward(): pl.pallas_call(functools.partial(forward_kernel, block=block, copied=copi...  8.52 us
    ppermute x1, starting transfers between devices, per_device(): left_upper = lax.ppermute(upper, 'rng', ahead)  3.71 us
    ppermute x1, starting transfers between devices, per_device(): direct = lax.ppermute(mixed, 'rng', across)  3.15 us
    ppermute x1, waiting for transfers between devices, per_device(): direct = lax.ppermute(mixed, 'rng', across)  2.69 us
    pallas_call x1, Pallas kernels, partial(): pl.pallas_call(functools.partial(partial_kernel, numbers=counts_of(blocks...  2.47 us
    ppermute x1, starting transfers between devices, per_device(): far = lax.ppermute(few, 'rng', swaps(1))  2.29 us
    ppermute x1, waiting for transfers between devices, per_device(): far = lax.ppermute(few, 'rng', swaps(1))  2.08 us
  transfers between devices with their start and end apart: 6, of which 3 were waited for; matrix products, arithmetic and copies ran while one was open for 0% of the time, Pallas kernels for 37%

profile of v5, /device:TPU:17, one launch (start us, length us, event | category | flops | bytes accessed | tf_op | source)
XLA Modules:
  0.0 42.3 jit_solution(8415347652714958282)
XLA Ops:
  0.0 0.0 copy-start.1
  0.0 0.0 copy-start.6
  0.0 0.0 copy-start.7
  0.0 0.0 copy-start.8
  0.0 0.0 copy-start.9
  0.0 5.1 %forward_dft.2.refs_2_.refs_5_ = bf16[2,8,128,256]{3,2,1,0:T(8,128)(2,1)} custom-call(f32[2,16,32768]{2,1,0:T(8,128)} %echo_hbm.2, bf16[2,256,256]{2,1,0:T(8,128)(2,1)} %constant.30.clone.outer_hbm, bf16[2,2,256,256]{3,2,1,0:T(8,128)(2,1)} %constant.31.clone.inner_hbm, f32[2,128,256]{2,1,0:T(8,128)} %constant.32.clone.twiddle_hbm.refs_10_.refs_7_, ...), custom_call_target="tpu_custom_call" | custom-call | flops 999999995904 | bytes 1000000000 | tf_op jit(solution)/shard_map/forward_dft/pallas_call | solution.py:211
  5.1 3.7 %collective-permute-start.1 = (bf16[2,8,128,256]{3,2,1,0:T(8,128)(2,1)}, bf16[2,8,128,256]{3,2,1,0:T(8,128)(2,1)}, u32[]{:S(2)}, u32[]{:S(2)}) collective-permute-start(bf16[2,8,128,256]{3,2,1,0:T(8,128)(2,1)} %forward_dft.2.refs_2_.refs_5_), channel_id=1, source_target_pairs={{0,1},{1,2},{2,3},{3,4},{4,5},{5,6},{6,7},{7,8},{8,9},{9,10},{10,1... | collective-permute-start | bytes 3145736 | tf_op jit(solution)/shard_map/ppermute | solution.py:576
  8.8 0.0 copy-done.1
  8.8 0.0 copy-done.6
  8.8 0.0 copy-done.7
  8.9 0.0 copy-done.8
  8.9 0.0 copy-done.9
  8.9 0.0 copy-start.4
  8.9 0.0 copy-start.10
  8.9 3.5 %forward_dft.3 = (bf16[2,4,128,256]{3,2,1,0:T(8,128)(2,1)S(1)}, bf16[2,4,128,256]{3,2,1,0:T(8,128)(2,1)S(1)}) custom-call(f32[2,16,32768]{2,1,0:T(8,128)S(1)} %copy-done.6, bf16[2,256,256]{2,1,0:T(8,128)(2,1)S(1)} %copy-done.9, bf16[2,2,256,256]{3,2,1,0:T(8,128)(2,1)S(1)} %copy-done.8, f32[2,128,256]{2,1,0:T(8,128)S(1)} %copy-done.1, f32[2,32768]{1,0:T(2,128)S(1)} %copy-done.7), custom_call_target="tpu_custom_call" | custom-call | flops 999999995904 | bytes 1000000000 | tf_op jit(solution)/shard_map/forward_dft/pallas_call | solution.py:211
  12.4 0.0 copy-start
  12.4 0.1 collective-permute-start
  12.5 1.9 %collective-permute-done.near.refs_1_ = bf16[2,4,128,256]{3,2,1,0:T(8,128)(2,1)S(1)} collective-permute-done((bf16[2,4,128,256]{3,2,1,0:T(8,128)(2,1)S(1)}, bf16[2,4,128,256]{3,2,1,0:T(8,128)(2,1)S(1)}, u32[]{:S(2)}, u32[]{:S(2)}) %collective-permute-start) | collective-permute-done | bytes 524320 | tf_op jit(solution)/shard_map/ppermute | solution.py:580
  14.4 0.0 copy-done.4
  14.4 1.0 %mix_rows.1 = bf16[2,4,128,256]{3,2,1,0:T(8,128)(2,1)} custom-call(s32[1]{0:T(128)} %bitcast.odd, bf16[2,4,128,256]{3,2,1,0:T(8,128)(2,1)S(1)} %get-tuple-element.20.own.refs_1_.refs_4_, bf16[2,4,128,256]{3,2,1,0:T(8,128)(2,1)S(1)} %collective-permute-done.near.refs_1_, s32[256,128]{1,0:T(8,128)S(1)} %bitcast.4), custom_call_target="tpu_custom_call" | custom-call | flops 1000 | bytes 1000 | tf_op jit(solution)/shard_map/mix_rows/pallas_call | solution.py:303
  15.3 3.1 %collective-permute-start.3 = (bf16[2,4,128,256]{3,2,1,0:T(8,128)(2,1)}, bf16[2,4,128,256]{3,2,1,0:T(8,128)(2,1)S(1)}, u32[]{:S(2)}, u32[]{:S(2)}) collective-permute-start(bf16[2,4,128,256]{3,2,1,0:T(8,128)(2,1)} %mix_rows.1), channel_id=1, source_target_pairs={{1,2},{5,6},{9,10},{13,14},{2,1},{6,5},{10,9},{14,13},{17,18},{21,... | collective-permute-start | bytes 1572872 | tf_op jit(solution)/shard_map/ppermute | solution.py:584
  18.5 0.1 collective-permute-start.5
  18.6 0.0 copy-done.10
  18.6 0.1 copy.12
  18.7 0.0 copy-start.5
  18.7 0.9 %copy-done.5 = s32[32768]{0:T(1024)S(1)} copy-done((s32[32768]{0:T(1024)S(1)}, s32[32768]{0:T(1024)}, u32[]{:S(2)}) %copy-start.5) | copy-done | bytes 131096
  19.6 0.8 %offset_weights.1.refs_3_.refs_7_.refs_4_ = f32[25,128,256]{2,1,0:T(8,128)S(1)} custom-call(s32[256,128]{1,0:T(8,128)S(1)} %bitcast.5, s32[256,128]{1,0:T(8,128)S(1)} %bitcast.6, f32[16,128]{1,0:T(8,128)S(1)} %pad.4.taps), custom_call_target="tpu_custom_call" | custom-call | flops 1000 | bytes 1000 | tf_op jit(solution)/shard_map/offset_weights/pallas_call | solution.py:269
  20.4 0.0 copy-done
  20.4 0.0 copy-start.2
  20.4 0.0 copy-start.3
  20.5 2.5 %migrate_known_rows.1.refs_6_ = f32[2,8,128,256]{3,2,1,0:T(8,128)S(1)} custom-call(s32[1]{0:T(128)} %bitcast.odd, bf16[2,4,128,256]{3,2,1,0:T(8,128)(2,1)S(1)} %get-tuple-element.27.refs_0_.refs_3_, bf16[2,4,128,256]{3,2,1,0:T(8,128)(2,1)S(1)} %get-tuple-element.20.own.refs_1_.refs_4_, bf16[2,8,128,256]{3,2,1,0:T(8,128)(2,1)S(1)} %copy-done, ...), custom_call_target="tpu_custom_call" | custom-call | flops 1000 | bytes 1000 | tf_op jit(solution)/shard_map/migrate_known_rows/pallas_call | solution.py:416
  22.9 0.0 collective-permute-done.1.refs_2_
  23.0 2.3 %collective-permute-start.2 = (bf16[2,4,128,256]{3,2,1,0:T(8,128)(2,1)S(1)}, bf16[2,4,128,256]{3,2,1,0:T(8,128)(2,1)S(1)}, u32[]{:S(2)}, u32[]{:S(2)}) collective-permute-start(bf16[2,4,128,256]{3,2,1,0:T(8,128)(2,1)S(1)} %get-tuple-element.27.refs_0_.refs_3_), channel_id=1, source_target_pairs={{1,2},{3,4},{5,6},{7,8},{9,10},{11,12},{13,14},{2,1},{4,3},{6,5},{... | collective-permute-start | bytes 1572872 | tf_op jit(solution)/shard_map/ppermute | solution.py:593
  25.2 2.7 %collective-permute-done.3.refs_1_ = bf16[2,4,128,256]{3,2,1,0:T(8,128)(2,1)S(1)} collective-permute-done((bf16[2,4,128,256]{3,2,1,0:T(8,128)(2,1)}, bf16[2,4,128,256]{3,2,1,0:T(8,128)(2,1)S(1)}, u32[]{:S(2)}, u32[]{:S(2)}) %collective-permute-start.3) | collective-permute-done | bytes 524320 | tf_op jit(solution)/shard_map/ppermute | solution.py:584
  27.9 1.3 %collective-permute-start.4 = (bf16[2,4,128,256]{3,2,1,0:T(8,128)(2,1)S(1)}, bf16[2,4,128,256]{3,2,1,0:T(8,128)(2,1)S(1)}, u32[]{:S(2)}, u32[]{:S(2)}) collective-permute-start(bf16[2,4,128,256]{3,2,1,0:T(8,128)(2,1)S(1)} %collective-permute-done.3.refs_1_), channel_id=1, source_target_pairs={{6,3},{10,7},{14,11},{1,4},{5,8},{9,12},{22,19},{26,23},{30,27},{1... | collective-permute-start | bytes 1572872 | tf_op jit(solution)/shard_map/ppermute | solution.py:594
  29.3 0.0 collective-permute-done.5.refs_0_
  29.3 0.0 copy-done.2
  29.3 0.0 copy-done.3
  29.3 7.8 %migrate_and_image.2 = (f32[2,16,32768]{2,1,0:T(8,128)}, f32[2,8,128,256]{3,2,1,0:T(8,128)S(1)}) custom-call(s32[1]{0:T(128)} %bitcast.odd, bf16[2,4,128,256]{3,2,1,0:T(8,128)(2,1)} %collective-permute-done.5.refs_0_, bf16[2,4,128,256]{3,2,1,0:T(8,128)(2,1)S(1)} %collective-permute-done.near.refs_1_, ...), custom_call_target="tpu_custom_call" | custom-call | flops 1000 | bytes 1000 | tf_op jit(solution)/shard_map/migrate_and_image/pallas_call | solution.py:532
  37.1 2.1 %collective-permute-done.2.refs_0_ = bf16[2,4,128,256]{3,2,1,0:T(8,128)(2,1)S(1)} collective-permute-done((bf16[2,4,128,256]{3,2,1,0:T(8,128)(2,1)S(1)}, bf16[2,4,128,256]{3,2,1,0:T(8,128)(2,1)S(1)}, u32[]{:S(2)}, u32[]{:S(2)}) %collective-permute-start.2) | collective-permute-done | bytes 524320 | tf_op jit(solution)/shard_map/ppermute | solution.py:593
  39.2 0.0 collective-permute-done.4.refs_2_
  39.2 3.1 %migrate_and_image.3 = f32[2,16,32768]{2,1,0:T(8,128)} custom-call(s32[1]{0:T(128)} %bitcast.odd, bf16[2,4,128,256]{3,2,1,0:T(8,128)(2,1)S(1)} %collective-permute-done.2.refs_0_, bf16[2,4,128,256]{3,2,1,0:T(8,128)(2,1)S(1)} %collective-permute-done.3.refs_1_, ...), custom_call_target="tpu_custom_call", output_to_operand_aliasing={{}: (9, {})} | custom-call | flops 1000 | bytes 1000 | tf_op jit(solution)/shard_map/migrate_and_image/pallas_call | solution.py:532
  (1 shorter events, 0.0 us)
Async XLA Ops:
  0.0 8.8 %copy-start.1 = (f32[2,128,256]{2,1,0:T(8,128)S(1)}, f32[2,128,256]{2,1,0:T(8,128)}, u32[]{:S(2)}) copy-start(f32[2,128,256]{2,1,0:T(8,128)} %constant.32.clone.twiddle_hbm.refs_10_.refs_7_) | copy-start | bytes 786436
  0.0 8.8 %copy-start.6 = (f32[2,16,32768]{2,1,0:T(8,128)S(1)}, f32[2,16,32768]{2,1,0:T(8,128)}, u32[]{:S(2)}) copy-start(f32[2,16,32768]{2,1,0:T(8,128)} %echo_hbm.2) | copy-start | bytes 12582916
  0.0 8.8 %copy-start.7 = (f32[2,32768]{1,0:T(2,128)S(1)}, f32[2,32768]{1,0:T(2,128)}, u32[]{:S(2)}) copy-start(f32[2,32768]{1,0:T(2,128)} %response_hbm.3) | copy-start | bytes 786436
  0.0 8.8 %copy-start.8 = (bf16[2,2,256,256]{3,2,1,0:T(8,128)(2,1)S(1)}, bf16[2,2,256,256]{3,2,1,0:T(8,128)(2,1)}, u32[]{:S(2)}) copy-start(bf16[2,2,256,256]{3,2,1,0:T(8,128)(2,1)} %constant.31.clone.inner_hbm) | copy-start | bytes 1572868
  0.0 8.8 %copy-start.9 = (bf16[2,256,256]{2,1,0:T(8,128)(2,1)S(1)}, bf16[2,256,256]{2,1,0:T(8,128)(2,1)}, u32[]{:S(2)}) copy-start(bf16[2,256,256]{2,1,0:T(8,128)(2,1)} %constant.30.clone.outer_hbm) | copy-start | bytes 786436
  5.1 17.8 %collective-permute-start.1 = (bf16[2,8,128,256]{3,2,1,0:T(8,128)(2,1)}, bf16[2,8,128,256]{3,2,1,0:T(8,128)(2,1)}, u32[]{:S(2)}, u32[]{:S(2)}) collective-permute-start(bf16[2,8,128,256]{3,2,1,0:T(8,128)(2,1)} %forward_dft.2.refs_2_.refs_5_), channel_id=1, source_target_pairs={{0,1},{1,2},{2,3},{3,4},{4,5},{5,6},{6,7},{7,8},{8,9},{9,10},{10,1... | collective-permute-start | bytes 3145736 | tf_op jit(solution)/shard_map/ppermute | solution.py:576
  8.9 5.5 %copy-start.4 = (s32[32768]{0:T(1024)S(1)}, s32[32768]{0:T(1024)}, u32[]{:S(2)}) copy-start(s32[32768]{0:T(1024)} %param.12) | copy-start | bytes 393220
  8.9 9.7 %copy-start.10 = (f32[16,16]{1,0:T(8,128)S(1)}, f32[16,16]{1,0:T(8,128)}, u32[]{:S(2)}) copy-start(f32[16,16]{1,0:T(8,128)} %param.14) | copy-start | bytes 3076
  12.4 8.1 %copy-start = (bf16[2,8,128,256]{3,2,1,0:T(8,128)(2,1)S(1)}, bf16[2,8,128,256]{3,2,1,0:T(8,128)(2,1)}, u32[]{:S(2)}) copy-start(bf16[2,8,128,256]{3,2,1,0:T(8,128)(2,1)} %forward_dft.2.refs_2_.refs_5_) | copy-start | bytes 3145732
  12.4 2.0 %collective-permute-start = (bf16[2,4,128,256]{3,2,1,0:T(8,128)(2,1)S(1)}, bf16[2,4,128,256]{3,2,1,0:T(8,128)(2,1)S(1)}, u32[]{:S(2)}, u32[]{:S(2)}) collective-permute-start(bf16[2,4,128,256]{3,2,1,0:T(8,128)(2,1)S(1)} %get-tuple-element.20.own.refs_1_.refs_4_), channel_id=1, source_target_pairs={{0,1},{2,3},{4,5},{6,7},{8,9},{10,11},{12,13},{14,15},{1,0},{3,2},... | collective-permute-start | bytes 1572872 | tf_op jit(solution)/shard_map/ppermute | solution.py:580
  15.3 12.6 %collective-permute-start.3 = (bf16[2,4,128,256]{3,2,1,0:T(8,128)(2,1)}, bf16[2,4,128,256]{3,2,1,0:T(8,128)(2,1)S(1)}, u32[]{:S(2)}, u32[]{:S(2)}) collective-permute-start(bf16[2,4,128,256]{3,2,1,0:T(8,128)(2,1)} %mix_rows.1), channel_id=1, source_target_pairs={{1,2},{5,6},{9,10},{13,14},{2,1},{6,5},{10,9},{14,13},{17,18},{21,... | collective-permute-start | bytes 1572872 | tf_op jit(solution)/shard_map/ppermute | solution.py:584
  18.5 10.8 %collective-permute-start.5 = (bf16[2,4,128,256]{3,2,1,0:T(8,128)(2,1)S(1)}, bf16[2,4,128,256]{3,2,1,0:T(8,128)(2,1)}, u32[]{:S(2)}, u32[]{:S(2)}) collective-permute-start(bf16[2,4,128,256]{3,2,1,0:T(8,128)(2,1)S(1)} %get-tuple-element.27.refs_0_.refs_3_), channel_id=1, source_target_pairs={{0,1},{2,3},{4,5},{6,7},{8,9},{10,11},{12,13},{14,15},{1,0},{3,2},... | collective-permute-start | bytes 1572872 | tf_op jit(solution)/shard_map/ppermute | solution.py:581
  18.7 0.9 %copy-start.5 = (s32[32768]{0:T(1024)S(1)}, s32[32768]{0:T(1024)}, u32[]{:S(2)}) copy-start(s32[32768]{0:T(1024)} %param.13) | copy-start | bytes 393220
  20.4 8.8 %copy-start.2 = (bf16[2,256,256]{2,1,0:T(8,128)(2,1)S(1)}, bf16[2,256,256]{2,1,0:T(8,128)(2,1)}, u32[]{:S(2)}) copy-start(bf16[2,256,256]{2,1,0:T(8,128)(2,1)} %constant.33.clone.refs_8_.refs_5_) | copy-start | bytes 786436
  20.4 8.8 %copy-start.3 = (bf16[256,256]{1,0:T(8,128)(2,1)S(1)}, bf16[256,256]{1,0:T(8,128)(2,1)}, u32[]{:S(2)}) copy-start(bf16[256,256]{1,0:T(8,128)(2,1)} %constant.34.clone.refs_9_.refs_6_) | copy-start | bytes 393220
  23.0 16.2 %collective-permute-start.2 = (bf16[2,4,128,256]{3,2,1,0:T(8,128)(2,1)S(1)}, bf16[2,4,128,256]{3,2,1,0:T(8,128)(2,1)S(1)}, u32[]{:S(2)}, u32[]{:S(2)}) collective-permute-start(bf16[2,4,128,256]{3,2,1,0:T(8,128)(2,1)S(1)} %get-tuple-element.27.refs_0_.refs_3_), channel_id=1, source_target_pairs={{1,2},{3,4},{5,6},{7,8},{9,10},{11,12},{13,14},{2,1},{4,3},{6,5},{... | collective-permute-start | bytes 1572872 | tf_op jit(solution)/shard_map/ppermute | solution.py:593
  27.9 11.2 %collective-permute-start.4 = (bf16[2,4,128,256]{3,2,1,0:T(8,128)(2,1)S(1)}, bf16[2,4,128,256]{3,2,1,0:T(8,128)(2,1)S(1)}, u32[]{:S(2)}, u32[]{:S(2)}) collective-permute-start(bf16[2,4,128,256]{3,2,1,0:T(8,128)(2,1)S(1)} %collective-permute-done.3.refs_1_), channel_id=1, source_target_pairs={{6,3},{10,7},{14,11},{1,4},{5,8},{9,12},{22,19},{26,23},{30,27},{1... | collective-permute-start | bytes 1572872 | tf_op jit(solution)/shard_map/ppermute | solution.py:594

commit v6 on v5

--- a/solution.py
+++ b/solution.py
@@ -111,15 +111,8 @@
                 semaphores.at[4 + index],
             )
         )
-    for index in [0, *range(4, 4 + chunks), 1, 2, 3]:
+    for index in [*range(4, 4 + chunks), 1, 2, 0, 3]:
         ready[index].start()
-    ready[0].wait()
-    for tile in range(INNER):
-        response_rows[pl.ds(tile * 2, 2), :] = response[:, pl.ds(tile * outer, outer)]
-    response_parts = [
-        [response_rows[pl.ds(2 * parity + part, half, stride=4), :].T for part in range(2)]
-        for parity in range(2)
-    ]
     for index in range(chunks):
         ready[4 + index].wait()
         for part in range(2):
@@ -134,6 +127,13 @@
                 place = pl.ds(part * outer + first, SUBLANES)
                 signal_high[:, place, :] = high
                 signal_low[:, place, :] = low
+    ready[0].wait()
+    for tile in range(INNER):
+        response_rows[pl.ds(tile * 2, 2), :] = response[:, pl.ds(tile * outer, outer)]
+    response_parts = [
+        [response_rows[pl.ds(2 * parity + part, half, stride=4), :].T for part in range(2)]
+        for parity in range(2)
+    ]
     ready[1].wait()
     ready[2].wait()
     outer_high, outer_low = outer_table[0], outer_table[1]

time: 42.5 us -> 42.7 us (level)
  no operation moved by 1% of the time
where the time goes in v6:
time: 42.7 us; the launch traced here: 42.4 us
  Pallas kernels  23.9 us (56%)
  starting transfers between devices  10.6 us (25%)
  waiting for transfers between devices  6.67 us (16%)
  local copies, waits for them, and re-layouts  1.04 us (2%)
    pallas_call x2, Pallas kernels, image(): pl.pallas_call(functools.partial(image_kernel, numbers=counts_of(blocks),...  10.9 us
    pallas_call x2, Pallas kernels, forward(): pl.pallas_call(functools.partial(forward_kernel, block=block, copied=copi...  8.7 us
    ppermute x1, starting transfers between devices, per_device(): left_upper = lax.ppermute(upper, 'rng', ahead)  3.71 us
    ppermute x1, starting transfers between devices, per_device(): direct = lax.ppermute(mixed, 'rng', across)  3.16 us
    ppermute x1, waiting for transfers between devices, per_device(): direct = lax.ppermute(mixed, 'rng', across)  2.69 us
    pallas_call x1, Pallas kernels, partial(): pl.pallas_call(functools.partial(partial_kernel, numbers=counts_of(blocks...  2.47 us
    ppermute x1, starting transfers between devices, per_device(): far = lax.ppermute(few, 'rng', swaps(1))  2.28 us
    ppermute x1, waiting for transfers between devices, per_device(): far = lax.ppermute(few, 'rng', swaps(1))  2.08 us
  transfers between devices with their start and end apart: 6, of which 3 were waited for; matrix products, arithmetic and copies ran while one was open for 0% of the time, Pallas kernels for 37%

profile of v6, /device:TPU:17, one launch (start us, length us, event | category | flops | bytes accessed | tf_op | source)
XLA Modules:
  0.0 42.4 jit_solution(16528914130326598157)
XLA Ops:
  0.0 0.0 copy-start.1
  0.0 0.0 copy-start.6
  0.0 0.0 copy-start.7
  0.0 0.0 copy-start.8
  0.0 0.0 copy-start.9
  0.0 5.2 %forward_dft.2.refs_2_.refs_5_ = bf16[2,8,128,256]{3,2,1,0:T(8,128)(2,1)} custom-call(f32[2,16,32768]{2,1,0:T(8,128)} %echo_hbm.2, bf16[2,256,256]{2,1,0:T(8,128)(2,1)} %constant.30.clone.outer_hbm, bf16[2,2,256,256]{3,2,1,0:T(8,128)(2,1)} %constant.31.clone.inner_hbm, f32[2,128,256]{2,1,0:T(8,128)} %constant.32.clone.twiddle_hbm.refs_10_.refs_7_, ...), custom_call_target="tpu_custom_call" | custom-call | flops 999999995904 | bytes 1000000000 | tf_op jit(solution)/shard_map/forward_dft/pallas_call | solution.py:211
  5.3 3.7 %collective-permute-start.1 = (bf16[2,8,128,256]{3,2,1,0:T(8,128)(2,1)}, bf16[2,8,128,256]{3,2,1,0:T(8,128)(2,1)}, u32[]{:S(2)}, u32[]{:S(2)}) collective-permute-start(bf16[2,8,128,256]{3,2,1,0:T(8,128)(2,1)} %forward_dft.2.refs_2_.refs_5_), channel_id=1, source_target_pairs={{0,1},{1,2},{2,3},{3,4},{4,5},{5,6},{6,7},{7,8},{8,9},{9,10},{10,1... | collective-permute-start | bytes 3145736 | tf_op jit(solution)/shard_map/ppermute | solution.py:576
  9.0 0.0 copy-done.1
  9.0 0.0 copy-done.6
  9.0 0.0 copy-done.7
  9.0 0.0 copy-done.8
  9.0 0.0 copy-done.9
  9.1 0.0 copy-start.4
  9.1 0.0 copy-start.10
  9.1 3.5 %forward_dft.3 = (bf16[2,4,128,256]{3,2,1,0:T(8,128)(2,1)S(1)}, bf16[2,4,128,256]{3,2,1,0:T(8,128)(2,1)S(1)}) custom-call(f32[2,16,32768]{2,1,0:T(8,128)S(1)} %copy-done.6, bf16[2,256,256]{2,1,0:T(8,128)(2,1)S(1)} %copy-done.9, bf16[2,2,256,256]{3,2,1,0:T(8,128)(2,1)S(1)} %copy-done.8, f32[2,128,256]{2,1,0:T(8,128)S(1)} %copy-done.1, f32[2,32768]{1,0:T(2,128)S(1)} %copy-done.7), custom_call_target="tpu_custom_call" | custom-call | flops 999999995904 | bytes 1000000000 | tf_op jit(solution)/shard_map/forward_dft/pallas_call | solution.py:211
  12.5 0.0 copy-start
  12.6 0.1 collective-permute-start
  12.6 1.9 %collective-permute-done.near.refs_1_ = bf16[2,4,128,256]{3,2,1,0:T(8,128)(2,1)S(1)} collective-permute-done((bf16[2,4,128,256]{3,2,1,0:T(8,128)(2,1)S(1)}, bf16[2,4,128,256]{3,2,1,0:T(8,128)(2,1)S(1)}, u32[]{:S(2)}, u32[]{:S(2)}) %collective-permute-start) | collective-permute-done | bytes 524320 | tf_op jit(solution)/shard_map/ppermute | solution.py:580
  14.5 0.0 copy-done.4
  14.5 1.0 %mix_rows.1 = bf16[2,4,128,256]{3,2,1,0:T(8,128)(2,1)} custom-call(s32[1]{0:T(128)} %bitcast.odd, bf16[2,4,128,256]{3,2,1,0:T(8,128)(2,1)S(1)} %get-tuple-element.20.own.refs_1_.refs_4_, bf16[2,4,128,256]{3,2,1,0:T(8,128)(2,1)S(1)} %collective-permute-done.near.refs_1_, s32[256,128]{1,0:T(8,128)S(1)} %bitcast.4), custom_call_target="tpu_custom_call" | custom-call | flops 1000 | bytes 1000 | tf_op jit(solution)/shard_map/mix_rows/pallas_call | solution.py:303
  15.5 3.2 %collective-permute-start.3 = (bf16[2,4,128,256]{3,2,1,0:T(8,128)(2,1)}, bf16[2,4,128,256]{3,2,1,0:T(8,128)(2,1)S(1)}, u32[]{:S(2)}, u32[]{:S(2)}) collective-permute-start(bf16[2,4,128,256]{3,2,1,0:T(8,128)(2,1)} %mix_rows.1), channel_id=1, source_target_pairs={{1,2},{5,6},{9,10},{13,14},{2,1},{6,5},{10,9},{14,13},{17,18},{21,... | collective-permute-start | bytes 1572872 | tf_op jit(solution)/shard_map/ppermute | solution.py:584
  18.7 0.1 collective-permute-start.5
  18.8 0.0 copy-done.10
  18.8 0.1 copy.12
  18.9 0.0 copy-start.5
  18.9 0.9 %copy-done.5 = s32[32768]{0:T(1024)S(1)} copy-done((s32[32768]{0:T(1024)S(1)}, s32[32768]{0:T(1024)}, u32[]{:S(2)}) %copy-start.5) | copy-done | bytes 131096
  19.8 0.8 %offset_weights.1.refs_3_.refs_7_.refs_4_ = f32[25,128,256]{2,1,0:T(8,128)S(1)} custom-call(s32[256,128]{1,0:T(8,128)S(1)} %bitcast.5, s32[256,128]{1,0:T(8,128)S(1)} %bitcast.6, f32[16,128]{1,0:T(8,128)S(1)} %pad.4.taps), custom_call_target="tpu_custom_call" | custom-call | flops 1000 | bytes 1000 | tf_op jit(solution)/shard_map/offset_weights/pallas_call | solution.py:269
  20.6 0.0 copy-done
  20.6 0.0 copy-start.2
  20.6 0.0 copy-start.3
  20.6 2.5 %migrate_known_rows.1.refs_6_ = f32[2,8,128,256]{3,2,1,0:T(8,128)S(1)} custom-call(s32[1]{0:T(128)} %bitcast.odd, bf16[2,4,128,256]{3,2,1,0:T(8,128)(2,1)S(1)} %get-tuple-element.27.refs_0_.refs_3_, bf16[2,4,128,256]{3,2,1,0:T(8,128)(2,1)S(1)} %get-tuple-element.20.own.refs_1_.refs_4_, bf16[2,8,128,256]{3,2,1,0:T(8,128)(2,1)S(1)} %copy-done, ...), custom_call_target="tpu_custom_call" | custom-call | flops 1000 | bytes 1000 | tf_op jit(solution)/shard_map/migrate_known_rows/pallas_call | solution.py:416
  23.1 0.0 collective-permute-done.1.refs_2_
  23.1 2.3 %collective-permute-start.2 = (bf16[2,4,128,256]{3,2,1,0:T(8,128)(2,1)S(1)}, bf16[2,4,128,256]{3,2,1,0:T(8,128)(2,1)S(1)}, u32[]{:S(2)}, u32[]{:S(2)}) collective-permute-start(bf16[2,4,128,256]{3,2,1,0:T(8,128)(2,1)S(1)} %get-tuple-element.27.refs_0_.refs_3_), channel_id=1, source_target_pairs={{1,2},{3,4},{5,6},{7,8},{9,10},{11,12},{13,14},{2,1},{4,3},{6,5},{... | collective-permute-start | bytes 1572872 | tf_op jit(solution)/shard_map/ppermute | solution.py:593
  25.4 2.7 %collective-permute-done.3.refs_1_ = bf16[2,4,128,256]{3,2,1,0:T(8,128)(2,1)S(1)} collective-permute-done((bf16[2,4,128,256]{3,2,1,0:T(8,128)(2,1)}, bf16[2,4,128,256]{3,2,1,0:T(8,128)(2,1)S(1)}, u32[]{:S(2)}, u32[]{:S(2)}) %collective-permute-start.3) | collective-permute-done | bytes 524320 | tf_op jit(solution)/shard_map/ppermute | solution.py:584
  28.1 1.3 %collective-permute-start.4 = (bf16[2,4,128,256]{3,2,1,0:T(8,128)(2,1)S(1)}, bf16[2,4,128,256]{3,2,1,0:T(8,128)(2,1)S(1)}, u32[]{:S(2)}, u32[]{:S(2)}) collective-permute-start(bf16[2,4,128,256]{3,2,1,0:T(8,128)(2,1)S(1)} %collective-permute-done.3.refs_1_), channel_id=1, source_target_pairs={{6,3},{10,7},{14,11},{1,4},{5,8},{9,12},{22,19},{26,23},{30,27},{1... | collective-permute-start | bytes 1572872 | tf_op jit(solution)/shard_map/ppermute | solution.py:594
  29.4 0.0 collective-permute-done.5.refs_0_
  29.4 0.0 copy-done.2
  29.5 0.0 copy-done.3
  29.5 7.8 %migrate_and_image.2 = (f32[2,16,32768]{2,1,0:T(8,128)}, f32[2,8,128,256]{3,2,1,0:T(8,128)S(1)}) custom-call(s32[1]{0:T(128)} %bitcast.odd, bf16[2,4,128,256]{3,2,1,0:T(8,128)(2,1)} %collective-permute-done.5.refs_0_, bf16[2,4,128,256]{3,2,1,0:T(8,128)(2,1)S(1)} %collective-permute-done.near.refs_1_, ...), custom_call_target="tpu_custom_call" | custom-call | flops 1000 | bytes 1000 | tf_op jit(solution)/shard_map/migrate_and_image/pallas_call | solution.py:532
  37.3 2.1 %collective-permute-done.2.refs_0_ = bf16[2,4,128,256]{3,2,1,0:T(8,128)(2,1)S(1)} collective-permute-done((bf16[2,4,128,256]{3,2,1,0:T(8,128)(2,1)S(1)}, bf16[2,4,128,256]{3,2,1,0:T(8,128)(2,1)S(1)}, u32[]{:S(2)}, u32[]{:S(2)}) %collective-permute-start.2) | collective-permute-done | bytes 524320 | tf_op jit(solution)/shard_map/ppermute | solution.py:593
  39.4 0.0 collective-permute-done.4.refs_2_
  39.4 3.1 %migrate_and_image.3 = f32[2,16,32768]{2,1,0:T(8,128)} custom-call(s32[1]{0:T(128)} %bitcast.odd, bf16[2,4,128,256]{3,2,1,0:T(8,128)(2,1)S(1)} %collective-permute-done.2.refs_0_, bf16[2,4,128,256]{3,2,1,0:T(8,128)(2,1)S(1)} %collective-permute-done.3.refs_1_, ...), custom_call_target="tpu_custom_call", output_to_operand_aliasing={{}: (9, {})} | custom-call | flops 1000 | bytes 1000 | tf_op jit(solution)/shard_map/migrate_and_image/pallas_call | solution.py:532
  (1 shorter events, 0.0 us)
Async XLA Ops:
  0.0 9.0 %copy-start.1 = (f32[2,128,256]{2,1,0:T(8,128)S(1)}, f32[2,128,256]{2,1,0:T(8,128)}, u32[]{:S(2)}) copy-start(f32[2,128,256]{2,1,0:T(8,128)} %constant.32.clone.twiddle_hbm.refs_10_.refs_7_) | copy-start | bytes 786436
  0.0 9.0 %copy-start.6 = (f32[2,16,32768]{2,1,0:T(8,128)S(1)}, f32[2,16,32768]{2,1,0:T(8,128)}, u32[]{:S(2)}) copy-start(f32[2,16,32768]{2,1,0:T(8,128)} %echo_hbm.2) | copy-start | bytes 12582916
  0.0 9.0 %copy-start.7 = (f32[2,32768]{1,0:T(2,128)S(1)}, f32[2,32768]{1,0:T(2,128)}, u32[]{:S(2)}) copy-start(f32[2,32768]{1,0:T(2,128)} %response_hbm.3) | copy-start | bytes 786436
  0.0 9.0 %copy-start.8 = (bf16[2,2,256,256]{3,2,1,0:T(8,128)(2,1)S(1)}, bf16[2,2,256,256]{3,2,1,0:T(8,128)(2,1)}, u32[]{:S(2)}) copy-start(bf16[2,2,256,256]{3,2,1,0:T(8,128)(2,1)} %constant.31.clone.inner_hbm) | copy-start | bytes 1572868
  0.0 9.0 %copy-start.9 = (bf16[2,256,256]{2,1,0:T(8,128)(2,1)S(1)}, bf16[2,256,256]{2,1,0:T(8,128)(2,1)}, u32[]{:S(2)}) copy-start(bf16[2,256,256]{2,1,0:T(8,128)(2,1)} %constant.30.clone.outer_hbm) | copy-start | bytes 786436
  5.3 17.8 %collective-permute-start.1 = (bf16[2,8,128,256]{3,2,1,0:T(8,128)(2,1)}, bf16[2,8,128,256]{3,2,1,0:T(8,128)(2,1)}, u32[]{:S(2)}, u32[]{:S(2)}) collective-permute-start(bf16[2,8,128,256]{3,2,1,0:T(8,128)(2,1)} %forward_dft.2.refs_2_.refs_5_), channel_id=1, source_target_pairs={{0,1},{1,2},{2,3},{3,4},{4,5},{5,6},{6,7},{7,8},{8,9},{9,10},{10,1... | collective-permute-start | bytes 3145736 | tf_op jit(solution)/shard_map/ppermute | solution.py:576
  9.1 5.5 %copy-start.4 = (s32[32768]{0:T(1024)S(1)}, s32[32768]{0:T(1024)}, u32[]{:S(2)}) copy-start(s32[32768]{0:T(1024)} %param.12) | copy-start | bytes 393220
  9.1 9.7 %copy-start.10 = (f32[16,16]{1,0:T(8,128)S(1)}, f32[16,16]{1,0:T(8,128)}, u32[]{:S(2)}) copy-start(f32[16,16]{1,0:T(8,128)} %param.14) | copy-start | bytes 3076
  12.5 8.1 %copy-start = (bf16[2,8,128,256]{3,2,1,0:T(8,128)(2,1)S(1)}, bf16[2,8,128,256]{3,2,1,0:T(8,128)(2,1)}, u32[]{:S(2)}) copy-start(bf16[2,8,128,256]{3,2,1,0:T(8,128)(2,1)} %forward_dft.2.refs_2_.refs_5_) | copy-start | bytes 3145732
  12.6 2.0 %collective-permute-start = (bf16[2,4,128,256]{3,2,1,0:T(8,128)(2,1)S(1)}, bf16[2,4,128,256]{3,2,1,0:T(8,128)(2,1)S(1)}, u32[]{:S(2)}, u32[]{:S(2)}) collective-permute-start(bf16[2,4,128,256]{3,2,1,0:T(8,128)(2,1)S(1)} %get-tuple-element.20.own.refs_1_.refs_4_), channel_id=1, source_target_pairs={{0,1},{2,3},{4,5},{6,7},{8,9},{10,11},{12,13},{14,15},{1,0},{3,2},... | collective-permute-start | bytes 1572872 | tf_op jit(solution)/shard_map/ppermute | solution.py:580
  15.5 12.6 %collective-permute-start.3 = (bf16[2,4,128,256]{3,2,1,0:T(8,128)(2,1)}, bf16[2,4,128,256]{3,2,1,0:T(8,128)(2,1)S(1)}, u32[]{:S(2)}, u32[]{:S(2)}) collective-permute-start(bf16[2,4,128,256]{3,2,1,0:T(8,128)(2,1)} %mix_rows.1), channel_id=1, source_target_pairs={{1,2},{5,6},{9,10},{13,14},{2,1},{6,5},{10,9},{14,13},{17,18},{21,... | collective-permute-start | bytes 1572872 | tf_op jit(solution)/shard_map/ppermute | solution.py:584
  18.7 10.8 %collective-permute-start.5 = (bf16[2,4,128,256]{3,2,1,0:T(8,128)(2,1)S(1)}, bf16[2,4,128,256]{3,2,1,0:T(8,128)(2,1)}, u32[]{:S(2)}, u32[]{:S(2)}) collective-permute-start(bf16[2,4,128,256]{3,2,1,0:T(8,128)(2,1)S(1)} %get-tuple-element.27.refs_0_.refs_3_), channel_id=1, source_target_pairs={{0,1},{2,3},{4,5},{6,7},{8,9},{10,11},{12,13},{14,15},{1,0},{3,2},... | collective-permute-start | bytes 1572872 | tf_op jit(solution)/shard_map/ppermute | solution.py:581
  18.9 0.9 %copy-start.5 = (s32[32768]{0:T(1024)S(1)}, s32[32768]{0:T(1024)}, u32[]{:S(2)}) copy-start(s32[32768]{0:T(1024)} %param.13) | copy-start | bytes 393220
  20.6 8.8 %copy-start.2 = (bf16[2,256,256]{2,1,0:T(8,128)(2,1)S(1)}, bf16[2,256,256]{2,1,0:T(8,128)(2,1)}, u32[]{:S(2)}) copy-start(bf16[2,256,256]{2,1,0:T(8,128)(2,1)} %constant.33.clone.refs_8_.refs_5_) | copy-start | bytes 786436
  20.6 8.8 %copy-start.3 = (bf16[256,256]{1,0:T(8,128)(2,1)S(1)}, bf16[256,256]{1,0:T(8,128)(2,1)}, u32[]{:S(2)}) copy-start(bf16[256,256]{1,0:T(8,128)(2,1)} %constant.34.clone.refs_9_.refs_6_) | copy-start | bytes 393220
  23.1 16.2 %collective-permute-start.2 = (bf16[2,4,128,256]{3,2,1,0:T(8,128)(2,1)S(1)}, bf16[2,4,128,256]{3,2,1,0:T(8,128)(2,1)S(1)}, u32[]{:S(2)}, u32[]{:S(2)}) collective-permute-start(bf16[2,4,128,256]{3,2,1,0:T(8,128)(2,1)S(1)} %get-tuple-element.27.refs_0_.refs_3_), channel_id=1, source_target_pairs={{1,2},{3,4},{5,6},{7,8},{9,10},{11,12},{13,14},{2,1},{4,3},{6,5},{... | collective-permute-start | bytes 1572872 | tf_op jit(solution)/shard_map/ppermute | solution.py:593
  28.1 11.2 %collective-permute-start.4 = (bf16[2,4,128,256]{3,2,1,0:T(8,128)(2,1)S(1)}, bf16[2,4,128,256]{3,2,1,0:T(8,128)(2,1)S(1)}, u32[]{:S(2)}, u32[]{:S(2)}) collective-permute-start(bf16[2,4,128,256]{3,2,1,0:T(8,128)(2,1)S(1)} %collective-permute-done.3.refs_1_), channel_id=1, source_target_pairs={{6,3},{10,7},{14,11},{1,4},{5,8},{9,12},{22,19},{26,23},{30,27},{1... | collective-permute-start | bytes 1572872 | tf_op jit(solution)/shard_map/ppermute | solution.py:594
